TPU v7x, 256 devices: a whole 4x4x8 slice. The times are simulated.
256 devices in a mesh: seq: 16 (over z, core), mp: 4 (over x), batch: 4 (over y).
Axes of the slice: x: 4, y: 4, z: 8, core: 2. Of those that a mesh axis runs over, the one named last changes fastest.
Arguments:
- latent: bfloat16 [32768, 2048], P(('batch', 'seq')), parts along dimension 0, may hold values from -6 to 6
- order: int32 [8192], P('seq'), may hold values from 0 to 8191, as said below
- inverse: int32 [8192], P('seq'), may hold values from 0 to 8191
- w_gate: bfloat16 [2048, 4096], P(None, 'mp'), may hold values from -0.125 to 0.125
- w_value: bfloat16 [2048, 4096], P(None, 'mp'), may hold values from -0.125 to 0.125
- w_input_output: bfloat16 [2048, 256], replicated, may hold values from -0.125 to 0.125
- w_step: bfloat16 [2048, 32], P(None, 'mp'), may hold values from -0.125 to 0.125
- conv_value: float32 [4, 4096], P(None, 'mp'), may hold values from -3 to 3
- conv_input_output: float32 [4, 256], replicated, may hold values from -3 to 3
- step_bias: float32 [32], P('mp'), may hold values from -4.5 to -2
- log_rate: float32 [32], P('mp'), may hold values from -8 to 1
- skip_gain: float32 [32], P('mp'), may hold values from 0.5 to 1.5
- norm_gain: float32 [4096], P('mp'), may hold values from 0.5 to 1.5
Outputs:
- mixed_out: bfloat16 [32768, 4096], P(('batch', 'seq'), 'mp'), parts along dimension 0
There are 4 independent parts, one for each index of `batch`. A program takes and returns all parts, laid end to end along the dimension named above; an argument that names none is the same for every part. Nothing has to cross between parts.
Inputs may be any that keep to these rules, and one draw needn't show every extreme that they name: order and inverse are permutations of 0 to 8191 and inverse of each other. Of the 512 storage rows of one index of seq, at most 64 have their scan positions on one index of seq, and the same holds for scan positions and storage rows; in every draw some pair of indices reaches 64.
All inputs are finite; a program needn't handle non-finite values.
Results may differ from a plain program's by a relative error of at most 0.012.
Values may be sent and summed in bfloat16 or wider, within the bound.
No kernel may reach another device: no remote copies, remote signals or barrier semaphores. Data moves between devices by JAX's collectives and lax.ppermute only.
A program may use at most 128 MiB of HBM per device.

v0:
```python
import jax
import jax.numpy as jnp
from jax import lax
from jax.sharding import PartitionSpec as P

Q = 128


def from_behind(value, axis, steps):
    count = lax.axis_size(axis)
    initial, last = (max(0, -steps), min(count, count - steps))
    return lax.ppermute(value, axis, [(source, source + steps) for source in range(initial, last)])


def carried_in(part, axis, combine, identity):
    place = lax.axis_index(axis)
    gathered = jax.tree.map(lambda a: lax.all_gather(a, axis), part)
    state = jax.tree.map(lambda a, e: jnp.zeros_like(a) + jnp.asarray(e, a.dtype), part, identity)

    def one(lap, state):
        return combine(
            state, jax.tree.map(lambda a: lax.dynamic_index_in_dim(a, lap, 0, False), gathered)
        )

    return lax.fori_loop(0, place, one, state)


def pack_rows(row_data, targets, peer_count, tok_rows, slot_cap):
    dest_dev = targets // tok_rows
    local_pos = targets % tok_rows
    onehot = (dest_dev[:, None] == lax.iota(jnp.int32, peer_count)[None, :]).astype(jnp.int32)
    rank_in = jnp.sum(jnp.cumsum(onehot, axis=0) * onehot, axis=1) - 1
    slot_index = dest_dev * slot_cap + rank_in
    buffer = (
        jnp.zeros((peer_count * slot_cap,) + row_data.shape[1:], row_data.dtype)
        .at[slot_index]
        .set(row_data)
    )
    places = jnp.full((peer_count * slot_cap,), tok_rows, jnp.int32).at[slot_index].set(local_pos)
    return (buffer, places)


def unpack_rows(buffer, places, tok_rows):
    blank = jnp.zeros((tok_rows,) + buffer.shape[1:], buffer.dtype)
    return blank.at[places].set(buffer, mode="drop")


def combine(first_part, second_part):
    return (
        first_part[0] + second_part[0],
        jnp.exp(second_part[0])[:, None, None] * first_part[1] + second_part[1],
    )


def body(
    latent,
    order,
    inverse,
    w_gate,
    w_value,
    w_input_output,
    w_step,
    conv_value,
    conv_input_output,
    step_bias,
    log_rate,
    skip_gain,
    norm_gain,
):
    tok_rows = latent.shape[0]
    peer_count = lax.axis_size("seq")
    slot_cap = 2 * tok_rows // peer_count
    weights = (w_gate, w_value, w_input_output, w_step)
    buffer, places = pack_rows(latent, inverse, peer_count, tok_rows, slot_cap)
    arrived, arrived_at = (
        lax.all_to_all(buffer, "seq", split_axis=0, concat_axis=0, tiled=True),
        lax.all_to_all(places, "seq", split_axis=0, concat_axis=0, tiled=True),
    )
    scan_rows = unpack_rows(arrived, arrived_at, tok_rows)
    gate_lin, value_lin, io_lin, step_raw = tuple(
        (jnp.dot(scan_rows, matrix, preferred_element_type=jnp.float32) for matrix in weights)
    )
    gate_act = gate_lin.astype(jnp.bfloat16)
    conv_in = jnp.concatenate([value_lin, io_lin], axis=1).astype(jnp.bfloat16)
    tap_count = conv_value.shape[0]
    prior_rim = from_behind(conv_in[tok_rows - tap_count + 1 :], "seq", 1)
    padded = jnp.concatenate([prior_rim, conv_in], axis=0)
    kernel = jnp.concatenate([conv_value, conv_input_output], axis=1)
    conv_sum = padded[0:tok_rows].astype(jnp.float32) * kernel[0]
    for tap_index in range(1, tap_count):
        conv_sum = (
            conv_sum
            + padded[tap_index : tap_index + tok_rows].astype(jnp.float32) * kernel[tap_index]
        )
    conv_act = jax.nn.silu(conv_sum).astype(jnp.bfloat16)
    inner_width = conv_value.shape[1]
    state_dim = conv_input_output.shape[1] // 2
    head_count = step_bias.shape[0]
    head_size = inner_width // head_count
    block_count = tok_rows // Q
    x_blocks = conv_act[:, :inner_width].reshape(block_count, Q, head_count, head_size)
    b_blocks = conv_act[:, inner_width : inner_width + state_dim].reshape(block_count, Q, state_dim)
    c_blocks = conv_act[:, inner_width + state_dim :].reshape(block_count, Q, state_dim)
    step_size = jax.nn.softplus(step_raw + step_bias)
    log_decay = -jnp.exp(log_rate) * step_size
    step_blocks = step_size.reshape(block_count, Q, head_count)
    cum_decay = jnp.cumsum(log_decay.reshape(block_count, Q, head_count), axis=1)
    scores = jnp.einsum("ctn,csn->cts", c_blocks, b_blocks, preferred_element_type=jnp.float32)
    cum_heads = jnp.transpose(cum_decay, (0, 2, 1))
    decay_gap = cum_heads[:, :, :, None] - cum_heads[:, :, None, :]
    causal = (lax.iota(jnp.int32, Q)[:, None] >= lax.iota(jnp.int32, Q)[None, :])[None, None, :, :]
    decay_factor = jnp.exp(jnp.where(causal, decay_gap, -jnp.inf))
    weight = (
        scores[:, None, :, :] * decay_factor * jnp.transpose(step_blocks, (0, 2, 1))[:, :, None, :]
    ).astype(jnp.bfloat16)
    y_local = jnp.einsum("chts,cshp->cthp", weight, x_blocks, preferred_element_type=jnp.float32)
    to_end = jnp.exp(cum_decay[:, -1:, :] - cum_decay) * step_blocks
    x_scaled = (x_blocks.astype(jnp.float32) * to_end[..., None]).astype(jnp.bfloat16)
    block_state = jnp.einsum(
        "cshp,csn->chpn", x_scaled, b_blocks, preferred_element_type=jnp.float32
    )
    totals = cum_decay[:, -1, :]
    running = jnp.zeros((head_count, head_size, state_dim), jnp.float32)
    lead_sum = jnp.zeros((head_count,), jnp.float32)
    entering = []
    lead_sums = []
    for block_index in range(block_count):
        entering.append(running)
        lead_sums.append(lead_sum)
        running = jnp.exp(totals[block_index])[:, None, None] * running + block_state[block_index]
        lead_sum = lead_sum + totals[block_index]
    prior_decay, prior_state = carried_in(
        (lead_sum, running), "seq", combine, (jnp.zeros_like(lead_sum), jnp.zeros_like(running))
    )
    entering_all = (
        jnp.stack(entering) + jnp.exp(jnp.stack(lead_sums))[:, :, None, None] * prior_state[None]
    )
    y_carried = jnp.exp(cum_decay)[..., None] * jnp.einsum(
        "ctn,chpn->cthp",
        c_blocks.astype(jnp.float32),
        entering_all,
        precision=lax.Precision.HIGHEST,
    )
    y_total = y_local + y_carried + skip_gain[None, None, :, None] * x_blocks.astype(jnp.float32)
    y_total = y_total.reshape(tok_rows, head_count, head_size)
    gated = y_total * jax.nn.silu(gate_act.astype(jnp.float32)).reshape(
        tok_rows, head_count, head_size
    )
    inv_rms = lax.rsqrt(jnp.mean(gated * gated, axis=2, keepdims=True) + 1e-05)
    normed = ((gated * inv_rms).reshape(tok_rows, inner_width) * norm_gain).astype(jnp.bfloat16)
    buffer, places = pack_rows(normed, order, peer_count, tok_rows, slot_cap)
    arrived, arrived_at = (
        lax.all_to_all(buffer, "seq", split_axis=0, concat_axis=0, tiled=True),
        lax.all_to_all(places, "seq", split_axis=0, concat_axis=0, tiled=True),
    )
    return unpack_rows(arrived, arrived_at, tok_rows)


def solution(mesh):
    return jax.shard_map(
        body,
        mesh=mesh,
        in_specs=(
            P(("batch", "seq"), None),
            P("seq"),
            P("seq"),
            P(None, "mp"),
            P(None, "mp"),
            P(),
            P(None, "mp"),
            P(None, "mp"),
            P(),
            P("mp"),
            P("mp"),
            P("mp"),
            P("mp"),
        ),
        out_specs=P(("batch", "seq"), "mp"),
        check_vma=False,
    )
```

profile of v0, /device:TPU:1, one launch (start us, length us, event | category | flops | bytes accessed | tf_op | source)
XLA Modules:
  0.0 325.0 jit_solution(14120442015446544121)
XLA Ops:
  8.8 2.4 scatter_custom_fusion.1
  12.0 10.0 %all-to-all-start.1 = ((s32[16,64,1]{1,2,0:T(1,128)}), s32[16,64,1]{1,2,0:T(1,128)S(1)}, u32[]{:S(2)}, u32[]{:S(2)}) async-start(s32[16,64,1]{1,2,0:T(1,128)} %all_to_all.35), calls=%async_computation.1 | async-start | bytes 16384 | tf_op jit(solution)/shard_map/all_to_all | solution.py:77
  22.0 7.3 %scatter_custom_fusion.2 = bf16[1024,2048]{1,0:T(8,128)(2,1)} fusion(s32[512]{0:T(512)S(1)} %compare_select_fusion.3, bf16[512,2048]{1,0:T(8,128)(2,1)} %param.15, bf16[]{:T(256)} %constant.89.clone.1), kind=kCustom, calls=%fused_computation.33 | custom fusion | bytes 4194816 | tf_op jit(solution)/shard_map/scatter | solution.py:37
  29.2 7.4 %all-to-all-start.2 = ((bf16[16,64,2048]{2,1,0:T(8,128)(2,1)}), bf16[16,64,2048]{2,1,0:T(8,128)(2,1)}, u32[]{:S(2)}, u32[]{:S(2)}) async-start(bf16[16,64,2048]{2,1,0:T(8,128)(2,1)} %bitcast.141), calls=%async_computation.2 | async-start | bytes 8388608 | tf_op jit(solution)/shard_map/all_to_all | solution.py:76
  38.2 92.0 %all-to-all-done.2 = bf16[16,64,2048]{2,1,0:T(8,128)(2,1)} async-done(((bf16[16,64,2048]{2,1,0:T(8,128)(2,1)}), bf16[16,64,2048]{2,1,0:T(8,128)(2,1)}, u32[]{:S(2)}, u32[]{:S(2)}) %all-to-all-start.2) | async-done | bytes 4194336 | tf_op jit(solution)/shard_map/all_to_all | solution.py:76
  130.2 8.2 %scatter_custom_fusion.3 = bf16[512,2048]{1,0:T(8,128)(2,1)S(1)} fusion(s32[1024]{0:T(1024)S(1)} %bitcast.162, bf16[1024,2048]{1,0:T(8,128)(2,1)} %bitcast.10, bf16[]{:T(256)} %constant.89.clone.1), kind=kCustom, calls=%fused_computation.56 | custom fusion | bytes 2097664 | tf_op jit(solution)/shard_map/scatter | solution.py:45
  142.9 5.2 %convolution_convert_fusion.1 = bf16[512,1024]{1,0:T(8,128)(2,1)S(1)} fusion(bf16[512,2048]{1,0:T(8,128)(2,1)} %copy-done.1, bf16[2048,1024]{1,0:T(8,128)(2,1)} %param.19), kind=kOutput, calls=%fused_computation.38 | convolution fusion | flops 2148007936 | bytes 7340032 | tf_op jit(solution)/shard_map/dot_general | solution.py:81
  148.1 2.4 collective-permute-start
  162.2 3.1 reduce-window.14
  170.9 3.2 scatter_custom_fusion
  175.4 7.0 %all-to-all-start = ((s32[16,64,1]{1,2,0:T(1,128)}), s32[16,64,1]{1,2,0:T(1,128)}, u32[]{:S(2)}, u32[]{:S(2)}) async-start(s32[16,64,1]{1,2,0:T(1,128)} %bitcast.158), calls=%async_computation | async-start | bytes 16384 | tf_op jit(solution)/shard_map/all_to_all | solution.py:154
  184.3 1.6 copy.64
  185.9 4.8 %convert_multiply_fusion = f32[512,1024]{1,0:T(8,128)S(1)} fusion(bf16[512,2048]{1,0:T(8,128)(2,1)S(1)} %copy-done.2, bf16[2048,1024]{1,0:T(8,128)(2,1)} %param.18), kind=kOutput, calls=%fused_computation.8 | convolution fusion | flops 2150629376 | bytes 8388608 | tf_op jit(solution)/shard_map/dot_general | solution.py:81
  192.2 1.8 copy.71
  194.0 17.4 %all-gather = f32[16,1,8]{2,1,0:T(1,128)} all-gather(f32[1,1,8]{2,1,0:T(1,128)S(1)} %get-tuple-element.88), channel_id=1, replica_groups=mesh['seq'=16,'mp'=4,'batch'=4] {'seq'}, dimensions={0}, use_global_device_ids=true | all-gather | bytes 544 | tf_op jit(solution)/shard_map/all_gather | solution.py:17
  213.8 3.4 %all-gather.3.cloned.1.call-done = f32[16,8,128,128]{3,2,1,0:T(8,128)} async-done(((f32[1,8,128,128]{3,2,1,0:T(8,128)}), f32[16,8,128,128]{3,2,1,0:T(8,128)}) %all-gather.3.cloned.1.call-update) | async-done | bytes 8388624 | tf_op jit(solution)/shard_map/all_gather | solution.py:17
  217.3 2.2 while.12
  219.7 2.1 fusion.7
  223.4 1.9 copy.70
  225.3 1.9 mul.258
  227.2 6.4 %scatter_custom_fusion.4 = bf16[1024,1024]{1,0:T(8,128)(2,1)} fusion(s32[512]{0:T(512)} %compare_select_fusion.4, f32[64,8,8,128]{3,2,1,0:T(8,128)} %bitcast.146, f32[512,1024]{1,0:T(8,128)S(1)} %copy-done.4, f32[64,8,8,128]{3,2,1,0:T(8,128)} %bitcast.145, f32[1024]{0:T(1024)S(1)} %copy-done.18, bf16[]{:T(256)} %constant.89.clone.1), kind=kCustom, calls=%fused_computation.43 | custom fusion | flops 2097152 | bytes 8393216 | tf_op jit(solution)/shard_map/scatter | solution.py:37
  233.6 29.4 %all-to-all-start.3 = ((bf16[16,64,1024]{2,1,0:T(8,128)(2,1)}), bf16[16,64,1024]{2,1,0:T(8,128)(2,1)S(1)}, u32[]{:S(2)}, u32[]{:S(2)}) async-start(bf16[16,64,1024]{2,1,0:T(8,128)(2,1)} %bitcast.144), calls=%async_computation.3 | async-start | bytes 4194304 | tf_op jit(solution)/shard_map/all_to_all | solution.py:153
  264.5 47.5 %all-to-all-done.3 = bf16[16,64,1024]{2,1,0:T(8,128)(2,1)S(1)} async-done(((bf16[16,64,1024]{2,1,0:T(8,128)(2,1)}), bf16[16,64,1024]{2,1,0:T(8,128)(2,1)S(1)}, u32[]{:S(2)}, u32[]{:S(2)}) %all-to-all-start.3) | async-done | bytes 2097184 | tf_op jit(solution)/shard_map/all_to_all | solution.py:153
  311.9 6.2 %scatter_custom_fusion.5 = bf16[512,1024]{1,0:T(8,128)(2,1)} fusion(s32[1024]{0:T(1024)S(1)} %bitcast.161, bf16[1024,1024]{1,0:T(8,128)(2,1)S(1)} %bitcast.149, bf16[]{:T(256)} %constant.89.clone.1), kind=kCustom, calls=%fused_computation.64 | custom fusion | bytes 1048578 | tf_op jit(solution)/shard_map/scatter | solution.py:45
  (119 shorter events, 38.1 us)
Async XLA Ops:
  6.5 134.8 %copy-start = (bf16[2048,256]{1,0:T(8,128)(2,1)S(1)}, bf16[2048,256]{1,0:T(8,128)(2,1)}, u32[]{:S(2)}) copy-start(bf16[2048,256]{1,0:T(8,128)(2,1)} %param.20) | copy-start | bytes 3145732
  12.0 17.2 %all-to-all-start.1 = ((s32[16,64,1]{1,2,0:T(1,128)}), s32[16,64,1]{1,2,0:T(1,128)S(1)}, u32[]{:S(2)}, u32[]{:S(2)}) async-start(s32[16,64,1]{1,2,0:T(1,128)} %all_to_all.35), calls=%async_computation.1 | async-start | bytes 16384 | tf_op jit(solution)/shard_map/all_to_all | solution.py:77
  29.2 7.5 %copy-start.16 = (f32[4,1024]{1,0:T(4,128)S(1)}, f32[4,1024]{1,0:T(4,128)}, u32[]{:S(2)}) copy-start(f32[4,1024]{1,0:T(4,128)} %param.22) | copy-start | bytes 49156
  29.2 7.5 %copy-start.19 = (f32[4,256]{1,0:T(4,128)S(1)}, f32[4,256]{1,0:T(4,128)}, u32[]{:S(2)}) copy-start(f32[4,256]{1,0:T(4,128)} %param.23) | copy-start | bytes 12292
  29.2 7.6 %copy-start.25 = (f32[8]{0:T(128)S(1)}, f32[8]{0:T(128)}, u32[]{:S(2)}) copy-start(f32[8]{0:T(128)} %param.25) | copy-start | bytes 100
  29.2 101.0 %all-to-all-start.2 = ((bf16[16,64,2048]{2,1,0:T(8,128)(2,1)}), bf16[16,64,2048]{2,1,0:T(8,128)(2,1)}, u32[]{:S(2)}, u32[]{:S(2)}) async-start(bf16[16,64,2048]{2,1,0:T(8,128)(2,1)} %bitcast.141), calls=%async_computation.2 | async-start | bytes 8388608 | tf_op jit(solution)/shard_map/all_to_all | solution.py:76
  36.6 101.8 %copy-start.12 = (bf16[2048,8]{0,1:T(8,128)(2,1)S(1)}, bf16[2048,8]{0,1:T(8,128)(2,1)}, u32[]{:S(2)}) copy-start(bf16[2048,8]{0,1:T(8,128)(2,1)} %param.21) | copy-start | bytes 98308
  36.6 101.9 %copy-start.24 = (f32[8]{0:T(128)S(1)}, f32[8]{0:T(128)}, u32[]{:S(2)}) copy-start(f32[8]{0:T(128)} %param.24) | copy-start | bytes 100
  36.6 180.6 %all-gather.3.cloned.1.call-start = ((), (), s32[]{:S(2)}) async-start(), calls=%async_computation.4 | async-start | bytes 8912896 | tf_op jit(solution)/shard_map/all_gather | solution.py:17
  138.5 4.3 %copy-start.1 = (bf16[512,2048]{1,0:T(8,128)(2,1)}, bf16[512,2048]{1,0:T(8,128)(2,1)S(1)}, u32[]{:S(2)}) copy-start(bf16[512,2048]{1,0:T(8,128)(2,1)S(1)} %scatter_custom_fusion.3) | copy-start | bytes 6291460
  142.8 5.2 %copy-start.7 = (bf16[512,256]{1,0:T(8,128)(2,1)S(1)}, bf16[512,256]{1,0:T(8,128)(2,1)}, u32[]{:S(2)}) copy-start(bf16[512,256]{1,0:T(8,128)(2,1)} %convolution_convert_fusion.2) | copy-start | bytes 786436
  148.1 4.5 %collective-permute-start = (bf16[3,1280]{1,0:T(4,128)(2,1)S(1)}, bf16[3,1280]{1,0:T(4,128)(2,1)S(1)}, u32[]{:S(2)}, u32[]{:S(2)}) collective-permute-start(bf16[3,1280]{1,0:T(4,128)(2,1)S(1)} %fusion.42), channel_id=1, source_target_pairs={{0,16},{16,32},{32,48},{48,64},{64,80},{80,96},{96,112},{112,128},... | collective-permute-start | bytes 23048 | tf_op jit(solution)/shard_map/ppermute | solution.py:12
  158.1 27.8 %copy-start.2 = (bf16[512,2048]{1,0:T(8,128)(2,1)S(1)}, bf16[512,2048]{1,0:T(8,128)(2,1)}, u32[]{:S(2)}) copy-start(bf16[512,2048]{1,0:T(8,128)(2,1)} %copy-done.1) | copy-start | bytes 6291460
  175.4 58.2 %all-to-all-start = ((s32[16,64,1]{1,2,0:T(1,128)}), s32[16,64,1]{1,2,0:T(1,128)}, u32[]{:S(2)}, u32[]{:S(2)}) async-start(s32[16,64,1]{1,2,0:T(1,128)} %bitcast.158), calls=%async_computation | async-start | bytes 16384 | tf_op jit(solution)/shard_map/all_to_all | solution.py:154
  217.3 2.3 copy-start.9
  217.3 2.3 copy-start.10
  217.3 2.3 copy-start.11
  219.6 2.2 copy-start.6
  219.6 2.2 copy-start.8
  219.6 2.2 copy-start.14
  219.6 2.2 copy-start.15
  219.6 2.2 copy-start.17
  219.6 2.2 copy-start.26
  233.6 78.3 %all-to-all-start.3 = ((bf16[16,64,1024]{2,1,0:T(8,128)(2,1)}), bf16[16,64,1024]{2,1,0:T(8,128)(2,1)S(1)}, u32[]{:S(2)}, u32[]{:S(2)}) async-start(bf16[16,64,1024]{2,1,0:T(8,128)(2,1)} %bitcast.144), calls=%async_computation.3 | async-start | bytes 4194304 | tf_op jit(solution)/shard_map/all_to_all | solution.py:153
  (9 other events, 13.9 us)
Sparse Core Ops, SparseCore 0:
  159.8 57.3 all-gather.2
where the time goes:
time: 327 us; the launch traced here: 325 us
  waiting for transfers between devices  143 us (44%)
  starting transfers between devices  56.2 us (17%)
  local copies, waits for them, and re-layouts  47.6 us (15%)
  other arithmetic  28.4 us (9%)
  matrix products  18.3 us (6%)
  blocking collectives  17.4 us (5%)
  between operations  14 us (4%)
    all_to_all x2, waiting for transfers between devices, body(): lax.all_to_all(buffer, 'seq', split_axis=0, concat_axis=0, tiled=True)  139 us
    all_to_all x2, starting transfers between devices, body(): lax.all_to_all(buffer, 'seq', split_axis=0, concat_axis=0, tiled=True)  36.7 us
    all_gather x1, blocking collectives, carried_in(): gathered = jax.tree.map(lambda a: lax.all_gather(a, axis), part)  17.4 us
    all_to_all x2, starting transfers between devices, body(): lax.all_to_all(places, 'seq', split_axis=0, concat_axis=0, tiled=True)  17 us
    scatter x2, local copies, waits for them, and re-layouts, unpack_rows(): return blank.at[places].set(buffer, mode='drop')  14.5 us
    dot_general x4, matrix products, body(): jnp.dot(scan_rows, matrix, preferred_element_type=jnp.float32)  12.1 us
    scatter x1, local copies, waits for them, and re-layouts, pack_rows(): buffer = jnp.zeros((peer_count * slot_cap,) + row_data.shape[1:], row_dat...  7.25 us
  transfers between devices with their start and end apart: 6, of which 3 were waited for; matrix products, arithmetic and copies ran while one was open for 17% of the time, Pallas kernels for 0%

commit v1 on v0

v1 whole, which is shorter than its diff:
```python
import jax
import jax.numpy as jnp
from jax import lax
from jax.experimental import pallas as pl
from jax.experimental.pallas import tpu as pltpu
from jax.sharding import PartitionSpec as P

F32, BF, I32 = jnp.float32, jnp.bfloat16, jnp.int32
ROWS = 512
SEQ = 16
QUAD = ROWS // 4
SLOT = QUAD + 16
WIN = 32
KEYS = SEQ * WIN
CH = 64
BLOCK = 128
MIB = 1 << 20


def iota(shape, dim):
    return lax.broadcasted_iota(I32, shape, dim)


def dot(a, b, dims=((1,), (0,))):
    return lax.dot_general(a, b, (dims, ((), ())), preferred_element_type=F32)


def column(row):
    return jnp.transpose(jnp.broadcast_to(row, (128, row.shape[1])))


def tiles(row):
    return [row[:, g : g + 128] for g in range(0, row.shape[1], 128)]


def sorted_place(inv, inv_col):
    rank = jnp.concatenate(
        [jnp.sum((inv_col < part).astype(F32), axis=0, keepdims=True) for part in tiles(inv)],
        axis=1,
    )
    packed = jnp.floor(rank * 0.25)
    return (rank - 4.0 * packed) * QUAD + packed


def one_hot(place, count):
    return (iota((count, place.shape[1]), 0) == place.astype(I32)).astype(F32).astype(BF)


def stacked(rows, shape):
    place = iota(shape, 0)
    block = jnp.zeros(shape, F32)
    for index, row in enumerate(rows):
        block = jnp.where(place == index, row, block)
    return block


def side_by_side(low, high):
    first = iota((QUAD, 128), 1) < 64
    return [
        jnp.where(first, low[u : u + QUAD], high[u + QUAD : u + 2 * QUAD]) for u in (0, 2 * QUAD)
    ]


def front_body(at_ref, inv_ref, ord_ref, lat_ref, wio_ref, out_ref):
    inv = inv_ref[...].astype(F32)
    inv_col = column(inv)
    deal = one_hot(sorted_place(inv, inv_col), ROWS)
    io = dot(lat_ref[...], wio_ref[...]).astype(BF)
    io = dot(deal, io)
    m = at_ref[0]
    half = jnp.where(m >= 2, io[:, 128:], io[:, :128])
    turned = pltpu.roll(half, 64, 1)
    odd = m % 2 == 1
    packed = side_by_side(jnp.where(odd, turned, half), jnp.where(odd, half, turned))
    source = (ord_ref[...] >> 9).astype(F32)
    source_col = column(source)
    earlier = [
        jnp.sum(
            jnp.where(
                (source_col == part) & (iota((ROWS, 128), 0) < iota((ROWS, 128), 1) + 128 * g),
                1.0,
                0.0,
            ),
            axis=0,
            keepdims=True,
        )
        for g, part in enumerate(tiles(source))
    ]
    bound = (iota((ROWS, 128), 1) * ROWS).astype(F32)
    start = jnp.sum((inv_col < bound).astype(F32), axis=0, keepdims=True)
    tile = jnp.minimum(jnp.floor(start * (1.0 / 64.0)), 6.0)
    offset = start - 64.0 * tile
    blank = jnp.zeros((1, 128), F32)
    side = stacked(
        [
            source[:, :256],
            source[:, 256:],
            jnp.concatenate(earlier[:2], axis=1),
            jnp.concatenate(earlier[2:], axis=1),
            jnp.concatenate([tile, blank], axis=1),
            jnp.concatenate([offset, blank], axis=1),
        ],
        (16, 256),
    )
    slot = jnp.concatenate([jnp.concatenate(packed, axis=1), side], axis=0).astype(BF)
    for index in range(out_ref.shape[0]):
        out_ref[index] = slot


def value_body(inv_ref, lat_ref, wv_ref, ws_ref, out_ref, deal_ref, step_ref):
    n = pl.program_id(0)

    @pl.when(n == 0)
    def _():
        inv = inv_ref[...].astype(F32)
        deal_ref[...] = one_hot(sorted_place(inv, column(inv)), ROWS)
        rest = dot(ws_ref[...], lat_ref[...], ((1,), (1,)))
        for part in range(3):
            piece = rest.astype(BF)
            step_ref[part] = dot(piece, deal_ref[...], ((1,), (1,)))
            rest = rest - piece.astype(F32)

    value = dot(lat_ref[...], wv_ref[...]).astype(BF)
    value = dot(deal_ref[...], value)
    for jj in range(4):
        group = value[:, 128 * (jj // 2) : 128 * (jj // 2) + 128]
        turned = pltpu.roll(group, 64, 1)
        packed = side_by_side(group, turned) if jj % 2 == 0 else side_by_side(turned, group)
        head = 2 * n + jj // 2
        rows = []
        for part in range(3):
            steps = step_ref[part, pl.ds(head, 1), :]
            rows += [steps[:, :256], steps[:, 256:]]
        side = stacked(rows, (16, 256))
        out_ref[jj] = jnp.concatenate([jnp.concatenate(packed, axis=1), side], axis=0).astype(BF)


def conv_silu(cur, prev, taps):
    ext = jnp.concatenate([prev, cur], axis=1)
    total = cur * taps[3]
    for back in range(1, 4):
        total = total + pltpu.roll(ext, back, 1)[:, 128:] * taps[3 - back]
    return total * (1.0 / (1.0 + jnp.exp(-total)))


def pick_quarter(res, quarter):
    out = jnp.zeros((CH, res.shape[1]), F32)
    for q in range(4):
        out = out + jnp.where(quarter == q, res[CH * q : CH * q + CH], 0.0)
    return out


def bc_body(at_ref, ab_ref, own_ref, oth_ref, conv_ref, out_ref, code_ref, win_ref, tap_ref):
    m, c = at_ref[0], at_ref[1]
    for z in range(8):
        for ref, core in ((own_ref, c), (oth_ref, 1 - c)):
            d = 2 * z + core
            side = ref[z, QUAD:SLOT, :].astype(F32)
            source = jnp.concatenate([side[0:1], side[1:2]], axis=1).astype(I32)
            place = jnp.concatenate([side[2:3], side[3:4]], axis=1).astype(I32)
            for s in range(SEQ):
                j = (s >> 1) + 8 * ((s + c) % 2)
                place = place + jnp.where(source == s, ab_ref[32 * j + 16 + d], 0)
            code_ref[pl.ds(d, 1), :] = source * 128 + place

    group = conv_ref[:, pl.ds(pl.multiple_of(128 * (m // 2), 128), 128)]
    tap_ref[...] = jnp.transpose(stacked([group[k : k + 1] for k in range(4)], (128, 128)))
    tap_cols = tap_ref[pl.ds(pl.multiple_of(64 * (m % 2), 64), 64), :]
    taps = [tap_cols[:, k : k + 1] for k in range(4)]

    def rows_of(d, lo, hi):
        for j in range(SEQ):
            ref = own_ref if j < 8 else oth_ref
            at = pl.multiple_of(16 * ab_ref[32 * j + d], 16)
            win_ref[WIN * j : WIN * j + WIN, :] = ref[j % 8, pl.ds(at, WIN), :]
        code = code_ref[pl.ds(d, 1), :][:, lo:hi]
        source = code >> 7
        j_of = (source >> 1) + 8 * ((source + c) & 1)
        key = j_of * WIN + ((code >> 2) & (WIN - 1))
        spread = one_hot(key, KEYS)
        return pick_quarter(dot(win_ref[...], spread, ((0,), (0,))), code & 3)

    prev = rows_of(jnp.maximum(8 * c - 1, 0), ROWS - 128, ROWS)
    prev = jnp.where(c > 0, prev, 0.0)

    def one(e, prev):
        cur = rows_of(8 * c + e, 0, ROWS)
        act = conv_silu(cur, prev, taps)
        out_ref[:, pl.ds(pl.multiple_of(ROWS * e, ROWS), ROWS)] = act.astype(BF)
        return cur[:, ROWS - 128 :]

    lax.fori_loop(0, 8, one, prev)


def scan_body(
    at_ref,
    ab_ref,
    bias_ref,
    rate_ref,
    skip_ref,
    code_ref,
    x_ref,
    conv_ref,
    own0,
    own1,
    own2,
    own3,
    oth0,
    oth1,
    oth2,
    oth3,
    out_ref,
    bc_ref,
    win_ref,
    stepwin_ref,
    stepcol_ref,
    tap_ref,
    xact_ref,
    step_ref,
    cum_ref,
    acc_ref,
):
    m, c, sq = at_ref[0], at_ref[1], at_ref[2]
    head = sq // 2
    for k, (own, oth) in enumerate(((own0, oth0), (own1, oth1), (own2, oth2), (own3, oth3))):
        at = pl.multiple_of(CH * ((m - k + 4) % 4), CH)
        bc_ref[c, pl.ds(at, CH), :] = own[...]
        bc_ref[1 - c, pl.ds(at, CH), :] = oth[...]

    group = conv_ref[:, pl.ds(pl.multiple_of(128 * head, 128), 128)]
    tap_ref[...] = jnp.transpose(stacked([group[k : k + 1] for k in range(4)], (128, 128)))
    tap_cols = tap_ref[pl.ds(pl.multiple_of(64 * (sq % 2), 64), 64), :]
    taps = [tap_cols[:, k : k + 1] for k in range(4)]

    for s0 in range(0, SEQ, 8):
        blocks = []
        for s in range(s0, s0 + 8):
            side = x_ref[s, QUAD:SLOT, :].astype(F32)
            blocks += [side[0:8, :128], side[0:8, 128:]]
        turned = jnp.transpose(jnp.concatenate(blocks, axis=0))
        for s in range(s0, s0 + 8):
            own = turned if s == s0 else pltpu.roll(turned, 128 - 16 * (s - s0), 1)
            stepcol_ref[s] = own.astype(BF)

    def tile_at(s, d):
        j = (s >> 1) + 8 * ((s + c) % 2)
        return pl.multiple_of(16 * ab_ref[32 * j + d], 16)

    def spread_of(d):
        code = code_ref[pl.ds(d, 1), :]
        key = (code >> 7) * WIN + ((code >> 2) & (WIN - 1))
        return one_hot(key, KEYS), code & 3

    def gather(d, prev):
        for s in range(SEQ):
            at = tile_at(s, d)
            win_ref[WIN * s : WIN * s + WIN, :] = x_ref[s, pl.ds(at, WIN), :]
            stepwin_ref[WIN * s : WIN * s + WIN, :] = stepcol_ref[s, pl.ds(at, WIN), :]
        spread, quarter = spread_of(d)
        cur = pick_quarter(dot(win_ref[...], spread, ((0,), (0,))), quarter)
        act = conv_silu(cur, prev, taps)
        xact_ref[:, pl.ds(pl.multiple_of(ROWS * d, ROWS), ROWS)] = act.astype(BF)
        parts = dot(stepwin_ref[...], spread, ((0,), (0,)))
        step = jnp.zeros((1, ROWS), F32)
        for q in range(4):
            row = (q >> 1) + 8 * (q & 1)
            value = parts[row : row + 1] + parts[row + 2 : row + 3] + parts[row + 4 : row + 5]
            step = step + jnp.where(quarter == q, value, 0.0)
        step_ref[pl.ds(d, 1), :] = step
        return cur[:, ROWS - 128 :]

    lax.fori_loop(0, SEQ, gather, jnp.zeros((CH, 128), F32))

    raw = step_ref[...] + bias_ref[head]
    size = jnp.maximum(raw, 0.0) + jnp.log1p(jnp.exp(-jnp.abs(raw)))
    step_ref[...] = size
    rate = jnp.exp(jnp.full((1, ROWS), rate_ref[head], F32))
    cum = -rate * size
    lane = iota((SEQ, ROWS), 1) % BLOCK
    for shift in (1, 2, 4, 8, 16, 32, 64):
        cum = cum + jnp.where(lane >= shift, pltpu.roll(cum, shift, 1), 0.0)
    cum_ref[...] = cum
    acc_ref[...] = jnp.zeros_like(acc_ref)
    skip = skip_ref[head]
    causal = iota((BLOCK, BLOCK), 0) <= iota((BLOCK, BLOCK), 1)

    def scan(d, state):
        x_all = xact_ref[:, pl.ds(pl.multiple_of(ROWS * d, ROWS), ROWS)]
        bc = bc_ref[d // 8, :, pl.ds(pl.multiple_of(ROWS * (d % 8), ROWS), ROWS)]
        cum_all = cum_ref[pl.ds(d, 1), :]
        size_all = step_ref[pl.ds(d, 1), :]
        ys = []
        for k in range(ROWS // BLOCK):
            at = slice(BLOCK * k, BLOCK * k + BLOCK)
            x = x_all[:, at].astype(F32)
            b, cc = bc[:BLOCK, at], bc[BLOCK:, at]
            cum_row, size = cum_all[:, at], size_all[:, at]
            scores = dot(b, cc, ((0,), (0,)))
            gap = jnp.where(causal, cum_row - column(cum_row), -1e30)
            weight = (scores * jnp.exp(gap)).astype(BF)
            y = dot((x * size).astype(BF), weight)
            y = y + dot(state.astype(BF), cc) * jnp.exp(cum_row) + skip * x
            ys.append(y)
            total = cum_row[:, BLOCK - 1 :]
            scaled = (x * (jnp.exp(total - cum_row) * size)).astype(BF)
            state = jnp.exp(total) * state + dot(scaled, b, ((1,), (1,)))
        y_all = jnp.concatenate(ys, axis=1)
        spread, quarter = spread_of(d)
        apart = jnp.concatenate(
            [jnp.where(quarter == q, y_all, 0.0).astype(BF) for q in range(4)], axis=0
        )
        back = dot(spread, apart, ((1,), (1,)))
        for s in range(SEQ):
            at = pl.ds(tile_at(s, d), WIN)
            acc_ref[s, at, :] = acc_ref[s, at, :] + back[WIN * s : WIN * s + WIN]
        return state

    lax.fori_loop(0, SEQ, scan, jnp.zeros((CH, BLOCK), F32))
    out_ref[...] = acc_ref[...].astype(BF)


def final_body(inv_ref, y_ref, gate_ref, gain_ref, out_ref, pick_ref):
    @pl.when(pl.program_id(0) == 0)
    def _():
        inv = inv_ref[...].astype(F32)
        place = column(sorted_place(inv, column(inv)))
        lane = iota((ROWS, 128), 1)
        for g in range(4):
            hit = place == (lane + 128 * g).astype(F32)
            pick_ref[:, 128 * g : 128 * g + 128] = hit.astype(F32).astype(BF)

    low = iota((QUAD, 128), 1) < 64
    rows = []
    for q in range(4):
        at = slice(128 * (q // 2), 128 * (q // 2) + 128)
        even, odd = y_ref[0, :, at].astype(F32), y_ref[1, :, at].astype(F32)
        if q % 2 == 0:
            rows.append(jnp.where(low, even, pltpu.roll(odd, 64, 1)))
        else:
            rows.append(jnp.where(low, pltpu.roll(even, 64, 1), odd))
    y = dot(pick_ref[...], jnp.concatenate(rows, axis=0).astype(BF))
    gate = gate_ref[...].astype(F32)
    gated = y * (gate * (1.0 / (1.0 + jnp.exp(-gate))))
    mean = jnp.mean(gated * gated, axis=1, keepdims=True)
    out_ref[...] = (gated * lax.rsqrt(mean + 1e-5) * gain_ref[...]).astype(BF)


def vmem(*_):
    return pl.BlockSpec(memory_space=pltpu.VMEM)


def smem(*_):
    return pl.BlockSpec(memory_space=pltpu.SMEM)


def params(mib):
    return pltpu.CompilerParams(vmem_limit_bytes=mib * MIB)


def cost(flops, data, exps=0):
    return pl.CostEstimate(flops=flops, bytes_accessed=data, transcendentals=exps)


def body(
    latent,
    order,
    inverse,
    w_gate,
    w_value,
    w_input_output,
    w_step,
    conv_value,
    conv_input_output,
    step_bias,
    log_rate,
    skip_gain,
    norm_gain,
):
    m, sq = lax.axis_index("mp"), lax.axis_index("seq")
    at = jnp.stack([m, sq % 2, sq, m]).astype(I32)
    inv = inverse.reshape(1, ROWS)
    pairs = [(i, i ^ 1) for i in range(SEQ)]
    lines = [[2 * i + core for i in range(SEQ // 2)] for core in range(2)]

    bc_slots = pl.pallas_call(
        front_body,
        out_shape=jax.ShapeDtypeStruct((8, SLOT, 256), BF),
        in_specs=[smem(), vmem(), vmem(), vmem(), vmem()],
        out_specs=vmem(),
        compiler_params=params(24),
        cost_estimate=cost(1 << 30, 4 << 20),
        name="front",
    )(at, inv, order.reshape(1, ROWS), latent, w_input_output)
    own = lax.all_to_all(bc_slots, "seq", 0, 0, axis_index_groups=lines, tiled=True)

    x_slots = pl.pallas_call(
        value_body,
        grid=(4,),
        out_shape=jax.ShapeDtypeStruct((SEQ, SLOT, 256), BF),
        in_specs=[
            pl.BlockSpec((1, ROWS), lambda n: (0, 0)),
            pl.BlockSpec((ROWS, latent.shape[1]), lambda n: (0, 0)),
            pl.BlockSpec((latent.shape[1], 256), lambda n: (0, n)),
            pl.BlockSpec((8, latent.shape[1]), lambda n: (0, 0)),
        ],
        out_specs=pl.BlockSpec((4, SLOT, 256), lambda n: (n, 0, 0)),
        scratch_shapes=[pltpu.VMEM((ROWS, ROWS), BF), pltpu.VMEM((3, 8, ROWS), F32)],
        compiler_params=params(24),
        cost_estimate=cost(3 << 30, 8 << 20),
        name="value",
    )(inv, latent, w_value, w_step.T)
    gate = jnp.dot(latent, w_gate, preferred_element_type=F32).astype(BF)

    x_slots, own = lax.optimization_barrier((x_slots, own))
    oth = lax.ppermute(own, "seq", pairs)
    x_all = lax.all_to_all(x_slots, "seq", 0, 0, tiled=True)

    side = jnp.concatenate([own[:, QUAD + 4 : QUAD + 6, :16], oth[:, QUAD + 4 : QUAD + 6, :16]], 0)
    ab = side.astype(I32).reshape(-1)
    bc, code = pl.pallas_call(
        bc_body,
        out_shape=(
            jax.ShapeDtypeStruct((CH, 8 * ROWS), BF),
            jax.ShapeDtypeStruct((SEQ, ROWS), I32),
        ),
        in_specs=[smem(), smem(), vmem(), vmem(), vmem()],
        out_specs=(vmem(), vmem()),
        scratch_shapes=[pltpu.VMEM((KEYS, 256), BF), pltpu.VMEM((128, 128), F32)],
        compiler_params=params(24),
        cost_estimate=cost(1 << 30, 2 << 20),
        name="bc",
    )(at, ab, own, oth, conv_input_output)
    owns = [bc] + [
        lax.ppermute(bc, "mp", [(i, (i + k) % 4) for i in range(4)]) for k in range(1, 4)
    ]
    oths = [lax.ppermute(v, "seq", pairs) for v in owns]

    y_slots = pl.pallas_call(
        scan_body,
        out_shape=jax.ShapeDtypeStruct((SEQ, QUAD, 256), BF),
        in_specs=[smem()] * 5 + [vmem()] * 11,
        out_specs=vmem(),
        scratch_shapes=[
            pltpu.VMEM((2, 256, 8 * ROWS), BF),
            pltpu.VMEM((KEYS, 256), BF),
            pltpu.VMEM((KEYS, 128), BF),
            pltpu.VMEM((SEQ, 128, 128), BF),
            pltpu.VMEM((128, 128), F32),
            pltpu.VMEM((CH, SEQ * ROWS), BF),
            pltpu.VMEM((SEQ, ROWS), F32),
            pltpu.VMEM((SEQ, ROWS), F32),
            pltpu.VMEM((SEQ, QUAD, 256), F32),
        ],
        compiler_params=params(32),
        cost_estimate=cost(8 << 30, 8 << 20),
        name="scan",
    )(at, ab, step_bias, log_rate, skip_gain, code, x_all, conv_value, *owns, *oths)
    y_all = lax.all_to_all(y_slots, "seq", 0, 0, tiled=True)

    heads = step_bias.shape[0]
    return pl.pallas_call(
        final_body,
        grid=(heads,),
        out_shape=jax.ShapeDtypeStruct((ROWS, heads * 128), BF),
        in_specs=[
            pl.BlockSpec((1, ROWS), lambda h: (0, 0)),
            pl.BlockSpec((2, QUAD, 256), lambda h: (h, 0, 0)),
            pl.BlockSpec((ROWS, 128), lambda h: (0, h)),
            pl.BlockSpec((1, 128), lambda h: (0, h)),
        ],
        out_specs=pl.BlockSpec((ROWS, 128), lambda h: (0, h)),
        scratch_shapes=[pltpu.VMEM((ROWS, ROWS), BF)],
        compiler_params=params(24),
        cost_estimate=cost(1 << 30, 3 << 20),
        name="final",
    )(inv, y_all, gate, norm_gain.reshape(1, -1))


def solution(mesh):
    return jax.shard_map(
        body,
        mesh=mesh,
        in_specs=(
            P(("batch", "seq"), None),
            P("seq"),
            P("seq"),
            P(None, "mp"),
            P(None, "mp"),
            P(),
            P(None, "mp"),
            P(None, "mp"),
            P(),
            P("mp"),
            P("mp"),
            P("mp"),
            P("mp"),
        ),
        out_specs=P(("batch", "seq"), "mp"),
        check_vma=False,
    )
```

time: 327 us -> 155 us (0.47)
  waiting for transfers between devices: 143 us -> 52.1 us
  Pallas kernels: 0 us -> 51.1 us
  local copies, waits for them, and re-layouts: 47.6 us -> 16.7 us
  other arithmetic: 28.4 us -> 0.1 us
  starting transfers between devices: 56.2 us -> 28.9 us
  blocking collectives: 17.4 us -> 0 us
  between operations: 14 us -> 0.15 us
  matrix products: 18.3 us -> 5.53 us
    all_to_all x4 -> x3, waiting for transfers between devices: 139 us -> 30.5 us  [the longest x1 22.4 us: body(): y_all = lax.all_to_all(y_slots, 'seq', 0, 0, tiled=True)]
    pallas_call x0 -> x5, Pallas kernels: none -> 51.1 us  [the longest x1 29.7 us: body(): pl.pallas_call(scan_body, out_shape=jax.ShapeDtypeStruct((SEQ, QUAD, 256)...]
    all_to_all x4 -> x3, starting transfers between devices: 53.8 us -> 20.5 us  [the longest x1 9.02 us: body(): lax.all_to_all(bc_slots, 'seq', 0, 0, axis_index_groups=lines, tiled=True)]
    scatter x5 -> x0, local copies, waits for them, and re-layouts: 27.3 us -> none  [the longest x2 14.5 us: unpack_rows(): return blank.at[places].set(buffer, mode='drop')]
    ppermute x1 -> x8, waiting for transfers between devices: 0.01 us -> 21.6 us  [the longest x3 19.8 us: body(): lax.ppermute(bc, 'mp', [(i, (i + k) % 4) for i in range(4)])]
    all_gather x1 -> x0, blocking collectives: 17.4 us -> none  [carried_in(): gathered = jax.tree.map(lambda a: lax.all_gather(a, axis), part)]
    unnamed x58 -> x48, local copies, waits for them, and re-layouts: 2.47 us -> 16.6 us
    dot_general x8 -> x1, matrix products: 18.3 us -> 5.53 us  [body(): gate = jnp.dot(latent, w_gate, preferred_element_type=F32).astype(BF)]
  transfers between devices with their start and end apart: 6 -> 11, of which waited for: 3 -> 5; matrix products, arithmetic and copies ran while one was open for 17% -> 4% of each run, Pallas kernels for 0% -> 9%
where the time goes in v1:
time: 155 us
  waiting for transfers between devices  52.1 us (34%)
  Pallas kernels  51.1 us (33%)
  starting transfers between devices  28.9 us (19%)
  local copies, waits for them, and re-layouts  16.7 us (11%)
  matrix products  5.53 us (4%)
    pallas_call x1, Pallas kernels, body(): pl.pallas_call(scan_body, out_shape=jax.ShapeDtypeStruct((SEQ, QUAD, 256)...  29.7 us
    all_to_all x1, waiting for transfers between devices, body(): y_all = lax.all_to_all(y_slots, 'seq', 0, 0, tiled=True)  22.4 us
    ppermute x3, waiting for transfers between devices, body(): lax.ppermute(bc, 'mp', [(i, (i + k) % 4) for i in range(4)])  19.8 us
    unnamed x48, local copies, waits for them, and re-layouts  16.6 us
    all_to_all x1, starting transfers between devices, body(): lax.all_to_all(bc_slots, 'seq', 0, 0, axis_index_groups=lines, tiled=True)  9.02 us
    all_to_all x1, waiting for transfers between devices, body(): lax.all_to_all(bc_slots, 'seq', 0, 0, axis_index_groups=lines, tiled=True)  8.12 us
    all_to_all x1, starting transfers between devices, body(): y_all = lax.all_to_all(y_slots, 'seq', 0, 0, tiled=True)  7.54 us
    pallas_call x1, Pallas kernels, body(): pl.pallas_call(value_body, grid=(4,), out_shape=jax.ShapeDtypeStruct((SEQ...  7.44 us
  transfers between devices with their start and end apart: 11, of which 5 were waited for; matrix products, arithmetic and copies ran while one was open for 4% of the time, Pallas kernels for 9%

profile of v1, /device:TPU:1, one launch (start us, length us, event | category | flops | bytes accessed | tf_op | source)
XLA Modules:
  0.0 154.5 jit_solution(12810567784289447575)
XLA Ops:
  0.1 1.6 %copy-done.1 = bf16[512,2048]{1,0:T(8,128)(2,1)S(1)} copy-done((bf16[512,2048]{1,0:T(8,128)(2,1)S(1)}, bf16[512,2048]{1,0:T(8,128)(2,1)}, u32[]{:S(2)}) %copy-start.1) | copy-done | bytes 2097176
  1.7 1.2 copy-done.4
  4.3 2.6 %front.1 = bf16[8,144,256]{2,1,0:T(8,128)(2,1)} custom-call(s32[4]{0:T(128)S(1)} %pad_add_fusion.at_ref, s32[1,512]{1,0:T(1,128)S(1)} %bitcast.12, s32[1,512]{1,0:T(1,128)S(1)} %bitcast.11, bf16[512,2048]{1,0:T(8,128)(2,1)S(1)} %copy-done.1, bf16[2048,256]{1,0:T(8,128)(2,1)S(1)} %copy-done.4), custom_call_target="tpu_custom_call" | custom-call | flops 1073741824 | bytes 4194304 | tf_op jit(solution)/shard_map/front/pallas_call | solution.py:385
  6.9 9.0 %all-to-all-start = ((bf16[8,144,256]{2,1,0:T(8,128)(2,1)}), bf16[8,144,256]{2,1,0:T(8,128)(2,1)S(1)}, u32[]{:S(2)}, u32[]{:S(2)}) async-start(bf16[8,144,256]{2,1,0:T(8,128)(2,1)} %front.1), calls=%async_computation | async-start | bytes 1179648 | tf_op jit(solution)/shard_map/all_to_all | solution.py:394
  16.0 2.2 %copy-done = bf16[2048,1024]{1,0:T(8,128)(2,1)S(1)} copy-done((bf16[2048,1024]{1,0:T(8,128)(2,1)S(1)}, bf16[2048,1024]{1,0:T(8,128)(2,1)}, u32[]{:S(2)}) %copy-start) | copy-done | bytes 4194328
  18.1 1.6 %copy-done.2 = bf16[512,2048]{1,0:T(8,128)(2,1)S(1)} copy-done((bf16[512,2048]{1,0:T(8,128)(2,1)S(1)}, bf16[512,2048]{1,0:T(8,128)(2,1)}, u32[]{:S(2)}) %copy-start.2) | copy-done | bytes 2097176
  19.7 7.4 %value.1 = bf16[16,144,256]{2,1,0:T(8,128)(2,1)} custom-call(s32[1,512]{1,0:T(1,128)S(1)} %bitcast.13, bf16[512,2048]{1,0:T(8,128)(2,1)S(1)} %copy-done.2, bf16[2048,1024]{1,0:T(8,128)(2,1)S(1)} %copy-done, bf16[8,2048]{1,0:T(8,128)(2,1)S(1)} %bitcast.9), custom_call_target="tpu_custom_call" | custom-call | flops 3221225472 | bytes 8388608 | tf_op jit(solution)/shard_map/value/pallas_call | solution.py:396
  27.2 8.1 %all-to-all-done.own_ref = bf16[8,144,256]{2,1,0:T(8,128)(2,1)S(1)} async-done(((bf16[8,144,256]{2,1,0:T(8,128)(2,1)}), bf16[8,144,256]{2,1,0:T(8,128)(2,1)S(1)}, u32[]{:S(2)}, u32[]{:S(2)}) %all-to-all-start) | async-done | bytes 589856 | tf_op jit(solution)/shard_map/all_to_all | solution.py:394
  35.3 4.0 %all-to-all-start.1 = ((bf16[16,144,256]{2,1,0:T(8,128)(2,1)}), bf16[16,144,256]{2,1,0:T(8,128)(2,1)S(1)}, u32[]{:S(2)}, u32[]{:S(2)}) async-start(bf16[16,144,256]{2,1,0:T(8,128)(2,1)} %value.1), calls=%async_computation.1 | async-start | bytes 2359296 | tf_op jit(solution)/shard_map/all_to_all | solution.py:416
  39.6 1.8 %collective-permute-done.oth_ref = bf16[8,144,256]{2,1,0:T(8,128)(2,1)S(1)} collective-permute-done((bf16[8,144,256]{2,1,0:T(8,128)(2,1)S(1)}, bf16[8,144,256]{2,1,0:T(8,128)(2,1)S(1)}, u32[]{:S(2)}, u32[]{:S(2)}) %collective-permute-start) | collective-permute-done | bytes 589856 | tf_op jit(solution)/shard_map/ppermute | solution.py:415
  41.5 5.8 %bc.1 = (bf16[64,4096]{1,0:T(8,128)(2,1)S(1)}, s32[16,512]{1,0:T(8,128)S(1)}) custom-call(s32[4]{0:T(128)S(1)} %pad_add_fusion.at_ref, s32[512]{0:T(512)S(1)} %reshape.16.ab_ref, bf16[8,144,256]{2,1,0:T(8,128)(2,1)S(1)} %all-to-all-done.own_ref, bf16[8,144,256]{2,1,0:T(8,128)(2,1)S(1)} %collective-permute-done.oth_ref, f32[4,256]{1,0:T(4,128)S(1)} %copy-done.15), custom_call_target="tpu_custom_call" | custom-call | flops 1073741824 | bytes 2097152 | tf_op jit(solution)/shard_map/bc/pallas_call | solution.py:420
  47.4 1.3 collective-permute-start.1
  48.6 2.4 %collective-permute-start.2 = (bf16[64,4096]{1,0:T(8,128)(2,1)S(1)}, bf16[64,4096]{1,0:T(8,128)(2,1)S(1)}, u32[]{:S(2)}, u32[]{:S(2)}) collective-permute-start(bf16[64,4096]{1,0:T(8,128)(2,1)S(1)} %get-tuple-element.12.own0), channel_id=1, source_target_pairs={{0,8},{4,12},{8,0},{12,4},{1,9},{5,13},{9,1},{13,5},{2,10},{6,14},... | collective-permute-start | bytes 1572872 | tf_op jit(solution)/shard_map/ppermute | solution.py:434
  51.1 1.2 collective-permute-start.3
  52.2 1.1 collective-permute-start.4
  53.3 8.6 %collective-permute-done.1.own1 = bf16[64,4096]{1,0:T(8,128)(2,1)S(1)} collective-permute-done((bf16[64,4096]{1,0:T(8,128)(2,1)S(1)}, bf16[64,4096]{1,0:T(8,128)(2,1)S(1)}, u32[]{:S(2)}, u32[]{:S(2)}) %collective-permute-start.1) | collective-permute-done | bytes 524320 | tf_op jit(solution)/shard_map/ppermute | solution.py:434
  63.0 11.2 %collective-permute-done.2.own2 = bf16[64,4096]{1,0:T(8,128)(2,1)S(1)} collective-permute-done((bf16[64,4096]{1,0:T(8,128)(2,1)S(1)}, bf16[64,4096]{1,0:T(8,128)(2,1)S(1)}, u32[]{:S(2)}, u32[]{:S(2)}) %collective-permute-start.2) | collective-permute-done | bytes 524320 | tf_op jit(solution)/shard_map/ppermute | solution.py:434
  74.1 1.0 collective-permute-start.6
  82.6 29.7 %scan.1 = bf16[16,128,256]{2,1,0:T(8,128)(2,1)} custom-call(s32[4]{0:T(128)S(1)} %pad_add_fusion.at_ref, s32[512]{0:T(512)S(1)} %reshape.16.ab_ref, f32[8]{0:T(128)S(1)} %copy-done.20, f32[8]{0:T(128)S(1)} %copy-done.21, f32[8]{0:T(128)S(1)} %copy-done.22, s32[16,512]{1,0:T(8,128)S(1)} %get-tuple-element.10.code_ref, ...), custom_call_target="tpu_custom_call" | custom-call | flops 8589934592 | bytes 8388608 | tf_op jit(solution)/shard_map/scan/pallas_call | solution.py:438
  112.3 7.5 %all-to-all-start.2 = ((bf16[16,128,256]{2,1,0:T(8,128)(2,1)}), bf16[16,128,256]{2,1,0:T(8,128)(2,1)S(1)}, u32[]{:S(2)}, u32[]{:S(2)}) async-start(bf16[16,128,256]{2,1,0:T(8,128)(2,1)} %scan.1), calls=%async_computation.2 | async-start | bytes 2097152 | tf_op jit(solution)/shard_map/all_to_all | solution.py:458
  119.9 5.5 %convolution_convert_fusion.gate_ref = bf16[512,1024]{1,0:T(8,128)(2,1)} fusion(bf16[512,2048]{1,0:T(8,128)(2,1)S(1)} %copy-done.3, bf16[2048,1024]{1,0:T(8,128)(2,1)} %param.16), kind=kOutput, calls=%fused_computation | convolution fusion | flops 2148007936 | bytes 7340032 | tf_op jit(solution)/shard_map/dot_general | solution.py:412
  125.4 22.4 %all-to-all-done.2.y_ref = bf16[16,128,256]{2,1,0:T(8,128)(2,1)S(1)} async-done(((bf16[16,128,256]{2,1,0:T(8,128)(2,1)}), bf16[16,128,256]{2,1,0:T(8,128)(2,1)S(1)}, u32[]{:S(2)}, u32[]{:S(2)}) %all-to-all-start.2) | async-done | bytes 1048608 | tf_op jit(solution)/shard_map/all_to_all | solution.py:458
  147.8 1.2 copy-done.23
  149.0 5.5 %final.1 = bf16[512,1024]{1,0:T(8,128)(2,1)} custom-call(s32[1,512]{1,0:T(1,128)S(1)} %bitcast.14, bf16[16,128,256]{2,1,0:T(8,128)(2,1)S(1)} %all-to-all-done.2.y_ref, bf16[512,1024]{1,0:T(8,128)(2,1)S(1)} %copy-done.23, f32[1,1024]{1,0:T(1,128)S(1)} %bitcast.10), custom_call_target="tpu_custom_call" | custom-call | flops 1073741824 | bytes 3145728 | tf_op jit(solution)/shard_map/final/pallas_call | solution.py:461
  (57 shorter events, 10.3 us)
Async XLA Ops:
  0.1 1.6 %copy-start.1 = (bf16[512,2048]{1,0:T(8,128)(2,1)S(1)}, bf16[512,2048]{1,0:T(8,128)(2,1)}, u32[]{:S(2)}) copy-start(bf16[512,2048]{1,0:T(8,128)(2,1)} %lat_ref.3) | copy-start | bytes 6291460
  4.3 11.7 %copy-start.13 = (bf16[2048,8]{0,1:T(8,128)(2,1)S(1)}, bf16[2048,8]{0,1:T(8,128)(2,1)}, u32[]{:S(2)}) copy-start(bf16[2048,8]{0,1:T(8,128)(2,1)} %param.19) | copy-start | bytes 98308
  4.3 11.7 %copy-start.19 = (s32[512]{0:T(512)S(1)}, s32[512]{0:T(512)}, u32[]{:S(2)}) copy-start(s32[512]{0:T(512)} %param.15) | copy-start | bytes 6148
  6.9 28.4 %all-to-all-start = ((bf16[8,144,256]{2,1,0:T(8,128)(2,1)}), bf16[8,144,256]{2,1,0:T(8,128)(2,1)S(1)}, u32[]{:S(2)}, u32[]{:S(2)}) async-start(bf16[8,144,256]{2,1,0:T(8,128)(2,1)} %front.1), calls=%async_computation | async-start | bytes 1179648 | tf_op jit(solution)/shard_map/all_to_all | solution.py:394
  15.9 2.2 %copy-start = (bf16[2048,1024]{1,0:T(8,128)(2,1)S(1)}, bf16[2048,1024]{1,0:T(8,128)(2,1)}, u32[]{:S(2)}) copy-start(bf16[2048,1024]{1,0:T(8,128)(2,1)} %wv_ref.1) | copy-start | bytes 12582916
  18.1 1.6 %copy-start.2 = (bf16[512,2048]{1,0:T(8,128)(2,1)S(1)}, bf16[512,2048]{1,0:T(8,128)(2,1)}, u32[]{:S(2)}) copy-start(bf16[512,2048]{1,0:T(8,128)(2,1)} %lat_ref.3) | copy-start | bytes 6291460
  27.2 14.4 %copy-start.15 = (f32[4,256]{1,0:T(4,128)S(1)}, f32[4,256]{1,0:T(4,128)}, u32[]{:S(2)}) copy-start(f32[4,256]{1,0:T(4,128)} %conv_ref.2) | copy-start | bytes 12292
  35.3 43.1 %all-to-all-start.1 = ((bf16[16,144,256]{2,1,0:T(8,128)(2,1)}), bf16[16,144,256]{2,1,0:T(8,128)(2,1)S(1)}, u32[]{:S(2)}, u32[]{:S(2)}) async-start(bf16[16,144,256]{2,1,0:T(8,128)(2,1)} %value.1), calls=%async_computation.1 | async-start | bytes 2359296 | tf_op jit(solution)/shard_map/all_to_all | solution.py:416
  39.3 39.2 %copy-start.14 = (f32[4,1024]{1,0:T(4,128)S(1)}, f32[4,1024]{1,0:T(4,128)}, u32[]{:S(2)}) copy-start(f32[4,1024]{1,0:T(4,128)} %conv_ref.3) | copy-start | bytes 49156
  39.3 39.1 %copy-start.20 = (f32[8]{0:T(128)S(1)}, f32[8]{0:T(128)}, u32[]{:S(2)}) copy-start(f32[8]{0:T(128)} %bias_ref.1) | copy-start | bytes 100
  39.3 39.1 %copy-start.21 = (f32[8]{0:T(128)S(1)}, f32[8]{0:T(128)}, u32[]{:S(2)}) copy-start(f32[8]{0:T(128)} %rate_ref.1) | copy-start | bytes 100
  39.3 39.1 %copy-start.22 = (f32[8]{0:T(128)S(1)}, f32[8]{0:T(128)}, u32[]{:S(2)}) copy-start(f32[8]{0:T(128)} %skip_ref.1) | copy-start | bytes 100
  39.3 2.1 %collective-permute-start = (bf16[8,144,256]{2,1,0:T(8,128)(2,1)S(1)}, bf16[8,144,256]{2,1,0:T(8,128)(2,1)S(1)}, u32[]{:S(2)}, u32[]{:S(2)}) collective-permute-start(bf16[8,144,256]{2,1,0:T(8,128)(2,1)S(1)} %all-to-all-done.own_ref), channel_id=1, source_target_pairs={{0,16},{16,0},{32,48},{48,32},{64,80},{80,64},{96,112},{112,96},{1... | collective-permute-start | bytes 1769480 | tf_op jit(solution)/shard_map/ppermute | solution.py:415
  47.4 14.6 %collective-permute-start.1 = (bf16[64,4096]{1,0:T(8,128)(2,1)S(1)}, bf16[64,4096]{1,0:T(8,128)(2,1)S(1)}, u32[]{:S(2)}, u32[]{:S(2)}) collective-permute-start(bf16[64,4096]{1,0:T(8,128)(2,1)S(1)} %get-tuple-element.12.own0), channel_id=1, source_target_pairs={{0,4},{4,8},{8,12},{12,0},{1,5},{5,9},{9,13},{13,1},{2,6},{6,10},{... | collective-permute-start | bytes 1572872 | tf_op jit(solution)/shard_map/ppermute | solution.py:434
  48.6 25.5 %collective-permute-start.2 = (bf16[64,4096]{1,0:T(8,128)(2,1)S(1)}, bf16[64,4096]{1,0:T(8,128)(2,1)S(1)}, u32[]{:S(2)}, u32[]{:S(2)}) collective-permute-start(bf16[64,4096]{1,0:T(8,128)(2,1)S(1)} %get-tuple-element.12.own0), channel_id=1, source_target_pairs={{0,8},{4,12},{8,0},{12,4},{1,9},{5,13},{9,1},{13,5},{2,10},{6,14},... | collective-permute-start | bytes 1572872 | tf_op jit(solution)/shard_map/ppermute | solution.py:434
  51.1 24.1 %collective-permute-start.3 = (bf16[64,4096]{1,0:T(8,128)(2,1)S(1)}, bf16[64,4096]{1,0:T(8,128)(2,1)S(1)}, u32[]{:S(2)}, u32[]{:S(2)}) collective-permute-start(bf16[64,4096]{1,0:T(8,128)(2,1)S(1)} %get-tuple-element.12.own0), channel_id=1, source_target_pairs={{0,12},{4,0},{8,4},{12,8},{1,13},{5,1},{9,5},{13,9},{2,14},{6,2},{... | collective-permute-start | bytes 1572872 | tf_op jit(solution)/shard_map/ppermute | solution.py:434
  52.2 23.0 %collective-permute-start.4 = (bf16[64,4096]{1,0:T(8,128)(2,1)S(1)}, bf16[64,4096]{1,0:T(8,128)(2,1)S(1)}, u32[]{:S(2)}, u32[]{:S(2)}) collective-permute-start(bf16[64,4096]{1,0:T(8,128)(2,1)S(1)} %get-tuple-element.12.own0), channel_id=1, source_target_pairs={{0,16},{16,0},{32,48},{48,32},{64,80},{80,64},{96,112},{112,96},{1... | collective-permute-start | bytes 1572872 | tf_op jit(solution)/shard_map/ppermute | solution.py:436
  62.0 14.1 %collective-permute-start.5 = (bf16[64,4096]{1,0:T(8,128)(2,1)S(1)}, bf16[64,4096]{1,0:T(8,128)(2,1)S(1)}, u32[]{:S(2)}, u32[]{:S(2)}) collective-permute-start(bf16[64,4096]{1,0:T(8,128)(2,1)S(1)} %collective-permute-done.1.own1), channel_id=1, source_target_pairs={{0,16},{16,0},{32,48},{48,32},{64,80},{80,64},{96,112},{112,96},{1... | collective-permute-start | bytes 1572872 | tf_op jit(solution)/shard_map/ppermute | solution.py:436
  74.1 2.7 %collective-permute-start.6 = (bf16[64,4096]{1,0:T(8,128)(2,1)S(1)}, bf16[64,4096]{1,0:T(8,128)(2,1)S(1)}, u32[]{:S(2)}, u32[]{:S(2)}) collective-permute-start(bf16[64,4096]{1,0:T(8,128)(2,1)S(1)} %collective-permute-done.2.own2), channel_id=1, source_target_pairs={{0,16},{16,0},{32,48},{48,32},{64,80},{80,64},{96,112},{112,96},{1... | collective-permute-start | bytes 1572872 | tf_op jit(solution)/shard_map/ppermute | solution.py:436
  75.2 2.4 %collective-permute-start.7 = (bf16[64,4096]{1,0:T(8,128)(2,1)S(1)}, bf16[64,4096]{1,0:T(8,128)(2,1)S(1)}, u32[]{:S(2)}, u32[]{:S(2)}) collective-permute-start(bf16[64,4096]{1,0:T(8,128)(2,1)S(1)} %collective-permute-done.3.own3), channel_id=1, source_target_pairs={{0,16},{16,0},{32,48},{48,32},{64,80},{80,64},{96,112},{112,96},{1... | collective-permute-start | bytes 1572872 | tf_op jit(solution)/shard_map/ppermute | solution.py:436
  112.3 7.5 %copy-start.3 = (bf16[512,2048]{1,0:T(8,128)(2,1)S(1)}, bf16[512,2048]{1,0:T(8,128)(2,1)}, u32[]{:S(2)}) copy-start(bf16[512,2048]{1,0:T(8,128)(2,1)} %lat_ref.3) | copy-start | bytes 6291460
  112.3 35.5 %all-to-all-start.2 = ((bf16[16,128,256]{2,1,0:T(8,128)(2,1)}), bf16[16,128,256]{2,1,0:T(8,128)(2,1)S(1)}, u32[]{:S(2)}, u32[]{:S(2)}) async-start(bf16[16,128,256]{2,1,0:T(8,128)(2,1)} %scan.1), calls=%async_computation.2 | async-start | bytes 2097152 | tf_op jit(solution)/shard_map/all_to_all | solution.py:458
  119.9 27.9 %copy-start.16 = (f32[1024]{0:T(1024)S(1)}, f32[1024]{0:T(1024)}, u32[]{:S(2)}) copy-start(f32[1024]{0:T(1024)} %param.25) | copy-start | bytes 12292
  147.8 1.2 copy-start.23
  (11 other events, 10.0 us)

commit v2 on v1

v2 whole, which is shorter than its diff:
```python
import jax
import jax.numpy as jnp
from jax import lax
from jax.experimental import pallas as pl
from jax.experimental.pallas import tpu as pltpu
from jax.sharding import PartitionSpec as P

F32, BF, I32 = jnp.float32, jnp.bfloat16, jnp.int32
ROWS = 512
SEQ = 16
QUAD = ROWS // 4
SLOT = QUAD + 16
WIN = 32
KEYS = SEQ * WIN
CH = 64
BLOCK = 256
BC = 128
MIB = 1 << 20


def iota(shape, dim):
    return lax.broadcasted_iota(I32, shape, dim)


def dot(a, b, dims=((1,), (0,))):
    return lax.dot_general(a, b, (dims, ((), ())), preferred_element_type=F32)


def column(row):
    return jnp.transpose(jnp.broadcast_to(row, (128, row.shape[1])))


def tiles(row):
    return [row[:, g : g + 128] for g in range(0, row.shape[1], 128)]


def sorted_place(inv, inv_col):
    rank = jnp.concatenate(
        [jnp.sum((inv_col < part).astype(F32), axis=0, keepdims=True) for part in tiles(inv)],
        axis=1,
    )
    packed = jnp.floor(rank * 0.25)
    return (rank - 4.0 * packed) * QUAD + packed


def one_hot(place, count):
    row = iota((count, place.shape[1]), 0).astype(jnp.int16)
    return jnp.where(row == place.astype(I32).astype(jnp.int16), BF(1), BF(0))


def stacked(rows, shape):
    place = iota(shape, 0)
    block = jnp.zeros(shape, F32)
    for index, row in enumerate(rows):
        block = jnp.where(place == index, row, block)
    return block


def side_by_side(low, high):
    first = iota((QUAD, 128), 1) < 64
    return [
        jnp.where(first, low[u : u + QUAD], high[u + QUAD : u + 2 * QUAD]) for u in (0, 2 * QUAD)
    ]


def front_body(
    at_ref,
    inv_hbm,
    ord_hbm,
    lat_hbm,
    wio_hbm,
    ws_ref,
    out_ref,
    inv_ref,
    ord_ref,
    lat_ref,
    wio_ref,
    sem_ref,
):
    small = [
        pltpu.make_async_copy(inv_hbm, inv_ref, sem_ref.at[0]),
        pltpu.make_async_copy(ord_hbm, ord_ref, sem_ref.at[1]),
    ]
    large = []
    for k in range(4):
        part = pl.ds(512 * k, 512)
        large.append(
            (
                pltpu.make_async_copy(lat_hbm.at[:, part], lat_ref.at[:, part], sem_ref.at[2 + k]),
                pltpu.make_async_copy(wio_hbm.at[part], wio_ref.at[part], sem_ref.at[6 + k]),
            )
        )
    for copy in small:
        copy.start()
    for pair in large:
        for copy in pair:
            copy.start()
    for copy in small:
        copy.wait()
    inv = inv_ref[...].astype(F32)
    inv_col = column(inv)
    deal = one_hot(sorted_place(inv, inv_col), ROWS)
    source = (ord_ref[...] >> 9).astype(F32)
    source_col = column(source)
    earlier = [
        jnp.sum(
            jnp.where(
                (source_col == part) & (iota((ROWS, 128), 0) < iota((ROWS, 128), 1) + 128 * g),
                1.0,
                0.0,
            ),
            axis=0,
            keepdims=True,
        )
        for g, part in enumerate(tiles(source))
    ]
    bound = (iota((ROWS, 128), 1) * ROWS).astype(F32)
    start = jnp.sum((inv_col < bound).astype(F32), axis=0, keepdims=True)
    tile = jnp.minimum(jnp.floor(start * (1.0 / 64.0)), 6.0)
    offset = start - 64.0 * tile
    blank = jnp.zeros((1, 128), F32)
    rows = [
        source[:, :256],
        source[:, 256:],
        jnp.concatenate(earlier[:2], axis=1),
        jnp.concatenate(earlier[2:], axis=1),
        jnp.concatenate([tile, blank], axis=1),
        jnp.concatenate([offset, blank], axis=1),
    ]
    io = jnp.zeros((ROWS, 256), F32)
    rest = jnp.zeros((ROWS, 128), F32)
    ws = jnp.concatenate([ws_ref[...], jnp.zeros((120, ws_ref.shape[1]), BF)], axis=0)
    for k, pair in enumerate(large):
        for copy in pair:
            copy.wait()
        part = slice(512 * k, 512 * k + 512)
        io = io + dot(lat_ref[:, part], wio_ref[part, :])
        rest = rest + dot(lat_ref[:, part], ws[:, part], ((1,), (1,)))
    io = dot(deal, io.astype(BF))
    rest = jnp.transpose(rest)[:8]
    pieces = []
    for _ in range(3):
        piece = rest.astype(BF)
        pieces.append(piece.astype(F32))
        rest = rest - pieces[-1]
    pieces = jnp.concatenate(pieces + [rest], axis=0).astype(BF)
    dealt = dot(pieces, deal, ((1,), (1,)))
    steps = [dealt[8 * k : 8 * k + 8] for k in range(3)]
    m = at_ref[0]
    half = jnp.where(m >= 2, io[:, 128:], io[:, :128])
    turned = pltpu.roll(half, 64, 1)
    odd = m % 2 == 1
    packed = side_by_side(jnp.where(odd, turned, half), jnp.where(odd, half, turned))
    slot = jnp.concatenate(packed, axis=1).astype(BF)
    for head in range(out_ref.shape[0]):
        halves = []
        for step in steps:
            own = step[head : head + 1]
            halves += [own[:, :256], own[:, 256:]]
        out_ref[head, :QUAD, :] = slot
        out_ref[head, QUAD:, :] = stacked(rows + halves, (16, 256)).astype(BF)


def value_body(inv_ref, lat_ref, wv_ref, out_ref, deal_ref):
    @pl.when(pl.program_id(0) == 0)
    def _():
        inv = inv_ref[...].astype(F32)
        deal_ref[...] = one_hot(sorted_place(inv, column(inv)), ROWS)

    value = dot(lat_ref[...], wv_ref[...]).astype(BF)
    value = dot(deal_ref[...], value)
    for jj in range(4):
        group = value[:, 128 * (jj // 2) : 128 * (jj // 2) + 128]
        turned = pltpu.roll(group, 64, 1)
        packed = side_by_side(group, turned) if jj % 2 == 0 else side_by_side(turned, group)
        out_ref[jj] = jnp.concatenate(packed, axis=1).astype(BF)


def silu(x):
    half = 0.5 * x
    return half + half * jnp.tanh(half)


def conv_silu(cur, prev, taps):
    ext = jnp.concatenate([prev, cur], axis=1)
    total = cur * taps[3]
    for back in range(1, 4):
        total = total + pltpu.roll(ext, back, 1)[:, 128:] * taps[3 - back]
    return silu(total)


def pick_quarter(res, quarter):
    out = jnp.zeros((CH, res.shape[1]), F32)
    for q in range(4):
        out = out + jnp.where(quarter == q, res[CH * q : CH * q + CH], 0.0)
    return out


def code_body(at_ref, ab_ref, own_ref, oth_ref, code_ref):
    c = at_ref[1]
    for z in range(8):
        for ref, core in ((own_ref, c), (oth_ref, 1 - c)):
            d = 2 * z + core
            side = ref[z, QUAD:SLOT, :].astype(F32)
            source = jnp.concatenate([side[0:1], side[1:2]], axis=1).astype(I32)
            place = jnp.concatenate([side[2:3], side[3:4]], axis=1).astype(I32)
            for s in range(SEQ):
                j = (s >> 1) + 8 * ((s + c) % 2)
                place = place + jnp.where(source == s, ab_ref[32 * j + 16 + d], 0)
            code_ref[pl.ds(d, 1), :] = source * 128 + place


def bc_body(
    at_ref, ab_ref, own_ref, oth_ref, conv_ref, out_a, out_b, code_ref, win_ref, tap_ref
):
    code_body(at_ref, ab_ref, own_ref, oth_ref, code_ref)
    m, c = at_ref[0], at_ref[1]
    group = conv_ref[:, pl.ds(pl.multiple_of(128 * (m // 2), 128), 128)]
    tap_ref[...] = jnp.transpose(stacked([group[k : k + 1] for k in range(4)], (128, 128)))
    tap_cols = tap_ref[pl.ds(pl.multiple_of(64 * (m % 2), 64), 64), :]
    taps = [tap_cols[:, k : k + 1] for k in range(4)]

    def rows_of(d, lo, hi):
        for j in range(SEQ):
            ref = own_ref if j < 8 else oth_ref
            at = pl.multiple_of(16 * ab_ref[32 * j + d], 16)
            win_ref[WIN * j : WIN * j + WIN, :] = ref[j % 8, pl.ds(at, WIN), :]
        code = code_ref[pl.ds(d, 1), :][:, lo:hi]
        source = code >> 7
        j_of = (source >> 1) + 8 * ((source + c) & 1)
        key = j_of * WIN + ((code >> 2) & (WIN - 1))
        spread = one_hot(key, KEYS)
        return pick_quarter(dot(win_ref[...], spread, ((0,), (0,))), code & 3)

    first = 8 * c
    prev = rows_of(jnp.maximum(first - 1, 0), ROWS - 128, ROWS)
    prev = jnp.where(first > 0, prev, 0.0)

    for e in range(8):
        cur = rows_of(first + e, 0, ROWS)
        out_ref = out_a if e < 4 else out_b
        out_ref[:, ROWS * (e % 4) : ROWS * (e % 4) + ROWS] = conv_silu(cur, prev, taps).astype(BF)
        prev = cur[:, ROWS - 128 :]


def tile_at(ab_ref, c, s, d):
    j = (s >> 1) + 8 * ((s + c) % 2)
    return pl.multiple_of(16 * ab_ref[32 * j + d], 16)


def time_body(
    at_ref, ab_ref, bias_ref, rate_ref, skip_ref, code_ref, own_ref, oth_ref, conv_ref,
    table_ref, win_ref, col_ref, step_ref, tap_ref
):
    c, sq = at_ref[1], at_ref[2]
    head = sq // 2
    group = conv_ref[:, pl.ds(pl.multiple_of(128 * head, 128), 128)]
    tap_ref[...] = jnp.transpose(stacked([group[k : k + 1] for k in range(4)], (128, 128)))
    table_ref[64:, :128] = tap_ref[pl.ds(pl.multiple_of(64 * (sq % 2), 64), 64), :]
    table_ref[0:SEQ, :] = code_ref[...].astype(F32)
    table_ref[48:64, :] = jnp.full((16, ROWS), skip_ref[head], F32)
    for core, ref in enumerate((own_ref, oth_ref)):
        blocks = []
        for z in range(8):
            side = ref[z, QUAD:SLOT, :].astype(F32)
            side = pltpu.roll(side, 10, 0)[0:8]
            blocks += [side[:, :128], side[:, 128:]]
        turned = jnp.transpose(jnp.concatenate(blocks, axis=0))
        for z in range(8):
            own = turned if z == 0 else pltpu.roll(turned, 128 - 16 * z, 1)
            col_ref[8 * core + z] = own.astype(BF)

    def gather(d, carry):
        for j in range(SEQ):
            at = pl.multiple_of(16 * ab_ref[32 * j + d], 16)
            win_ref[WIN * j : WIN * j + WIN, :] = col_ref[j, pl.ds(at, WIN), :]
        code = code_ref[pl.ds(d, 1), :]
        source = code >> 7
        j_of = (source >> 1) + 8 * ((source + c) & 1)
        spread = one_hot(j_of * WIN + ((code >> 2) & (WIN - 1)), KEYS)
        quarter = code & 3
        parts = dot(win_ref[...], spread, ((0,), (0,)))
        step = jnp.zeros((1, ROWS), F32)
        for q in range(4):
            row = (q >> 1) + 8 * (q & 1)
            value = parts[row : row + 1] + parts[row + 2 : row + 3] + parts[row + 4 : row + 5]
            step = step + jnp.where(quarter == q, value, 0.0)
        step_ref[pl.ds(d, 1), :] = step
        return carry

    lax.fori_loop(0, SEQ, gather, 0, unroll=4)

    raw = step_ref[...] + bias_ref[head]
    size = jnp.maximum(raw, 0.0) + jnp.log1p(jnp.exp(-jnp.abs(raw)))
    table_ref[SEQ : 2 * SEQ, :] = size
    rate = jnp.exp(jnp.full((1, ROWS), rate_ref[head], F32))
    cum = -rate * size
    lane = iota((SEQ, ROWS), 1) & (BLOCK - 1)
    shift = 1
    while shift < BLOCK:
        cum = cum + jnp.where(lane >= shift, pltpu.roll(cum, shift, 1), 0.0)
        shift *= 2
    table_ref[2 * SEQ : 3 * SEQ, :] = cum


def gate_body(lat_ref, w_ref, out_ref):
    out_ref[...] = silu(dot(lat_ref[...], w_ref[...])).astype(BF)


def spread_of(table_ref, d):
    code = table_ref[pl.ds(d, 1), :].astype(I32)
    return one_hot((code >> 7) * WIN + ((code >> 2) & (WIN - 1)), KEYS), code & 3


def place_half(first, prev, at_ref, ab_ref, table_ref, x_ref, xact_ref, win_ref):
    c = at_ref[1]
    taps = [table_ref[64:, k : k + 1] for k in range(4)]

    def gather(e, prev):
        d = first + e
        for s in range(SEQ):
            at = tile_at(ab_ref, c, s, d)
            win_ref[WIN * s : WIN * s + WIN, :] = x_ref[s, pl.ds(at, WIN), :]
        spread, quarter = spread_of(table_ref, d)
        cur = pick_quarter(dot(win_ref[...], spread, ((0,), (0,))), quarter)
        act = conv_silu(cur, prev, taps)
        xact_ref[:, pl.ds(pl.multiple_of(ROWS * e, ROWS), ROWS)] = act.astype(BF)
        return cur[:, ROWS - 128 :]

    return lax.fori_loop(0, SEQ // 2, gather, prev, unroll=4)


def place_first(at_ref, ab_ref, table_ref, x_ref, xact_ref, last_ref, win_ref):
    prev = jnp.zeros((CH, 128), F32)
    last_ref[...] = place_half(0, prev, at_ref, ab_ref, table_ref, x_ref, xact_ref, win_ref)


def place_second(at_ref, ab_ref, table_ref, x_ref, last_ref, xact_ref, win_ref):
    place_half(8, last_ref[...], at_ref, ab_ref, table_ref, x_ref, xact_ref, win_ref)


def scan_body(at_ref, ab_ref, table_ref, xact_a, xact_b, *refs):
    owns, oths = refs[:8], refs[8:16]
    out_ref, bc_ref, acc_ref, sem_ref = refs[16:]
    m, c = at_ref[0], at_ref[1]
    copies = []
    for index in range(8):
        rows = pl.ds(pl.multiple_of(CH * ((m - index // 2 + 4) % 4), CH), CH)
        cols = pl.ds(4 * ROWS * (index % 2), 4 * ROWS)
        for side, ref in enumerate((owns[index], oths[index])):
            half = c if side == 0 else 1 - c
            copies.append(
                pltpu.make_async_copy(ref, bc_ref.at[half, rows, cols], sem_ref.at[index, side])
            )
    for copy in copies:
        copy.start()
    acc_ref[...] = jnp.zeros_like(acc_ref)
    skip = table_ref[48:49, :BLOCK]
    causal = iota((BLOCK, BLOCK), 0) <= iota((BLOCK, BLOCK), 1)
    for copy in copies:
        copy.wait()

    def scan(half, e, state):
        d = 8 * half + e
        cols = pl.ds(pl.multiple_of(ROWS * e, ROWS), ROWS)
        x_all = (xact_b if half else xact_a)[:, cols].astype(F32)
        bc = bc_ref[half, :, cols]
        size_all = table_ref[pl.ds(SEQ + d, 1), :]
        cum_all = table_ref[pl.ds(2 * SEQ + d, 1), :]
        ys = []
        for k in range(ROWS // BLOCK):
            at = slice(BLOCK * k, BLOCK * k + BLOCK)
            x, b, cc = x_all[:, at], bc[:BC, at], bc[BC:, at]
            cum_row, size = cum_all[:, at], size_all[:, at]
            scores = dot(b, cc, ((0,), (0,)))
            col = column(cum_row)
            gap = cum_row - jnp.concatenate([col] * (BLOCK // 128), axis=1)
            weight = (scores * jnp.exp(jnp.where(causal, gap, -1e30))).astype(BF)
            y = dot((x * size).astype(BF), weight)
            y = y + dot(state.astype(BF), cc) * jnp.exp(cum_row) + skip * x
            ys.append(y)
            total = cum_row[:, BLOCK - 1 :]
            scaled = (x * (jnp.exp(total - cum_row) * size)).astype(BF)
            state = jnp.exp(total) * state + dot(scaled, b, ((1,), (1,)))
        y_all = jnp.concatenate(ys, axis=1)
        spread, quarter = spread_of(table_ref, d)
        apart = jnp.concatenate(
            [jnp.where(quarter == q, y_all, 0.0).astype(BF) for q in range(4)], axis=0
        )
        back = dot(spread, apart, ((1,), (1,)))
        for s in range(SEQ):
            at = pl.ds(tile_at(ab_ref, c, s, d), WIN)
            acc_ref[s, at, :] = acc_ref[s, at, :] + back[WIN * s : WIN * s + WIN]
        return state

    state = jnp.zeros((CH, BC), F32)
    for half in range(2):
        state = lax.fori_loop(0, 8, lambda e, state, half=half: scan(half, e, state), state, unroll=4)
    out_ref[...] = acc_ref[...].astype(BF)


def final_body(inv_ref, y_ref, gate_hbm, gain_ref, out_ref, pick_ref, gate_ref, sem_ref):
    h = pl.program_id(0)

    def gate_copy(n):
        part = pl.ds(pl.multiple_of(256 * n, 256), 256)
        return pltpu.make_async_copy(gate_hbm.at[:, part], gate_ref.at[n], sem_ref.at[n])

    @pl.when(h == 0)
    def _():
        for n in range(gate_ref.shape[0]):
            gate_copy(n).start()
        inv = inv_ref[...].astype(F32)
        place = column(sorted_place(inv, column(inv)))
        lane = iota((ROWS, 128), 1)
        for g in range(4):
            hit = place == (lane + 128 * g).astype(F32)
            pick_ref[:, 128 * g : 128 * g + 128] = hit.astype(F32).astype(BF)

    low = iota((QUAD, 128), 1) < 64
    heads = []
    for n in range(2):
        rows = []
        for q in range(4):
            at = slice(128 * (q // 2), 128 * (q // 2) + 128)
            even = y_ref[4 * h + 2 * n, :, at].astype(F32)
            odd = y_ref[4 * h + 2 * n + 1, :, at].astype(F32)
            if q % 2 == 0:
                rows.append(jnp.where(low, even, pltpu.roll(odd, 64, 1)))
            else:
                rows.append(jnp.where(low, pltpu.roll(even, 64, 1), odd))
        heads.append(jnp.concatenate(rows, axis=0).astype(BF))
    y = dot(pick_ref[...], jnp.concatenate(heads, axis=1))
    gate_copy(h).wait()
    for n in range(2):
        at = slice(128 * n, 128 * n + 128)
        gated = y[:, at] * gate_ref[h, :, at].astype(F32)
        mean = jnp.mean(gated * gated, axis=1, keepdims=True)
        out_ref[:, at] = (gated * lax.rsqrt(mean + 1e-5) * gain_ref[:, at]).astype(BF)


def vmem(*_):
    return pl.BlockSpec(memory_space=pltpu.VMEM)


def hbm(*_):
    return pl.BlockSpec(memory_space=pl.ANY)


def smem(*_):
    return pl.BlockSpec(memory_space=pltpu.SMEM)


def params(mib):
    return pltpu.CompilerParams(vmem_limit_bytes=mib * MIB)


def cost(flops, data, exps=0):
    return pl.CostEstimate(flops=flops, bytes_accessed=data, transcendentals=exps)


def run_time(*args):
    return pl.pallas_call(
        time_body,
        out_shape=jax.ShapeDtypeStruct((128, ROWS), F32),
        in_specs=[smem()] * 5 + [vmem()] * 4,
        out_specs=vmem(),
        scratch_shapes=[
            pltpu.VMEM((KEYS, 128), BF),
            pltpu.VMEM((SEQ, 128, 128), BF),
            pltpu.VMEM((SEQ, ROWS), F32),
            pltpu.VMEM((128, 128), F32),
        ],
        compiler_params=params(8),
        cost_estimate=cost(2 << 30, 2 << 20),
        name="time",
    )(*args)


def run_place(kernel, outs, *args):
    return pl.pallas_call(
        kernel,
        out_shape=outs,
        in_specs=[smem()] * 2 + [vmem()] * (len(args) - 2),
        out_specs=tuple(vmem() for _ in outs),
        scratch_shapes=[pltpu.VMEM((KEYS, 256), BF)],
        compiler_params=params(24),
        cost_estimate=cost(2 << 30, 2 << 20),
        name="place",
    )(*args)


def run_scan(*args):
    return pl.pallas_call(
        scan_body,
        out_shape=jax.ShapeDtypeStruct((SEQ, QUAD, 256), BF),
        in_specs=[smem()] * 2 + [vmem()] * 3 + [hbm()] * 16,
        out_specs=vmem(),
        scratch_shapes=[
            pltpu.VMEM((2, 256, 8 * ROWS), BF),
            pltpu.VMEM((SEQ, QUAD, 256), F32),
            pltpu.SemaphoreType.DMA((8, 2)),
        ],
        compiler_params=params(24),
        cost_estimate=cost(8 << 30, 8 << 20),
        name="scan",
    )(*args)


def run_front(*args):
    return pl.pallas_call(
        front_body,
        out_shape=jax.ShapeDtypeStruct((8, SLOT, 256), BF),
        in_specs=[smem(), hbm(), hbm(), hbm(), hbm(), vmem()],
        out_specs=vmem(),
        scratch_shapes=[
            pltpu.VMEM((1, ROWS), I32),
            pltpu.VMEM((1, ROWS), I32),
            pltpu.VMEM(args[3].shape, BF),
            pltpu.VMEM(args[4].shape, BF),
            pltpu.SemaphoreType.DMA((10,)),
        ],
        compiler_params=params(60),
        cost_estimate=cost(1 << 30, 4 << 20),
        name="front",
    )(*args)


def body(
    latent,
    order,
    inverse,
    w_gate,
    w_value,
    w_input_output,
    w_step,
    conv_value,
    conv_input_output,
    step_bias,
    log_rate,
    skip_gain,
    norm_gain,
):
    m, sq = lax.axis_index("mp"), lax.axis_index("seq")
    at = jnp.stack([m, sq % 2, sq, m]).astype(I32)
    inv = inverse.reshape(1, ROWS)
    pairs = [(i, i ^ 1) for i in range(SEQ)]
    lines = [[2 * i + core for i in range(SEQ // 2)] for core in range(2)]

    bc_slots = run_front(at, inv, order.reshape(1, ROWS), latent, w_input_output, w_step.T)
    own = lax.all_to_all(bc_slots, "seq", 0, 0, axis_index_groups=lines, tiled=True)

    x_slots = pl.pallas_call(
        value_body,
        grid=(4,),
        out_shape=jax.ShapeDtypeStruct((SEQ, QUAD, 256), BF),
        in_specs=[
            pl.BlockSpec((1, ROWS), lambda n: (0, 0)),
            pl.BlockSpec((ROWS, latent.shape[1]), lambda n: (0, 0)),
            pl.BlockSpec((latent.shape[1], 256), lambda n: (0, n)),
        ],
        out_specs=pl.BlockSpec((4, QUAD, 256), lambda n: (n, 0, 0)),
        scratch_shapes=[pltpu.VMEM((ROWS, ROWS), BF)],
        compiler_params=params(24),
        cost_estimate=cost(3 << 30, 8 << 20),
        name="value",
    )(inv, latent, w_value)
    gate = pl.pallas_call(
        gate_body,
        grid=(4,),
        out_shape=jax.ShapeDtypeStruct((ROWS, w_gate.shape[1]), BF),
        in_specs=[
            pl.BlockSpec((ROWS, latent.shape[1]), lambda n: (0, 0)),
            pl.BlockSpec((latent.shape[1], 256), lambda n: (0, n)),
        ],
        out_specs=pl.BlockSpec((ROWS, 256), lambda n: (0, n)),
        compiler_params=params(24),
        cost_estimate=cost(2 << 30, 8 << 20),
        name="gate",
    )(latent, w_gate)

    x_slots, own = lax.optimization_barrier((x_slots, own))
    oth = lax.ppermute(own, "seq", pairs)
    x_all = lax.all_to_all(x_slots, "seq", 0, 0, tiled=True)

    side = jnp.concatenate([own[:, QUAD + 4 : QUAD + 6, :16], oth[:, QUAD + 4 : QUAD + 6, :16]], 0)
    ab = side.astype(I32).reshape(-1)
    half = jax.ShapeDtypeStruct((CH, 4 * ROWS), BF)
    bc_a, bc_b, code = pl.pallas_call(
        bc_body,
        out_shape=(half, half, jax.ShapeDtypeStruct((SEQ, ROWS), I32)),
        in_specs=[smem(), smem(), vmem(), vmem(), vmem()],
        out_specs=(vmem(), vmem(), vmem()),
        scratch_shapes=[pltpu.VMEM((KEYS, 256), BF), pltpu.VMEM((128, 128), F32)],
        compiler_params=params(8),
        cost_estimate=cost(1 << 30, 2 << 20),
        name="bc",
    )(at, ab, own, oth, conv_input_output)
    up = [(i, (i + 1) % 4) for i in range(4)]
    down = [(i, (i - 1) % 4) for i in range(4)]
    one_a, three_b = lax.ppermute(bc_a, "mp", up), lax.ppermute(bc_b, "mp", down)
    one_b, three_a = lax.ppermute(bc_b, "mp", up), lax.ppermute(bc_a, "mp", down)
    table = run_time(at, ab, step_bias, log_rate, skip_gain, code, own, oth, conv_value)
    one_a, three_b, table = lax.optimization_barrier((one_a, three_b, table))
    two_a, two_b = lax.ppermute(one_a, "mp", up), lax.ppermute(three_b, "mp", down)
    owns = [bc_a, bc_b, one_a, one_b, two_a, two_b, three_a, three_b]
    part = jax.ShapeDtypeStruct((CH, 8 * ROWS), BF)
    last = jax.ShapeDtypeStruct((CH, 128), F32)
    xact_a, last = run_place(place_first, (part, last), at, ab, table, x_all)
    owns, xact_a = lax.optimization_barrier((owns, xact_a))
    oths = [lax.ppermute(v, "seq", pairs) for v in owns]
    (xact_b,) = run_place(place_second, (part,), at, ab, table, x_all, last)
    y_slots = run_scan(at, ab, table, xact_a, xact_b, *owns, *oths)
    y_all = lax.all_to_all(y_slots, "seq", 0, 0, tiled=True)

    heads = step_bias.shape[0]
    return pl.pallas_call(
        final_body,
        grid=(heads // 2,),
        out_shape=jax.ShapeDtypeStruct((ROWS, heads * 128), BF),
        in_specs=[
            pl.BlockSpec((1, ROWS), lambda h: (0, 0)),
            vmem(),
            hbm(),
            pl.BlockSpec((1, 256), lambda h: (0, h)),
        ],
        out_specs=pl.BlockSpec((ROWS, 256), lambda h: (0, h)),
        scratch_shapes=[
            pltpu.VMEM((ROWS, ROWS), BF),
            pltpu.VMEM((heads // 2, ROWS, 256), BF),
            pltpu.SemaphoreType.DMA((heads // 2,)),
        ],
        compiler_params=params(12),
        cost_estimate=cost(1 << 30, 3 << 20),
        name="final",
    )(inv, y_all, gate, norm_gain.reshape(1, -1))


def solution(mesh):
    return jax.shard_map(
        body,
        mesh=mesh,
        in_specs=(
            P(("batch", "seq"), None),
            P("seq"),
            P("seq"),
            P(None, "mp"),
            P(None, "mp"),
            P(),
            P(None, "mp"),
            P(None, "mp"),
            P(),
            P("mp"),
            P("mp"),
            P("mp"),
            P("mp"),
        ),
        out_specs=P(("batch", "seq"), "mp"),
        check_vma=False,
    )
```

time: 155 us -> 123 us (0.79)
  waiting for transfers between devices: 52.1 us -> 42.1 us
  Pallas kernels: 51.1 us -> 42.1 us
  matrix products: 5.53 us -> 0 us
  local copies, waits for them, and re-layouts: 16.7 us -> 11.3 us
  starting transfers between devices: 28.9 us -> 25.7 us
    ppermute x3 -> x6, waiting for transfers between devices: 19.8 us -> 0.02 us  [the longest x1 0.01 us: body(): lax.ppermute(bc_a, 'mp', up)]
    all_to_all x1, waiting for transfers between devices: 0.01 us -> 9.55 us  [body(): x_all = lax.all_to_all(x_slots, 'seq', 0, 0, tiled=True)]
    pallas_call x4 -> x8, Pallas kernels: 43.6 us -> 35.5 us  [the longest x1 11.1 us: run_scan(): pl.pallas_call(scan_body, out_shape=jax.ShapeDtypeStruct((SEQ, QUAD, 256)...]
    dot_general x1 -> x0, matrix products: 5.53 us -> none  [body(): gate = jnp.dot(latent, w_gate, preferred_element_type=F32).astype(BF)]
    unnamed x48 -> x30, local copies, waits for them, and re-layouts: 16.6 us -> 11.2 us
    all_to_all x1, starting transfers between devices: 7.54 us -> 3.83 us  [body(): y_all = lax.all_to_all(y_slots, 'seq', 0, 0, tiled=True)]
    ppermute x3 -> x6, starting transfers between devices: 4.89 us -> 6.95 us  [the longest x1 2.73 us: body(): lax.ppermute(three_b, 'mp', down)]
    all_to_all x1, waiting for transfers between devices: 22.4 us -> 20.6 us  [body(): y_all = lax.all_to_all(y_slots, 'seq', 0, 0, tiled=True)]
  transfers between devices with their start and end apart: 11 -> 18, of which waited for: 5 -> 7; matrix products, arithmetic and copies ran while one was open for 4% -> 0% of each run, Pallas kernels for 9% -> 18%
where the time goes in v2:
time: 123 us; the launch traced here: 122 us
  Pallas kernels  42.1 us (34%)
  waiting for transfers between devices  42.1 us (34%)
  starting transfers between devices  25.7 us (21%)
  local copies, waits for them, and re-layouts  11.3 us (9%)
    all_to_all x1, waiting for transfers between devices, body(): y_all = lax.all_to_all(y_slots, 'seq', 0, 0, tiled=True)  20.6 us
    unnamed x30, local copies, waits for them, and re-layouts  11.2 us
    pallas_call x1, Pallas kernels, run_scan(): pl.pallas_call(scan_body, out_shape=jax.ShapeDtypeStruct((SEQ, QUAD, 256)...  11.1 us
    all_to_all x1, waiting for transfers between devices, body(): x_all = lax.all_to_all(x_slots, 'seq', 0, 0, tiled=True)  9.55 us
    all_to_all x1, starting transfers between devices, body(): lax.all_to_all(bc_slots, 'seq', 0, 0, axis_index_groups=lines, tiled=True)  9.03 us
    all_to_all x1, waiting for transfers between devices, body(): lax.all_to_all(bc_slots, 'seq', 0, 0, axis_index_groups=lines, tiled=True)  8.99 us
    pallas_call x1, Pallas kernels, body(): pl.pallas_call(value_body, grid=(4,), out_shape=jax.ShapeDtypeStruct((SEQ...  6.57 us
    pallas_call x2, Pallas kernels, run_place(): pl.pallas_call(kernel, out_shape=outs, in_specs=[smem()] * 2 + [vmem()] *...  5.61 us
  transfers between devices with their start and end apart: 18, of which 7 were waited for; matrix products, arithmetic and copies ran while one was open for 0% of the time, Pallas kernels for 18%

profile of v2, /device:TPU:1, one launch (start us, length us, event | category | flops | bytes accessed | tf_op | source)
XLA Modules:
  0.0 122.2 jit_solution(313700680234519391)
XLA Ops:
  0.6 4.8 %front.1 = bf16[8,144,256]{2,1,0:T(8,128)(2,1)} custom-call(s32[4]{0:T(128)} %pad_add_fusion.at_ref, s32[1,512]{1,0:T(1,128)} %bitcast.8, s32[1,512]{1,0:T(1,128)} %bitcast.12, bf16[512,2048]{1,0:T(8,128)(2,1)} %lat_ref.3, bf16[2048,256]{1,0:T(8,128)(2,1)} %wio_hbm.1, bf16[8,2048]{1,0:T(8,128)(2,1)} %bitcast.11), custom_call_target="tpu_custom_call" | custom-call | flops 1073741824 | bytes 4194304 | tf_op jit(solution)/shard_map/front/pallas_call | solution.py:511
  5.4 9.0 %all-to-all-start = ((bf16[8,144,256]{2,1,0:T(8,128)(2,1)}), bf16[8,144,256]{2,1,0:T(8,128)(2,1)S(1)}, u32[]{:S(2)}, u32[]{:S(2)}) async-start(bf16[8,144,256]{2,1,0:T(8,128)(2,1)} %front.1), calls=%async_computation | async-start | bytes 1179648 | tf_op jit(solution)/shard_map/all_to_all | solution.py:551
  14.4 2.2 %copy-done.1 = bf16[2048,1024]{1,0:T(8,128)(2,1)S(1)} copy-done((bf16[2048,1024]{1,0:T(8,128)(2,1)S(1)}, bf16[2048,1024]{1,0:T(8,128)(2,1)}, u32[]{:S(2)}) %copy-start.1) | copy-done | bytes 4194328
  16.6 1.6 %copy-done.3 = bf16[512,2048]{1,0:T(8,128)(2,1)S(1)} copy-done((bf16[512,2048]{1,0:T(8,128)(2,1)S(1)}, bf16[512,2048]{1,0:T(8,128)(2,1)}, u32[]{:S(2)}) %copy-start.3) | copy-done | bytes 2097176
  18.2 6.6 %value.1 = bf16[16,128,256]{2,1,0:T(8,128)(2,1)} custom-call(s32[1,512]{1,0:T(1,128)S(1)} %bitcast.9, bf16[512,2048]{1,0:T(8,128)(2,1)S(1)} %copy-done.3, bf16[2048,1024]{1,0:T(8,128)(2,1)S(1)} %copy-done.1), custom_call_target="tpu_custom_call" | custom-call | flops 3221225472 | bytes 8388608 | tf_op jit(solution)/shard_map/value/pallas_call | solution.py:553
  24.8 9.0 %all-to-all-done.own_ref = bf16[8,144,256]{2,1,0:T(8,128)(2,1)S(1)} async-done(((bf16[8,144,256]{2,1,0:T(8,128)(2,1)}), bf16[8,144,256]{2,1,0:T(8,128)(2,1)S(1)}, u32[]{:S(2)}, u32[]{:S(2)}) %all-to-all-start) | async-done | bytes 589856 | tf_op jit(solution)/shard_map/all_to_all | solution.py:551
  33.8 3.9 %all-to-all-start.1 = ((bf16[16,128,256]{2,1,0:T(8,128)(2,1)}), bf16[16,128,256]{2,1,0:T(8,128)(2,1)S(1)}, u32[]{:S(2)}, u32[]{:S(2)}) async-start(bf16[16,128,256]{2,1,0:T(8,128)(2,1)} %value.1), calls=%async_computation.1 | async-start | bytes 2097152 | tf_op jit(solution)/shard_map/all_to_all | solution.py:584
  38.0 1.7 %collective-permute-done.oth_ref = bf16[8,144,256]{2,1,0:T(8,128)(2,1)S(1)} collective-permute-done((bf16[8,144,256]{2,1,0:T(8,128)(2,1)S(1)}, bf16[8,144,256]{2,1,0:T(8,128)(2,1)S(1)}, u32[]{:S(2)}, u32[]{:S(2)}) %collective-permute-start) | collective-permute-done | bytes 589856 | tf_op jit(solution)/shard_map/ppermute | solution.py:583
  39.9 3.1 %bc.1 = (bf16[64,2048]{1,0:T(8,128)(2,1)S(1)}, bf16[64,2048]{1,0:T(8,128)(2,1)S(1)}, s32[16,512]{1,0:T(8,128)S(1)}) custom-call(s32[4]{0:T(128)S(1)} %copy-done, s32[512]{0:T(512)S(1)} %reshape.16.ab_ref, bf16[8,144,256]{2,1,0:T(8,128)(2,1)S(1)} %all-to-all-done.own_ref, bf16[8,144,256]{2,1,0:T(8,128)(2,1)S(1)} %collective-permute-done.oth_ref, ...), custom_call_target="tpu_custom_call" | custom-call | flops 1073741824 | bytes 2097152 | tf_op jit(solution)/shard_map/bc/pallas_call | solution.py:589
  42.9 1.3 %collective-permute-start.1 = (bf16[64,2048]{1,0:T(8,128)(2,1)S(1)}, bf16[64,2048]{1,0:T(8,128)(2,1)S(1)}, u32[]{:S(2)}, u32[]{:S(2)}) collective-permute-start(bf16[64,2048]{1,0:T(8,128)(2,1)S(1)} %get-tuple-element.35.refs_0_), channel_id=1, source_target_pairs={{0,4},{4,8},{8,12},{12,0},{1,5},{5,9},{9,13},{13,1},{2,6},{6,10},{... | collective-permute-start | bytes 786440 | tf_op jit(solution)/shard_map/ppermute | solution.py:601
  44.2 1.5 %collective-permute-start.2 = (bf16[64,2048]{1,0:T(8,128)(2,1)S(1)}, bf16[64,2048]{1,0:T(8,128)(2,1)S(1)}, u32[]{:S(2)}, u32[]{:S(2)}) collective-permute-start(bf16[64,2048]{1,0:T(8,128)(2,1)S(1)} %get-tuple-element.36.refs_1_), channel_id=1, source_target_pairs={{0,12},{4,0},{8,4},{12,8},{1,13},{5,1},{9,5},{13,9},{2,14},{6,2},{... | collective-permute-start | bytes 786440 | tf_op jit(solution)/shard_map/ppermute | solution.py:601
  45.7 1.3 %collective-permute-start.6 = (bf16[64,2048]{1,0:T(8,128)(2,1)S(1)}, bf16[64,2048]{1,0:T(8,128)(2,1)S(1)}, u32[]{:S(2)}, u32[]{:S(2)}) collective-permute-start(bf16[64,2048]{1,0:T(8,128)(2,1)S(1)} %get-tuple-element.35.refs_0_), channel_id=1, source_target_pairs={{0,12},{4,0},{8,4},{12,8},{1,13},{5,1},{9,5},{13,9},{2,14},{6,2},{... | collective-permute-start | bytes 786440 | tf_op jit(solution)/shard_map/ppermute | solution.py:602
  49.2 3.5 %time.1.table_ref = f32[128,512]{1,0:T(8,128)S(1)} custom-call(s32[4]{0:T(128)S(1)} %copy-done, s32[512]{0:T(512)S(1)} %reshape.16.ab_ref, f32[8]{0:T(128)S(1)} %copy-done.9, f32[8]{0:T(128)S(1)} %copy-done.10, f32[8]{0:T(128)S(1)} %copy-done.11, s32[16,512]{1,0:T(8,128)S(1)} %get-tuple-element.27.code_ref, bf16[8,144,256]{2,1,0:T(8,128)(2,1)S(1)} %all-to-all-done.own_ref, ...), custom_call_target="tpu_custom_call" | custom-call | flops 2147483648 | bytes 2097152 | tf_op jit(solution)/shard_map/time/pallas_call | solution.py:463
  53.4 2.7 %collective-permute-start.5 = (bf16[64,2048]{1,0:T(8,128)(2,1)S(1)}, bf16[64,2048]{1,0:T(8,128)(2,1)S(1)}, u32[]{:S(2)}, u32[]{:S(2)}) collective-permute-start(bf16[64,2048]{1,0:T(8,128)(2,1)S(1)} %collective-permute-done.2.refs_7_), channel_id=1, source_target_pairs={{0,12},{4,0},{8,4},{12,8},{1,13},{5,1},{9,5},{13,9},{2,14},{6,2},{... | collective-permute-start | bytes 786440 | tf_op jit(solution)/shard_map/ppermute | solution.py:605
  56.1 9.6 %all-to-all-done.1.x_ref = bf16[16,128,256]{2,1,0:T(8,128)(2,1)S(1)} async-done(((bf16[16,128,256]{2,1,0:T(8,128)(2,1)}), bf16[16,128,256]{2,1,0:T(8,128)(2,1)S(1)}, u32[]{:S(2)}, u32[]{:S(2)}) %all-to-all-start.1) | async-done | bytes 1048608 | tf_op jit(solution)/shard_map/all_to_all | solution.py:584
  66.6 2.8 %place.2 = (bf16[64,4096]{1,0:T(8,128)(2,1)S(1)}, f32[64,128]{1,0:T(8,128)S(1)}) custom-call(s32[4]{0:T(128)S(1)} %copy-done, s32[512]{0:T(512)S(1)} %reshape.16.ab_ref, f32[128,512]{1,0:T(8,128)S(1)} %copy-done.13, bf16[16,128,256]{2,1,0:T(8,128)(2,1)S(1)} %all-to-all-done.1.x_ref), custom_call_target="tpu_custom_call" | custom-call | flops 2147483648 | bytes 2097152 | tf_op jit(solution)/shard_map/place/pallas_call | solution.py:481
  72.4 2.8 %place.3.xact_b = bf16[64,4096]{1,0:T(8,128)(2,1)S(1)} custom-call(s32[4]{0:T(128)S(1)} %copy-done, s32[512]{0:T(512)S(1)} %reshape.16.ab_ref, f32[128,512]{1,0:T(8,128)S(1)} %copy-done.14, bf16[16,128,256]{2,1,0:T(8,128)(2,1)S(1)} %all-to-all-done.1.x_ref, f32[64,128]{1,0:T(8,128)S(1)} %get-tuple-element.34.last_ref), custom_call_target="tpu_custom_call" | custom-call | flops 2147483648 | bytes 2097152 | tf_op jit(solution)/shard_map/place/pallas_call | solution.py:481
  75.2 11.1 %scan.1 = bf16[16,128,256]{2,1,0:T(8,128)(2,1)} custom-call(s32[4]{0:T(128)S(1)} %copy-done, s32[512]{0:T(512)S(1)} %reshape.16.ab_ref, f32[128,512]{1,0:T(8,128)S(1)} %copy-done.14, bf16[64,4096]{1,0:T(8,128)(2,1)S(1)} %get-tuple-element.33.xact_a, bf16[64,4096]{1,0:T(8,128)(2,1)S(1)} %place.3.xact_b, bf16[64,2048]{1,0:T(8,128)(2,1)S(1)} %get-tuple-element.35.refs_0_, ...), custom_call_target="tpu_custom_call" | custom-call | flops 8589934592 | bytes 8388608 | tf_op jit(solution)/shard_map/scan/pallas_call | solution.py:494
  86.4 3.8 %all-to-all-start.2 = ((bf16[16,128,256]{2,1,0:T(8,128)(2,1)}), bf16[16,128,256]{2,1,0:T(8,128)(2,1)S(1)}, u32[]{:S(2)}, u32[]{:S(2)}) async-start(bf16[16,128,256]{2,1,0:T(8,128)(2,1)} %scan.1), calls=%async_computation.2 | async-start | bytes 2097152 | tf_op jit(solution)/shard_map/all_to_all | solution.py:614
  90.2 2.2 %copy-done.2 = bf16[2048,1024]{1,0:T(8,128)(2,1)S(1)} copy-done((bf16[2048,1024]{1,0:T(8,128)(2,1)S(1)}, bf16[2048,1024]{1,0:T(8,128)(2,1)}, u32[]{:S(2)}) %copy-start.2) | copy-done | bytes 4194328
  92.4 1.6 %copy-done.4 = bf16[512,2048]{1,0:T(8,128)(2,1)S(1)} copy-done((bf16[512,2048]{1,0:T(8,128)(2,1)S(1)}, bf16[512,2048]{1,0:T(8,128)(2,1)}, u32[]{:S(2)}) %copy-start.4) | copy-done | bytes 2097176
  94.0 3.6 %gate.1.gate_hbm = bf16[512,1024]{1,0:T(8,128)(2,1)S(1)} custom-call(bf16[512,2048]{1,0:T(8,128)(2,1)S(1)} %copy-done.4, bf16[2048,1024]{1,0:T(8,128)(2,1)S(1)} %copy-done.2), custom_call_target="tpu_custom_call" | custom-call | flops 2147483648 | bytes 8388608 | tf_op jit(solution)/shard_map/gate/pallas_call | solution.py:568
  97.6 20.6 %all-to-all-done.2.y_ref = bf16[16,128,256]{2,1,0:T(8,128)(2,1)S(1)} async-done(((bf16[16,128,256]{2,1,0:T(8,128)(2,1)}), bf16[16,128,256]{2,1,0:T(8,128)(2,1)S(1)}, u32[]{:S(2)}, u32[]{:S(2)}) %all-to-all-start.2) | async-done | bytes 1048608 | tf_op jit(solution)/shard_map/all_to_all | solution.py:614
  118.2 3.8 %final.1 = bf16[512,1024]{1,0:T(8,128)(2,1)} custom-call(s32[1,512]{1,0:T(1,128)S(1)} %bitcast.10, bf16[16,128,256]{2,1,0:T(8,128)(2,1)S(1)} %all-to-all-done.2.y_ref, bf16[512,1024]{1,0:T(8,128)(2,1)S(1)} %gate.1.gate_hbm, f32[1,1024]{1,0:T(1,128)S(1)} %bitcast.7), custom_call_target="tpu_custom_call" | custom-call | flops 1073741824 | bytes 3145728 | tf_op jit(solution)/shard_map/final/pallas_call | solution.py:617
  (56 shorter events, 7.9 us)
Async XLA Ops:
  0.0 14.4 %copy-start.8 = (s32[512]{0:T(512)S(1)}, s32[512]{0:T(512)}, u32[]{:S(2)}) copy-start(s32[512]{0:T(512)} %param.15) | copy-start | bytes 6148
  5.4 28.4 %all-to-all-start = ((bf16[8,144,256]{2,1,0:T(8,128)(2,1)}), bf16[8,144,256]{2,1,0:T(8,128)(2,1)S(1)}, u32[]{:S(2)}, u32[]{:S(2)}) async-start(bf16[8,144,256]{2,1,0:T(8,128)(2,1)} %front.1), calls=%async_computation | async-start | bytes 1179648 | tf_op jit(solution)/shard_map/all_to_all | solution.py:551
  18.2 21.6 %copy-start = (s32[4]{0:T(128)S(1)}, s32[4]{0:T(128)}, u32[]{:S(2)}) copy-start(s32[4]{0:T(128)} %pad_add_fusion.at_ref) | copy-start | bytes 52
  18.2 21.6 %copy-start.6 = (f32[4,256]{1,0:T(4,128)S(1)}, f32[4,256]{1,0:T(4,128)}, u32[]{:S(2)}) copy-start(f32[4,256]{1,0:T(4,128)} %conv_ref.2) | copy-start | bytes 12292
  24.8 22.4 %copy-start.9 = (f32[8]{0:T(128)S(1)}, f32[8]{0:T(128)}, u32[]{:S(2)}) copy-start(f32[8]{0:T(128)} %bias_ref.1) | copy-start | bytes 100
  33.8 31.9 %all-to-all-start.1 = ((bf16[16,128,256]{2,1,0:T(8,128)(2,1)}), bf16[16,128,256]{2,1,0:T(8,128)(2,1)S(1)}, u32[]{:S(2)}, u32[]{:S(2)}) async-start(bf16[16,128,256]{2,1,0:T(8,128)(2,1)} %value.1), calls=%async_computation.1 | async-start | bytes 2097152 | tf_op jit(solution)/shard_map/all_to_all | solution.py:584
  37.7 2.0 %collective-permute-start = (bf16[8,144,256]{2,1,0:T(8,128)(2,1)S(1)}, bf16[8,144,256]{2,1,0:T(8,128)(2,1)S(1)}, u32[]{:S(2)}, u32[]{:S(2)}) collective-permute-start(bf16[8,144,256]{2,1,0:T(8,128)(2,1)S(1)} %all-to-all-done.own_ref), channel_id=1, source_target_pairs={{0,16},{16,0},{32,48},{48,32},{64,80},{80,64},{96,112},{112,96},{1... | collective-permute-start | bytes 1769480 | tf_op jit(solution)/shard_map/ppermute | solution.py:583
  42.9 10.5 %collective-permute-start.1 = (bf16[64,2048]{1,0:T(8,128)(2,1)S(1)}, bf16[64,2048]{1,0:T(8,128)(2,1)S(1)}, u32[]{:S(2)}, u32[]{:S(2)}) collective-permute-start(bf16[64,2048]{1,0:T(8,128)(2,1)S(1)} %get-tuple-element.35.refs_0_), channel_id=1, source_target_pairs={{0,4},{4,8},{8,12},{12,0},{1,5},{5,9},{9,13},{13,1},{2,6},{6,10},{... | collective-permute-start | bytes 786440 | tf_op jit(solution)/shard_map/ppermute | solution.py:601
  44.2 9.2 %collective-permute-start.2 = (bf16[64,2048]{1,0:T(8,128)(2,1)S(1)}, bf16[64,2048]{1,0:T(8,128)(2,1)S(1)}, u32[]{:S(2)}, u32[]{:S(2)}) collective-permute-start(bf16[64,2048]{1,0:T(8,128)(2,1)S(1)} %get-tuple-element.36.refs_1_), channel_id=1, source_target_pairs={{0,12},{4,0},{8,4},{12,8},{1,13},{5,1},{9,5},{13,9},{2,14},{6,2},{... | collective-permute-start | bytes 786440 | tf_op jit(solution)/shard_map/ppermute | solution.py:601
  45.7 23.8 %collective-permute-start.6 = (bf16[64,2048]{1,0:T(8,128)(2,1)S(1)}, bf16[64,2048]{1,0:T(8,128)(2,1)S(1)}, u32[]{:S(2)}, u32[]{:S(2)}) collective-permute-start(bf16[64,2048]{1,0:T(8,128)(2,1)S(1)} %get-tuple-element.35.refs_0_), channel_id=1, source_target_pairs={{0,12},{4,0},{8,4},{12,8},{1,13},{5,1},{9,5},{13,9},{2,14},{6,2},{... | collective-permute-start | bytes 786440 | tf_op jit(solution)/shard_map/ppermute | solution.py:602
  46.9 22.5 %collective-permute-start.3 = (bf16[64,2048]{1,0:T(8,128)(2,1)S(1)}, bf16[64,2048]{1,0:T(8,128)(2,1)}, u32[]{:S(2)}, u32[]{:S(2)}) collective-permute-start(bf16[64,2048]{1,0:T(8,128)(2,1)S(1)} %get-tuple-element.36.refs_1_), channel_id=1, source_target_pairs={{0,4},{4,8},{8,12},{12,0},{1,5},{5,9},{9,13},{13,1},{2,6},{6,10},{... | collective-permute-start | bytes 786440 | tf_op jit(solution)/shard_map/ppermute | solution.py:602
  53.4 16.1 %collective-permute-start.4 = (bf16[64,2048]{1,0:T(8,128)(2,1)S(1)}, bf16[64,2048]{1,0:T(8,128)(2,1)S(1)}, u32[]{:S(2)}, u32[]{:S(2)}) collective-permute-start(bf16[64,2048]{1,0:T(8,128)(2,1)S(1)} %collective-permute-done.1.refs_2_), channel_id=1, source_target_pairs={{0,4},{4,8},{8,12},{12,0},{1,5},{5,9},{9,13},{13,1},{2,6},{6,10},{... | collective-permute-start | bytes 786440 | tf_op jit(solution)/shard_map/ppermute | solution.py:605
  53.4 16.1 %collective-permute-start.5 = (bf16[64,2048]{1,0:T(8,128)(2,1)S(1)}, bf16[64,2048]{1,0:T(8,128)(2,1)S(1)}, u32[]{:S(2)}, u32[]{:S(2)}) collective-permute-start(bf16[64,2048]{1,0:T(8,128)(2,1)S(1)} %collective-permute-done.2.refs_7_), channel_id=1, source_target_pairs={{0,12},{4,0},{8,4},{12,8},{1,13},{5,1},{9,5},{13,9},{2,14},{6,2},{... | collective-permute-start | bytes 786440 | tf_op jit(solution)/shard_map/ppermute | solution.py:605
  66.6 5.7 %copy-start.14 = (f32[128,512]{1,0:T(8,128)S(1)}, f32[128,512]{1,0:T(8,128)}, u32[]{:S(2)}) copy-start(f32[128,512]{1,0:T(8,128)} %copy-done.12) | copy-start | bytes 786436
  69.5 1.6 %collective-permute-start.7 = (bf16[64,2048]{1,0:T(8,128)(2,1)S(1)}, bf16[64,2048]{1,0:T(8,128)(2,1)S(1)}, u32[]{:S(2)}, u32[]{:S(2)}) collective-permute-start(bf16[64,2048]{1,0:T(8,128)(2,1)S(1)} %get-tuple-element.35.refs_0_), channel_id=1, source_target_pairs={{0,16},{16,0},{32,48},{48,32},{64,80},{80,64},{96,112},{112,96},{1... | collective-permute-start | bytes 786440 | tf_op jit(solution)/shard_map/ppermute | solution.py:611
  69.6 1.9 %collective-permute-start.8 = (bf16[64,2048]{1,0:T(8,128)(2,1)S(1)}, bf16[64,2048]{1,0:T(8,128)(2,1)S(1)}, u32[]{:S(2)}, u32[]{:S(2)}) collective-permute-start(bf16[64,2048]{1,0:T(8,128)(2,1)S(1)} %get-tuple-element.36.refs_1_), channel_id=1, source_target_pairs={{0,16},{16,0},{32,48},{48,32},{64,80},{80,64},{96,112},{112,96},{1... | collective-permute-start | bytes 786440 | tf_op jit(solution)/shard_map/ppermute | solution.py:611
  70.1 2.1 %collective-permute-start.9 = (bf16[64,2048]{1,0:T(8,128)(2,1)S(1)}, bf16[64,2048]{1,0:T(8,128)(2,1)S(1)}, u32[]{:S(2)}, u32[]{:S(2)}) collective-permute-start(bf16[64,2048]{1,0:T(8,128)(2,1)S(1)} %collective-permute-done.1.refs_2_), channel_id=1, source_target_pairs={{0,16},{16,0},{32,48},{48,32},{64,80},{80,64},{96,112},{112,96},{1... | collective-permute-start | bytes 786440 | tf_op jit(solution)/shard_map/ppermute | solution.py:611
  70.2 5.0 %collective-permute-start.10 = (bf16[64,2048]{1,0:T(8,128)(2,1)}, bf16[64,2048]{1,0:T(8,128)(2,1)S(1)}, u32[]{:S(2)}, u32[]{:S(2)}) collective-permute-start(bf16[64,2048]{1,0:T(8,128)(2,1)} %collective-permute-done.3.refs_3_), channel_id=1, source_target_pairs={{0,16},{16,0},{32,48},{48,32},{64,80},{80,64},{96,112},{112,96},{1... | collective-permute-start | bytes 786440 | tf_op jit(solution)/shard_map/ppermute | solution.py:611
  70.6 4.6 %collective-permute-start.11 = (bf16[64,2048]{1,0:T(8,128)(2,1)S(1)}, bf16[64,2048]{1,0:T(8,128)(2,1)S(1)}, u32[]{:S(2)}, u32[]{:S(2)}) collective-permute-start(bf16[64,2048]{1,0:T(8,128)(2,1)S(1)} %collective-permute-done.4.refs_4_), channel_id=1, source_target_pairs={{0,16},{16,0},{32,48},{48,32},{64,80},{80,64},{96,112},{112,96},{1... | collective-permute-start | bytes 786440 | tf_op jit(solution)/shard_map/ppermute | solution.py:611
  71.1 4.1 %collective-permute-start.12 = (bf16[64,2048]{1,0:T(8,128)(2,1)S(1)}, bf16[64,2048]{1,0:T(8,128)(2,1)S(1)}, u32[]{:S(2)}, u32[]{:S(2)}) collective-permute-start(bf16[64,2048]{1,0:T(8,128)(2,1)S(1)} %collective-permute-done.5.refs_5_), channel_id=1, source_target_pairs={{0,16},{16,0},{32,48},{48,32},{64,80},{80,64},{96,112},{112,96},{1... | collective-permute-start | bytes 786440 | tf_op jit(solution)/shard_map/ppermute | solution.py:611
  71.5 3.7 %collective-permute-start.13 = (bf16[64,2048]{1,0:T(8,128)(2,1)S(1)}, bf16[64,2048]{1,0:T(8,128)(2,1)S(1)}, u32[]{:S(2)}, u32[]{:S(2)}) collective-permute-start(bf16[64,2048]{1,0:T(8,128)(2,1)S(1)} %collective-permute-done.6.refs_6_), channel_id=1, source_target_pairs={{0,16},{16,0},{32,48},{48,32},{64,80},{80,64},{96,112},{112,96},{1... | collective-permute-start | bytes 786440 | tf_op jit(solution)/shard_map/ppermute | solution.py:611
  72.2 3.0 %collective-permute-start.14 = (bf16[64,2048]{1,0:T(8,128)(2,1)S(1)}, bf16[64,2048]{1,0:T(8,128)(2,1)S(1)}, u32[]{:S(2)}, u32[]{:S(2)}) collective-permute-start(bf16[64,2048]{1,0:T(8,128)(2,1)S(1)} %collective-permute-done.2.refs_7_), channel_id=1, source_target_pairs={{0,16},{16,0},{32,48},{48,32},{64,80},{80,64},{96,112},{112,96},{1... | collective-permute-start | bytes 786440 | tf_op jit(solution)/shard_map/ppermute | solution.py:611
  86.4 31.8 %all-to-all-start.2 = ((bf16[16,128,256]{2,1,0:T(8,128)(2,1)}), bf16[16,128,256]{2,1,0:T(8,128)(2,1)S(1)}, u32[]{:S(2)}, u32[]{:S(2)}) async-start(bf16[16,128,256]{2,1,0:T(8,128)(2,1)} %scan.1), calls=%async_computation.2 | async-start | bytes 2097152 | tf_op jit(solution)/shard_map/all_to_all | solution.py:614
  94.0 24.2 %copy-start.7 = (f32[1024]{0:T(1024)S(1)}, f32[1024]{0:T(1024)}, u32[]{:S(2)}) copy-start(f32[1024]{0:T(1024)} %param.25) | copy-start | bytes 12292
  (9 other events, 11.2 us)

commit v3 on v2

--- a/solution.py
+++ b/solution.py
@@ -64,7 +64,6 @@
 
 
 def front_body(
-    at_ref,
     inv_hbm,
     ord_hbm,
     lat_hbm,
@@ -146,7 +145,7 @@
     pieces = jnp.concatenate(pieces + [rest], axis=0).astype(BF)
     dealt = dot(pieces, deal, ((1,), (1,)))
     steps = [dealt[8 * k : 8 * k + 8] for k in range(3)]
-    m = at_ref[0]
+    m = lax.axis_index("mp")
     half = jnp.where(m >= 2, io[:, 128:], io[:, :128])
     turned = pltpu.roll(half, 64, 1)
     odd = m % 2 == 1
@@ -341,7 +340,7 @@
 
 def scan_body(at_ref, ab_ref, table_ref, xact_a, xact_b, *refs):
     owns, oths = refs[:8], refs[8:16]
-    out_ref, bc_ref, acc_ref, sem_ref = refs[16:]
+    out_ref, bc_ref, sem_ref = refs[16:]
     m, c = at_ref[0], at_ref[1]
     copies = []
     for index in range(8):
@@ -354,12 +353,9 @@
             )
     for copy in copies:
         copy.start()
-    acc_ref[...] = jnp.zeros_like(acc_ref)
+    out_ref[...] = jnp.zeros_like(out_ref)
     skip = table_ref[48:49, :BLOCK]
     causal = iota((BLOCK, BLOCK), 0) <= iota((BLOCK, BLOCK), 1)
-    for copy in copies:
-        copy.wait()
-
     def scan(half, e, state):
         d = 8 * half + e
         cols = pl.ds(pl.multiple_of(ROWS * e, ROWS), ROWS)
@@ -390,13 +386,17 @@
         back = dot(spread, apart, ((1,), (1,)))
         for s in range(SEQ):
             at = pl.ds(tile_at(ab_ref, c, s, d), WIN)
-            acc_ref[s, at, :] = acc_ref[s, at, :] + back[WIN * s : WIN * s + WIN]
+            out_ref[s, at, :] = out_ref[s, at, :] + back[WIN * s : WIN * s + WIN].astype(BF)
         return state
 
     state = jnp.zeros((CH, BC), F32)
     for half in range(2):
-        state = lax.fori_loop(0, 8, lambda e, state, half=half: scan(half, e, state), state, unroll=4)
-    out_ref[...] = acc_ref[...].astype(BF)
+        for index in range(8):
+            rows = pl.ds(pl.multiple_of(CH * ((m - index // 2 + 4) % 4), CH), CH)
+            cols = pl.ds(4 * ROWS * (index % 2), 4 * ROWS)
+            sem = sem_ref.at[index, c if half == 0 else 1 - c]
+            pltpu.make_async_copy(owns[index], bc_ref.at[half, rows, cols], sem).wait()
+        state = lax.fori_loop(0, 8, lambda e, state, half=half: scan(half, e, state), state, unroll=8)
 
 
 def final_body(inv_ref, y_ref, gate_hbm, gain_ref, out_ref, pick_ref, gate_ref, sem_ref):
@@ -498,7 +498,6 @@
         out_specs=vmem(),
         scratch_shapes=[
             pltpu.VMEM((2, 256, 8 * ROWS), BF),
-            pltpu.VMEM((SEQ, QUAD, 256), F32),
             pltpu.SemaphoreType.DMA((8, 2)),
         ],
         compiler_params=params(24),
@@ -511,13 +510,13 @@
     return pl.pallas_call(
         front_body,
         out_shape=jax.ShapeDtypeStruct((8, SLOT, 256), BF),
-        in_specs=[smem(), hbm(), hbm(), hbm(), hbm(), vmem()],
+        in_specs=[hbm(), hbm(), hbm(), hbm(), vmem()],
         out_specs=vmem(),
         scratch_shapes=[
             pltpu.VMEM((1, ROWS), I32),
             pltpu.VMEM((1, ROWS), I32),
+            pltpu.VMEM(args[2].shape, BF),
             pltpu.VMEM(args[3].shape, BF),
-            pltpu.VMEM(args[4].shape, BF),
             pltpu.SemaphoreType.DMA((10,)),
         ],
         compiler_params=params(60),
@@ -547,7 +546,7 @@
     pairs = [(i, i ^ 1) for i in range(SEQ)]
     lines = [[2 * i + core for i in range(SEQ // 2)] for core in range(2)]
 
-    bc_slots = run_front(at, inv, order.reshape(1, ROWS), latent, w_input_output, w_step.T)
+    bc_slots = run_front(inv, order.reshape(1, ROWS), latent, w_input_output, w_step.T)
     own = lax.all_to_all(bc_slots, "seq", 0, 0, axis_index_groups=lines, tiled=True)
 
     x_slots = pl.pallas_call(

time: 123 us -> 121 us (0.984)
  Pallas kernels: 42.1 us -> 40.5 us
    pallas_call x1, Pallas kernels: 11.1 us -> 9.55 us  [run_scan(): pl.pallas_call(scan_body, out_shape=jax.ShapeDtypeStruct((SEQ, QUAD, 256)...]
    unnamed x30 -> x28, local copies, waits for them, and re-layouts: 11.2 us -> 11.2 us
where the time goes in v3:
time: 121 us
  waiting for transfers between devices  42 us (35%)
  Pallas kernels  40.5 us (33%)
  starting transfers between devices  26.4 us (22%)
  local copies, waits for them, and re-layouts  11.3 us (9%)
    all_to_all x1, waiting for transfers between devices, body(): y_all = lax.all_to_all(y_slots, 'seq', 0, 0, tiled=True)  20.6 us
    unnamed x28, local copies, waits for them, and re-layouts  11.2 us
    all_to_all x1, waiting for transfers between devices, body(): x_all = lax.all_to_all(x_slots, 'seq', 0, 0, tiled=True)  9.56 us
    pallas_call x1, Pallas kernels, run_scan(): pl.pallas_call(scan_body, out_shape=jax.ShapeDtypeStruct((SEQ, QUAD, 256)...  9.55 us
    all_to_all x1, starting transfers between devices, body(): lax.all_to_all(bc_slots, 'seq', 0, 0, axis_index_groups=lines, tiled=True)  9.03 us
    all_to_all x1, waiting for transfers between devices, body(): lax.all_to_all(bc_slots, 'seq', 0, 0, axis_index_groups=lines, tiled=True)  9 us
    pallas_call x1, Pallas kernels, body(): pl.pallas_call(value_body, grid=(4,), out_shape=jax.ShapeDtypeStruct((SEQ...  6.57 us
    pallas_call x2, Pallas kernels, run_place(): pl.pallas_call(kernel, out_shape=outs, in_specs=[smem()] * 2 + [vmem()] *...  5.6 us
  transfers between devices with their start and end apart: 18, of which 7 were waited for; matrix products, arithmetic and copies ran while one was open for 0% of the time, Pallas kernels for 18%

profile of v3, /device:TPU:1, one launch (start us, length us, event | category | flops | bytes accessed | tf_op | source)
XLA Modules:
  0.0 120.7 jit_solution(10836128905220201967)
XLA Ops:
  0.0 4.8 %front.1 = bf16[8,144,256]{2,1,0:T(8,128)(2,1)} custom-call(s32[1,512]{1,0:T(1,128)} %bitcast.8, s32[1,512]{1,0:T(1,128)} %bitcast.12, bf16[512,2048]{1,0:T(8,128)(2,1)} %lat_ref.3, bf16[2048,256]{1,0:T(8,128)(2,1)} %wio_hbm.1, bf16[8,2048]{1,0:T(8,128)(2,1)} %bitcast.11), custom_call_target="tpu_custom_call" | custom-call | flops 1073741824 | bytes 4194304 | tf_op jit(solution)/shard_map/front/pallas_call | solution.py:510
  4.8 9.0 %all-to-all-start = ((bf16[8,144,256]{2,1,0:T(8,128)(2,1)}), bf16[8,144,256]{2,1,0:T(8,128)(2,1)S(1)}, u32[]{:S(2)}, u32[]{:S(2)}) async-start(bf16[8,144,256]{2,1,0:T(8,128)(2,1)} %front.1), calls=%async_computation | async-start | bytes 1179648 | tf_op jit(solution)/shard_map/all_to_all | solution.py:550
  13.8 2.2 %copy-done = bf16[2048,1024]{1,0:T(8,128)(2,1)S(1)} copy-done((bf16[2048,1024]{1,0:T(8,128)(2,1)S(1)}, bf16[2048,1024]{1,0:T(8,128)(2,1)}, u32[]{:S(2)}) %copy-start) | copy-done | bytes 4194328
  16.0 1.6 %copy-done.2 = bf16[512,2048]{1,0:T(8,128)(2,1)S(1)} copy-done((bf16[512,2048]{1,0:T(8,128)(2,1)S(1)}, bf16[512,2048]{1,0:T(8,128)(2,1)}, u32[]{:S(2)}) %copy-start.2) | copy-done | bytes 2097176
  17.6 6.6 %value.1 = bf16[16,128,256]{2,1,0:T(8,128)(2,1)} custom-call(s32[1,512]{1,0:T(1,128)S(1)} %bitcast.9, bf16[512,2048]{1,0:T(8,128)(2,1)S(1)} %copy-done.2, bf16[2048,1024]{1,0:T(8,128)(2,1)S(1)} %copy-done), custom_call_target="tpu_custom_call" | custom-call | flops 3221225472 | bytes 8388608 | tf_op jit(solution)/shard_map/value/pallas_call | solution.py:552
  24.2 9.0 %all-to-all-done.own_ref = bf16[8,144,256]{2,1,0:T(8,128)(2,1)S(1)} async-done(((bf16[8,144,256]{2,1,0:T(8,128)(2,1)}), bf16[8,144,256]{2,1,0:T(8,128)(2,1)S(1)}, u32[]{:S(2)}, u32[]{:S(2)}) %all-to-all-start) | async-done | bytes 589856 | tf_op jit(solution)/shard_map/all_to_all | solution.py:550
  33.2 3.9 %all-to-all-start.1 = ((bf16[16,128,256]{2,1,0:T(8,128)(2,1)}), bf16[16,128,256]{2,1,0:T(8,128)(2,1)S(1)}, u32[]{:S(2)}, u32[]{:S(2)}) async-start(bf16[16,128,256]{2,1,0:T(8,128)(2,1)} %value.1), calls=%async_computation.1 | async-start | bytes 2097152 | tf_op jit(solution)/shard_map/all_to_all | solution.py:583
  37.5 1.6 %collective-permute-done.oth_ref = bf16[8,144,256]{2,1,0:T(8,128)(2,1)S(1)} collective-permute-done((bf16[8,144,256]{2,1,0:T(8,128)(2,1)S(1)}, bf16[8,144,256]{2,1,0:T(8,128)(2,1)S(1)}, u32[]{:S(2)}, u32[]{:S(2)}) %collective-permute-start) | collective-permute-done | bytes 589856 | tf_op jit(solution)/shard_map/ppermute | solution.py:582
  39.2 3.1 %bc.1 = (bf16[64,2048]{1,0:T(8,128)(2,1)S(1)}, bf16[64,2048]{1,0:T(8,128)(2,1)S(1)}, s32[16,512]{1,0:T(8,128)S(1)}) custom-call(s32[4]{0:T(128)S(1)} %pad_add_fusion.at_ref, s32[512]{0:T(512)S(1)} %reshape.16.ab_ref, bf16[8,144,256]{2,1,0:T(8,128)(2,1)S(1)} %all-to-all-done.own_ref, bf16[8,144,256]{2,1,0:T(8,128)(2,1)S(1)} %collective-permute-done.oth_ref, ...), custom_call_target="tpu_custom_call" | custom-call | flops 1073741824 | bytes 2097152 | tf_op jit(solution)/shard_map/bc/pallas_call | solution.py:588
  42.3 1.3 %collective-permute-start.1 = (bf16[64,2048]{1,0:T(8,128)(2,1)S(1)}, bf16[64,2048]{1,0:T(8,128)(2,1)S(1)}, u32[]{:S(2)}, u32[]{:S(2)}) collective-permute-start(bf16[64,2048]{1,0:T(8,128)(2,1)S(1)} %get-tuple-element.35.refs_0_), channel_id=1, source_target_pairs={{0,4},{4,8},{8,12},{12,0},{1,5},{5,9},{9,13},{13,1},{2,6},{6,10},{... | collective-permute-start | bytes 786440 | tf_op jit(solution)/shard_map/ppermute | solution.py:600
  43.6 1.5 %collective-permute-start.2 = (bf16[64,2048]{1,0:T(8,128)(2,1)S(1)}, bf16[64,2048]{1,0:T(8,128)(2,1)S(1)}, u32[]{:S(2)}, u32[]{:S(2)}) collective-permute-start(bf16[64,2048]{1,0:T(8,128)(2,1)S(1)} %get-tuple-element.36.refs_1_), channel_id=1, source_target_pairs={{0,12},{4,0},{8,4},{12,8},{1,13},{5,1},{9,5},{13,9},{2,14},{6,2},{... | collective-permute-start | bytes 786440 | tf_op jit(solution)/shard_map/ppermute | solution.py:600
  45.1 1.3 %collective-permute-start.6 = (bf16[64,2048]{1,0:T(8,128)(2,1)S(1)}, bf16[64,2048]{1,0:T(8,128)(2,1)S(1)}, u32[]{:S(2)}, u32[]{:S(2)}) collective-permute-start(bf16[64,2048]{1,0:T(8,128)(2,1)S(1)} %get-tuple-element.35.refs_0_), channel_id=1, source_target_pairs={{0,12},{4,0},{8,4},{12,8},{1,13},{5,1},{9,5},{13,9},{2,14},{6,2},{... | collective-permute-start | bytes 786440 | tf_op jit(solution)/shard_map/ppermute | solution.py:601
  48.6 3.5 %time.1.table_ref = f32[128,512]{1,0:T(8,128)S(1)} custom-call(s32[4]{0:T(128)S(1)} %pad_add_fusion.at_ref, s32[512]{0:T(512)S(1)} %reshape.16.ab_ref, f32[8]{0:T(128)S(1)} %copy-done.8, f32[8]{0:T(128)S(1)} %copy-done.9, f32[8]{0:T(128)S(1)} %copy-done.10, s32[16,512]{1,0:T(8,128)S(1)} %get-tuple-element.27.code_ref, ...), custom_call_target="tpu_custom_call" | custom-call | flops 2147483648 | bytes 2097152 | tf_op jit(solution)/shard_map/time/pallas_call | solution.py:463
  52.8 2.7 %collective-permute-start.5 = (bf16[64,2048]{1,0:T(8,128)(2,1)S(1)}, bf16[64,2048]{1,0:T(8,128)(2,1)S(1)}, u32[]{:S(2)}, u32[]{:S(2)}) collective-permute-start(bf16[64,2048]{1,0:T(8,128)(2,1)S(1)} %collective-permute-done.2.refs_7_), channel_id=1, source_target_pairs={{0,12},{4,0},{8,4},{12,8},{1,13},{5,1},{9,5},{13,9},{2,14},{6,2},{... | collective-permute-start | bytes 786440 | tf_op jit(solution)/shard_map/ppermute | solution.py:604
  55.5 9.6 %all-to-all-done.1.x_ref = bf16[16,128,256]{2,1,0:T(8,128)(2,1)S(1)} async-done(((bf16[16,128,256]{2,1,0:T(8,128)(2,1)}), bf16[16,128,256]{2,1,0:T(8,128)(2,1)S(1)}, u32[]{:S(2)}, u32[]{:S(2)}) %all-to-all-start.1) | async-done | bytes 1048608 | tf_op jit(solution)/shard_map/all_to_all | solution.py:583
  66.0 2.8 %place.2 = (bf16[64,4096]{1,0:T(8,128)(2,1)S(1)}, f32[64,128]{1,0:T(8,128)S(1)}) custom-call(s32[4]{0:T(128)S(1)} %pad_add_fusion.at_ref, s32[512]{0:T(512)S(1)} %reshape.16.ab_ref, f32[128,512]{1,0:T(8,128)S(1)} %copy-done.12, bf16[16,128,256]{2,1,0:T(8,128)(2,1)S(1)} %all-to-all-done.1.x_ref), custom_call_target="tpu_custom_call" | custom-call | flops 2147483648 | bytes 2097152 | tf_op jit(solution)/shard_map/place/pallas_call | solution.py:481
  71.8 2.8 %place.3.xact_b = bf16[64,4096]{1,0:T(8,128)(2,1)S(1)} custom-call(s32[4]{0:T(128)S(1)} %pad_add_fusion.at_ref, s32[512]{0:T(512)S(1)} %reshape.16.ab_ref, f32[128,512]{1,0:T(8,128)S(1)} %copy-done.13, bf16[16,128,256]{2,1,0:T(8,128)(2,1)S(1)} %all-to-all-done.1.x_ref, f32[64,128]{1,0:T(8,128)S(1)} %get-tuple-element.34.last_ref), custom_call_target="tpu_custom_call" | custom-call | flops 2147483648 | bytes 2097152 | tf_op jit(solution)/shard_map/place/pallas_call | solution.py:481
  74.6 9.5 %scan.1 = bf16[16,128,256]{2,1,0:T(8,128)(2,1)} custom-call(s32[4]{0:T(128)S(1)} %pad_add_fusion.at_ref, s32[512]{0:T(512)S(1)} %reshape.16.ab_ref, f32[128,512]{1,0:T(8,128)S(1)} %copy-done.13, bf16[64,4096]{1,0:T(8,128)(2,1)S(1)} %get-tuple-element.33.xact_a, bf16[64,4096]{1,0:T(8,128)(2,1)S(1)} %place.3.xact_b, ...), custom_call_target="tpu_custom_call" | custom-call | flops 8589934592 | bytes 8388608 | tf_op jit(solution)/shard_map/scan/pallas_call | solution.py:494
  84.2 4.5 %all-to-all-start.2 = ((bf16[16,128,256]{2,1,0:T(8,128)(2,1)}), bf16[16,128,256]{2,1,0:T(8,128)(2,1)S(1)}, u32[]{:S(2)}, u32[]{:S(2)}) async-start(bf16[16,128,256]{2,1,0:T(8,128)(2,1)} %scan.1), calls=%async_computation.2 | async-start | bytes 2097152 | tf_op jit(solution)/shard_map/all_to_all | solution.py:613
  88.7 2.2 %copy-done.1 = bf16[2048,1024]{1,0:T(8,128)(2,1)S(1)} copy-done((bf16[2048,1024]{1,0:T(8,128)(2,1)S(1)}, bf16[2048,1024]{1,0:T(8,128)(2,1)}, u32[]{:S(2)}) %copy-start.1) | copy-done | bytes 4194328
  90.9 1.6 %copy-done.3 = bf16[512,2048]{1,0:T(8,128)(2,1)S(1)} copy-done((bf16[512,2048]{1,0:T(8,128)(2,1)S(1)}, bf16[512,2048]{1,0:T(8,128)(2,1)}, u32[]{:S(2)}) %copy-start.3) | copy-done | bytes 2097176
  92.5 3.6 %gate.1.gate_hbm = bf16[512,1024]{1,0:T(8,128)(2,1)S(1)} custom-call(bf16[512,2048]{1,0:T(8,128)(2,1)S(1)} %copy-done.3, bf16[2048,1024]{1,0:T(8,128)(2,1)S(1)} %copy-done.1), custom_call_target="tpu_custom_call" | custom-call | flops 2147483648 | bytes 8388608 | tf_op jit(solution)/shard_map/gate/pallas_call | solution.py:567
  96.1 20.6 %all-to-all-done.2.y_ref = bf16[16,128,256]{2,1,0:T(8,128)(2,1)S(1)} async-done(((bf16[16,128,256]{2,1,0:T(8,128)(2,1)}), bf16[16,128,256]{2,1,0:T(8,128)(2,1)S(1)}, u32[]{:S(2)}, u32[]{:S(2)}) %all-to-all-start.2) | async-done | bytes 1048608 | tf_op jit(solution)/shard_map/all_to_all | solution.py:613
  116.7 3.8 %final.1 = bf16[512,1024]{1,0:T(8,128)(2,1)} custom-call(s32[1,512]{1,0:T(1,128)S(1)} %bitcast.10, bf16[16,128,256]{2,1,0:T(8,128)(2,1)S(1)} %all-to-all-done.2.y_ref, bf16[512,1024]{1,0:T(8,128)(2,1)S(1)} %gate.1.gate_hbm, f32[1,1024]{1,0:T(1,128)S(1)} %bitcast.7), custom_call_target="tpu_custom_call" | custom-call | flops 1073741824 | bytes 3145728 | tf_op jit(solution)/shard_map/final/pallas_call | solution.py:616
  (54 shorter events, 7.3 us)
Async XLA Ops:
  0.0 13.8 %copy-start.7 = (s32[512]{0:T(512)S(1)}, s32[512]{0:T(512)}, u32[]{:S(2)}) copy-start(s32[512]{0:T(512)} %param.15) | copy-start | bytes 6148
  4.8 28.4 %all-to-all-start = ((bf16[8,144,256]{2,1,0:T(8,128)(2,1)}), bf16[8,144,256]{2,1,0:T(8,128)(2,1)S(1)}, u32[]{:S(2)}, u32[]{:S(2)}) async-start(bf16[8,144,256]{2,1,0:T(8,128)(2,1)} %front.1), calls=%async_computation | async-start | bytes 1179648 | tf_op jit(solution)/shard_map/all_to_all | solution.py:550
  13.8 2.2 %copy-start = (bf16[2048,1024]{1,0:T(8,128)(2,1)S(1)}, bf16[2048,1024]{1,0:T(8,128)(2,1)}, u32[]{:S(2)}) copy-start(bf16[2048,1024]{1,0:T(8,128)(2,1)} %wv_ref.1) | copy-start | bytes 12582916
  17.6 21.6 %copy-start.5 = (f32[4,256]{1,0:T(4,128)S(1)}, f32[4,256]{1,0:T(4,128)}, u32[]{:S(2)}) copy-start(f32[4,256]{1,0:T(4,128)} %conv_ref.2) | copy-start | bytes 12292
  24.2 22.4 %copy-start.8 = (f32[8]{0:T(128)S(1)}, f32[8]{0:T(128)}, u32[]{:S(2)}) copy-start(f32[8]{0:T(128)} %bias_ref.1) | copy-start | bytes 100
  33.2 31.9 %all-to-all-start.1 = ((bf16[16,128,256]{2,1,0:T(8,128)(2,1)}), bf16[16,128,256]{2,1,0:T(8,128)(2,1)S(1)}, u32[]{:S(2)}, u32[]{:S(2)}) async-start(bf16[16,128,256]{2,1,0:T(8,128)(2,1)} %value.1), calls=%async_computation.1 | async-start | bytes 2097152 | tf_op jit(solution)/shard_map/all_to_all | solution.py:583
  37.1 2.0 %collective-permute-start = (bf16[8,144,256]{2,1,0:T(8,128)(2,1)S(1)}, bf16[8,144,256]{2,1,0:T(8,128)(2,1)S(1)}, u32[]{:S(2)}, u32[]{:S(2)}) collective-permute-start(bf16[8,144,256]{2,1,0:T(8,128)(2,1)S(1)} %all-to-all-done.own_ref), channel_id=1, source_target_pairs={{0,16},{16,0},{32,48},{48,32},{64,80},{80,64},{96,112},{112,96},{1... | collective-permute-start | bytes 1769480 | tf_op jit(solution)/shard_map/ppermute | solution.py:582
  42.3 10.5 %collective-permute-start.1 = (bf16[64,2048]{1,0:T(8,128)(2,1)S(1)}, bf16[64,2048]{1,0:T(8,128)(2,1)S(1)}, u32[]{:S(2)}, u32[]{:S(2)}) collective-permute-start(bf16[64,2048]{1,0:T(8,128)(2,1)S(1)} %get-tuple-element.35.refs_0_), channel_id=1, source_target_pairs={{0,4},{4,8},{8,12},{12,0},{1,5},{5,9},{9,13},{13,1},{2,6},{6,10},{... | collective-permute-start | bytes 786440 | tf_op jit(solution)/shard_map/ppermute | solution.py:600
  43.6 9.2 %collective-permute-start.2 = (bf16[64,2048]{1,0:T(8,128)(2,1)S(1)}, bf16[64,2048]{1,0:T(8,128)(2,1)S(1)}, u32[]{:S(2)}, u32[]{:S(2)}) collective-permute-start(bf16[64,2048]{1,0:T(8,128)(2,1)S(1)} %get-tuple-element.36.refs_1_), channel_id=1, source_target_pairs={{0,12},{4,0},{8,4},{12,8},{1,13},{5,1},{9,5},{13,9},{2,14},{6,2},{... | collective-permute-start | bytes 786440 | tf_op jit(solution)/shard_map/ppermute | solution.py:600
  45.1 23.8 %collective-permute-start.6 = (bf16[64,2048]{1,0:T(8,128)(2,1)S(1)}, bf16[64,2048]{1,0:T(8,128)(2,1)S(1)}, u32[]{:S(2)}, u32[]{:S(2)}) collective-permute-start(bf16[64,2048]{1,0:T(8,128)(2,1)S(1)} %get-tuple-element.35.refs_0_), channel_id=1, source_target_pairs={{0,12},{4,0},{8,4},{12,8},{1,13},{5,1},{9,5},{13,9},{2,14},{6,2},{... | collective-permute-start | bytes 786440 | tf_op jit(solution)/shard_map/ppermute | solution.py:601
  46.3 22.5 %collective-permute-start.3 = (bf16[64,2048]{1,0:T(8,128)(2,1)S(1)}, bf16[64,2048]{1,0:T(8,128)(2,1)}, u32[]{:S(2)}, u32[]{:S(2)}) collective-permute-start(bf16[64,2048]{1,0:T(8,128)(2,1)S(1)} %get-tuple-element.36.refs_1_), channel_id=1, source_target_pairs={{0,4},{4,8},{8,12},{12,0},{1,5},{5,9},{9,13},{13,1},{2,6},{6,10},{... | collective-permute-start | bytes 786440 | tf_op jit(solution)/shard_map/ppermute | solution.py:601
  52.8 16.1 %collective-permute-start.4 = (bf16[64,2048]{1,0:T(8,128)(2,1)S(1)}, bf16[64,2048]{1,0:T(8,128)(2,1)S(1)}, u32[]{:S(2)}, u32[]{:S(2)}) collective-permute-start(bf16[64,2048]{1,0:T(8,128)(2,1)S(1)} %collective-permute-done.1.refs_2_), channel_id=1, source_target_pairs={{0,4},{4,8},{8,12},{12,0},{1,5},{5,9},{9,13},{13,1},{2,6},{6,10},{... | collective-permute-start | bytes 786440 | tf_op jit(solution)/shard_map/ppermute | solution.py:604
  52.8 16.1 %collective-permute-start.5 = (bf16[64,2048]{1,0:T(8,128)(2,1)S(1)}, bf16[64,2048]{1,0:T(8,128)(2,1)S(1)}, u32[]{:S(2)}, u32[]{:S(2)}) collective-permute-start(bf16[64,2048]{1,0:T(8,128)(2,1)S(1)} %collective-permute-done.2.refs_7_), channel_id=1, source_target_pairs={{0,12},{4,0},{8,4},{12,8},{1,13},{5,1},{9,5},{13,9},{2,14},{6,2},{... | collective-permute-start | bytes 786440 | tf_op jit(solution)/shard_map/ppermute | solution.py:604
  66.0 5.7 %copy-start.13 = (f32[128,512]{1,0:T(8,128)S(1)}, f32[128,512]{1,0:T(8,128)}, u32[]{:S(2)}) copy-start(f32[128,512]{1,0:T(8,128)} %copy-done.11) | copy-start | bytes 786436
  68.9 1.6 %collective-permute-start.7 = (bf16[64,2048]{1,0:T(8,128)(2,1)S(1)}, bf16[64,2048]{1,0:T(8,128)(2,1)S(1)}, u32[]{:S(2)}, u32[]{:S(2)}) collective-permute-start(bf16[64,2048]{1,0:T(8,128)(2,1)S(1)} %get-tuple-element.35.refs_0_), channel_id=1, source_target_pairs={{0,16},{16,0},{32,48},{48,32},{64,80},{80,64},{96,112},{112,96},{1... | collective-permute-start | bytes 786440 | tf_op jit(solution)/shard_map/ppermute | solution.py:610
  69.0 1.9 %collective-permute-start.8 = (bf16[64,2048]{1,0:T(8,128)(2,1)S(1)}, bf16[64,2048]{1,0:T(8,128)(2,1)S(1)}, u32[]{:S(2)}, u32[]{:S(2)}) collective-permute-start(bf16[64,2048]{1,0:T(8,128)(2,1)S(1)} %get-tuple-element.36.refs_1_), channel_id=1, source_target_pairs={{0,16},{16,0},{32,48},{48,32},{64,80},{80,64},{96,112},{112,96},{1... | collective-permute-start | bytes 786440 | tf_op jit(solution)/shard_map/ppermute | solution.py:610
  69.5 2.1 %collective-permute-start.9 = (bf16[64,2048]{1,0:T(8,128)(2,1)S(1)}, bf16[64,2048]{1,0:T(8,128)(2,1)S(1)}, u32[]{:S(2)}, u32[]{:S(2)}) collective-permute-start(bf16[64,2048]{1,0:T(8,128)(2,1)S(1)} %collective-permute-done.1.refs_2_), channel_id=1, source_target_pairs={{0,16},{16,0},{32,48},{48,32},{64,80},{80,64},{96,112},{112,96},{1... | collective-permute-start | bytes 786440 | tf_op jit(solution)/shard_map/ppermute | solution.py:610
  69.6 5.0 %collective-permute-start.10 = (bf16[64,2048]{1,0:T(8,128)(2,1)}, bf16[64,2048]{1,0:T(8,128)(2,1)S(1)}, u32[]{:S(2)}, u32[]{:S(2)}) collective-permute-start(bf16[64,2048]{1,0:T(8,128)(2,1)} %collective-permute-done.3.refs_3_), channel_id=1, source_target_pairs={{0,16},{16,0},{32,48},{48,32},{64,80},{80,64},{96,112},{112,96},{1... | collective-permute-start | bytes 786440 | tf_op jit(solution)/shard_map/ppermute | solution.py:610
  70.0 4.6 %collective-permute-start.11 = (bf16[64,2048]{1,0:T(8,128)(2,1)S(1)}, bf16[64,2048]{1,0:T(8,128)(2,1)S(1)}, u32[]{:S(2)}, u32[]{:S(2)}) collective-permute-start(bf16[64,2048]{1,0:T(8,128)(2,1)S(1)} %collective-permute-done.4.refs_4_), channel_id=1, source_target_pairs={{0,16},{16,0},{32,48},{48,32},{64,80},{80,64},{96,112},{112,96},{1... | collective-permute-start | bytes 786440 | tf_op jit(solution)/shard_map/ppermute | solution.py:610
  70.5 4.1 %collective-permute-start.12 = (bf16[64,2048]{1,0:T(8,128)(2,1)S(1)}, bf16[64,2048]{1,0:T(8,128)(2,1)S(1)}, u32[]{:S(2)}, u32[]{:S(2)}) collective-permute-start(bf16[64,2048]{1,0:T(8,128)(2,1)S(1)} %collective-permute-done.5.refs_5_), channel_id=1, source_target_pairs={{0,16},{16,0},{32,48},{48,32},{64,80},{80,64},{96,112},{112,96},{1... | collective-permute-start | bytes 786440 | tf_op jit(solution)/shard_map/ppermute | solution.py:610
  70.9 3.7 %collective-permute-start.13 = (bf16[64,2048]{1,0:T(8,128)(2,1)S(1)}, bf16[64,2048]{1,0:T(8,128)(2,1)S(1)}, u32[]{:S(2)}, u32[]{:S(2)}) collective-permute-start(bf16[64,2048]{1,0:T(8,128)(2,1)S(1)} %collective-permute-done.6.refs_6_), channel_id=1, source_target_pairs={{0,16},{16,0},{32,48},{48,32},{64,80},{80,64},{96,112},{112,96},{1... | collective-permute-start | bytes 786440 | tf_op jit(solution)/shard_map/ppermute | solution.py:610
  71.6 3.0 %collective-permute-start.14 = (bf16[64,2048]{1,0:T(8,128)(2,1)S(1)}, bf16[64,2048]{1,0:T(8,128)(2,1)S(1)}, u32[]{:S(2)}, u32[]{:S(2)}) collective-permute-start(bf16[64,2048]{1,0:T(8,128)(2,1)S(1)} %collective-permute-done.2.refs_7_), channel_id=1, source_target_pairs={{0,16},{16,0},{32,48},{48,32},{64,80},{80,64},{96,112},{112,96},{1... | collective-permute-start | bytes 786440 | tf_op jit(solution)/shard_map/ppermute | solution.py:610
  84.2 32.5 %all-to-all-start.2 = ((bf16[16,128,256]{2,1,0:T(8,128)(2,1)}), bf16[16,128,256]{2,1,0:T(8,128)(2,1)S(1)}, u32[]{:S(2)}, u32[]{:S(2)}) async-start(bf16[16,128,256]{2,1,0:T(8,128)(2,1)} %scan.1), calls=%async_computation.2 | async-start | bytes 2097152 | tf_op jit(solution)/shard_map/all_to_all | solution.py:613
  92.5 24.2 %copy-start.6 = (f32[1024]{0:T(1024)S(1)}, f32[1024]{0:T(1024)}, u32[]{:S(2)}) copy-start(f32[1024]{0:T(1024)} %param.25) | copy-start | bytes 12292
  (8 other events, 9.1 us)

commit v4 on v3

--- a/solution.py
+++ b/solution.py
@@ -329,9 +329,17 @@
     return lax.fori_loop(0, SEQ // 2, gather, prev, unroll=4)
 
 
-def place_first(at_ref, ab_ref, table_ref, x_ref, xact_ref, last_ref, win_ref):
+def place_first(at_ref, ab_ref, table_ref, x_ref, *refs):
+    parts, (xact_ref, last_ref, bundle_ref, win_ref, sem_ref) = refs[:4], refs[4:]
+    copies = [
+        pltpu.make_async_copy(part, bundle_ref.at[k], sem_ref.at[k]) for k, part in enumerate(parts)
+    ]
+    for copy in copies:
+        copy.start()
     prev = jnp.zeros((CH, 128), F32)
     last_ref[...] = place_half(0, prev, at_ref, ab_ref, table_ref, x_ref, xact_ref, win_ref)
+    for copy in copies:
+        copy.wait()
 
 
 def place_second(at_ref, ab_ref, table_ref, x_ref, last_ref, xact_ref, win_ref):
@@ -339,8 +347,9 @@
 
 
 def scan_body(at_ref, ab_ref, table_ref, xact_a, xact_b, *refs):
-    owns, oths = refs[:8], refs[8:16]
-    out_ref, bc_ref, sem_ref = refs[16:]
+    owns, bundle, late = refs[:8], refs[8], refs[9:13]
+    out_ref, bc_ref, sem_ref = refs[13:]
+    oths = [bundle.at[0], bundle.at[1], bundle.at[2], *late, bundle.at[3]]
     m, c = at_ref[0], at_ref[1]
     copies = []
     for index in range(8):
@@ -403,7 +412,7 @@
     h = pl.program_id(0)
 
     def gate_copy(n):
-        part = pl.ds(pl.multiple_of(256 * n, 256), 256)
+        part = pl.ds(pl.multiple_of(512 * n, 512), 512)
         return pltpu.make_async_copy(gate_hbm.at[:, part], gate_ref.at[n], sem_ref.at[n])
 
     @pl.when(h == 0)
@@ -419,12 +428,12 @@
 
     low = iota((QUAD, 128), 1) < 64
     heads = []
-    for n in range(2):
+    for n in range(4):
         rows = []
         for q in range(4):
             at = slice(128 * (q // 2), 128 * (q // 2) + 128)
-            even = y_ref[4 * h + 2 * n, :, at].astype(F32)
-            odd = y_ref[4 * h + 2 * n + 1, :, at].astype(F32)
+            even = y_ref[8 * h + 2 * n, :, at].astype(F32)
+            odd = y_ref[8 * h + 2 * n + 1, :, at].astype(F32)
             if q % 2 == 0:
                 rows.append(jnp.where(low, even, pltpu.roll(odd, 64, 1)))
             else:
@@ -432,7 +441,7 @@
         heads.append(jnp.concatenate(rows, axis=0).astype(BF))
     y = dot(pick_ref[...], jnp.concatenate(heads, axis=1))
     gate_copy(h).wait()
-    for n in range(2):
+    for n in range(4):
         at = slice(128 * n, 128 * n + 128)
         gated = y[:, at] * gate_ref[h, :, at].astype(F32)
         mean = jnp.mean(gated * gated, axis=1, keepdims=True)
@@ -477,24 +486,25 @@
     )(*args)
 
 
-def run_place(kernel, outs, *args):
+def run_place(kernel, outs, args, parts=()):
+    sems = [pltpu.SemaphoreType.DMA((len(parts),))] if parts else []
     return pl.pallas_call(
         kernel,
         out_shape=outs,
-        in_specs=[smem()] * 2 + [vmem()] * (len(args) - 2),
+        in_specs=[smem()] * 2 + [vmem()] * (len(args) - 2) + [hbm()] * len(parts),
         out_specs=tuple(vmem() for _ in outs),
-        scratch_shapes=[pltpu.VMEM((KEYS, 256), BF)],
+        scratch_shapes=[pltpu.VMEM((KEYS, 256), BF), *sems],
         compiler_params=params(24),
         cost_estimate=cost(2 << 30, 2 << 20),
         name="place",
-    )(*args)
+    )(*args, *parts)
 
 
 def run_scan(*args):
     return pl.pallas_call(
         scan_body,
         out_shape=jax.ShapeDtypeStruct((SEQ, QUAD, 256), BF),
-        in_specs=[smem()] * 2 + [vmem()] * 3 + [hbm()] * 16,
+        in_specs=[smem()] * 2 + [vmem()] * 3 + [hbm()] * 13,
         out_specs=vmem(),
         scratch_shapes=[
             pltpu.VMEM((2, 256, 8 * ROWS), BF),
@@ -522,6 +532,30 @@
         compiler_params=params(60),
         cost_estimate=cost(1 << 30, 4 << 20),
         name="front",
+    )(*args)
+
+
+def run_final(*args):
+    heads = args[1].shape[0] // 2
+    return pl.pallas_call(
+        final_body,
+        grid=(heads // 4,),
+        out_shape=jax.ShapeDtypeStruct((ROWS, heads * 128), BF),
+        in_specs=[
+            pl.BlockSpec((1, ROWS), lambda h: (0, 0)),
+            vmem(),
+            hbm(),
+            pl.BlockSpec((1, 512), lambda h: (0, h)),
+        ],
+        out_specs=pl.BlockSpec((ROWS, 512), lambda h: (0, h)),
+        scratch_shapes=[
+            pltpu.VMEM((ROWS, ROWS), BF),
+            pltpu.VMEM((heads // 4, ROWS, 512), BF),
+            pltpu.SemaphoreType.DMA((heads // 4,)),
+        ],
+        compiler_params=params(12),
+        cost_estimate=cost(1 << 30, 3 << 20),
+        name="final",
     )(*args)
 
 
@@ -605,34 +639,18 @@
     owns = [bc_a, bc_b, one_a, one_b, two_a, two_b, three_a, three_b]
     part = jax.ShapeDtypeStruct((CH, 8 * ROWS), BF)
     last = jax.ShapeDtypeStruct((CH, 128), F32)
-    xact_a, last = run_place(place_first, (part, last), at, ab, table, x_all)
-    owns, xact_a = lax.optimization_barrier((owns, xact_a))
-    oths = [lax.ppermute(v, "seq", pairs) for v in owns]
-    (xact_b,) = run_place(place_second, (part,), at, ab, table, x_all, last)
+    sheaf = jax.ShapeDtypeStruct((4, CH, 4 * ROWS), BF)
+    xact_a, last, bundle = run_place(
+        place_first, (part, last, sheaf), (at, ab, table, x_all), (bc_a, bc_b, one_a, three_b)
+    )
+    late, bundle, xact_a = lax.optimization_barrier((owns[3:7], bundle, xact_a))
+    owns = [*owns[:3], *late, owns[7]]
+    oths = [lax.ppermute(v, "seq", pairs) for v in (bundle, *late)]
+    (xact_b,) = run_place(place_second, (part,), (at, ab, table, x_all, last))
     y_slots = run_scan(at, ab, table, xact_a, xact_b, *owns, *oths)
     y_all = lax.all_to_all(y_slots, "seq", 0, 0, tiled=True)
 
-    heads = step_bias.shape[0]
-    return pl.pallas_call(
-        final_body,
-        grid=(heads // 2,),
-        out_shape=jax.ShapeDtypeStruct((ROWS, heads * 128), BF),
-        in_specs=[
-            pl.BlockSpec((1, ROWS), lambda h: (0, 0)),
-            vmem(),
-            hbm(),
-            pl.BlockSpec((1, 256), lambda h: (0, h)),
-        ],
-        out_specs=pl.BlockSpec((ROWS, 256), lambda h: (0, h)),
-        scratch_shapes=[
-            pltpu.VMEM((ROWS, ROWS), BF),
-            pltpu.VMEM((heads // 2, ROWS, 256), BF),
-            pltpu.SemaphoreType.DMA((heads // 2,)),
-        ],
-        compiler_params=params(12),
-        cost_estimate=cost(1 << 30, 3 << 20),
-        name="final",
-    )(inv, y_all, gate, norm_gain.reshape(1, -1))
+    return run_final(inv, y_all, gate, norm_gain.reshape(1, -1))
 
 
 def solution(mesh):

time: 121 us -> 119 us (0.983)
  waiting for transfers between devices: 42 us -> 39.8 us
    ppermute x1, starting transfers between devices: 1.27 us -> 2.67 us  [body(): lax.ppermute(bc_a, 'mp', down)]
  transfers between devices with their start and end apart: 18 -> 15, of which waited for: 7 -> 5; matrix products, arithmetic and copies ran while one was open for 0% -> 0% of each run, Pallas kernels for 18% -> 19%
where the time goes in v4:
time: 119 us
  Pallas kernels  40 us (34%)
  waiting for transfers between devices  39.8 us (33%)
  starting transfers between devices  27.1 us (23%)
  local copies, waits for them, and re-layouts  11.3 us (9%)
    all_to_all x1, waiting for transfers between devices, body(): y_all = lax.all_to_all(y_slots, 'seq', 0, 0, tiled=True)  20.6 us
    unnamed x28, local copies, waits for them, and re-layouts  11.2 us
    pallas_call x1, Pallas kernels, run_scan(): pl.pallas_call(scan_body, out_shape=jax.ShapeDtypeStruct((SEQ, QUAD, 256)...  9.5 us
    all_to_all x1, starting transfers between devices, body(): lax.all_to_all(bc_slots, 'seq', 0, 0, axis_index_groups=lines, tiled=True)  9.03 us
    all_to_all x1, waiting for transfers between devices, body(): lax.all_to_all(bc_slots, 'seq', 0, 0, axis_index_groups=lines, tiled=True)  9 us
    all_to_all x1, waiting for transfers between devices, body(): x_all = lax.all_to_all(x_slots, 'seq', 0, 0, tiled=True)  8.39 us
    pallas_call x1, Pallas kernels, body(): pl.pallas_call(value_body, grid=(4,), out_shape=jax.ShapeDtypeStruct((SEQ...  6.57 us
    pallas_call x2, Pallas kernels, run_place(): pl.pallas_call(kernel, out_shape=outs, in_specs=[smem()] * 2 + [vmem()] *...  5.73 us
  transfers between devices with their start and end apart: 15, of which 5 were waited for; matrix products, arithmetic and copies ran while one was open for 0% of the time, Pallas kernels for 19%

profile of v4, /device:TPU:1, one launch (start us, length us, event | category | flops | bytes accessed | tf_op | source)
XLA Modules:
  0.0 118.7 jit_solution(16402533960661681417)
XLA Ops:
  0.0 4.8 %front.1 = bf16[8,144,256]{2,1,0:T(8,128)(2,1)} custom-call(s32[1,512]{1,0:T(1,128)} %bitcast.8, s32[1,512]{1,0:T(1,128)} %bitcast.12, bf16[512,2048]{1,0:T(8,128)(2,1)} %lat_ref.3, bf16[2048,256]{1,0:T(8,128)(2,1)} %wio_hbm.1, bf16[8,2048]{1,0:T(8,128)(2,1)} %bitcast.11), custom_call_target="tpu_custom_call" | custom-call | flops 1073741824 | bytes 4194304 | tf_op jit(solution)/shard_map/front/pallas_call | solution.py:520
  4.8 9.0 %all-to-all-start = ((bf16[8,144,256]{2,1,0:T(8,128)(2,1)}), bf16[8,144,256]{2,1,0:T(8,128)(2,1)S(1)}, u32[]{:S(2)}, u32[]{:S(2)}) async-start(bf16[8,144,256]{2,1,0:T(8,128)(2,1)} %front.1), calls=%async_computation | async-start | bytes 1179648 | tf_op jit(solution)/shard_map/all_to_all | solution.py:584
  13.8 2.2 %copy-done = bf16[2048,1024]{1,0:T(8,128)(2,1)S(1)} copy-done((bf16[2048,1024]{1,0:T(8,128)(2,1)S(1)}, bf16[2048,1024]{1,0:T(8,128)(2,1)}, u32[]{:S(2)}) %copy-start) | copy-done | bytes 4194328
  16.0 1.6 %copy-done.2 = bf16[512,2048]{1,0:T(8,128)(2,1)S(1)} copy-done((bf16[512,2048]{1,0:T(8,128)(2,1)S(1)}, bf16[512,2048]{1,0:T(8,128)(2,1)}, u32[]{:S(2)}) %copy-start.2) | copy-done | bytes 2097176
  17.6 6.6 %value.1 = bf16[16,128,256]{2,1,0:T(8,128)(2,1)} custom-call(s32[1,512]{1,0:T(1,128)S(1)} %bitcast.9, bf16[512,2048]{1,0:T(8,128)(2,1)S(1)} %copy-done.2, bf16[2048,1024]{1,0:T(8,128)(2,1)S(1)} %copy-done), custom_call_target="tpu_custom_call" | custom-call | flops 3221225472 | bytes 8388608 | tf_op jit(solution)/shard_map/value/pallas_call | solution.py:586
  24.2 9.0 %all-to-all-done.own_ref = bf16[8,144,256]{2,1,0:T(8,128)(2,1)S(1)} async-done(((bf16[8,144,256]{2,1,0:T(8,128)(2,1)}), bf16[8,144,256]{2,1,0:T(8,128)(2,1)S(1)}, u32[]{:S(2)}, u32[]{:S(2)}) %all-to-all-start) | async-done | bytes 589856 | tf_op jit(solution)/shard_map/all_to_all | solution.py:584
  33.2 3.9 %all-to-all-start.1 = ((bf16[16,128,256]{2,1,0:T(8,128)(2,1)}), bf16[16,128,256]{2,1,0:T(8,128)(2,1)S(1)}, u32[]{:S(2)}, u32[]{:S(2)}) async-start(bf16[16,128,256]{2,1,0:T(8,128)(2,1)} %value.1), calls=%async_computation.1 | async-start | bytes 2097152 | tf_op jit(solution)/shard_map/all_to_all | solution.py:617
  37.5 1.6 %collective-permute-done.oth_ref = bf16[8,144,256]{2,1,0:T(8,128)(2,1)S(1)} collective-permute-done((bf16[8,144,256]{2,1,0:T(8,128)(2,1)S(1)}, bf16[8,144,256]{2,1,0:T(8,128)(2,1)S(1)}, u32[]{:S(2)}, u32[]{:S(2)}) %collective-permute-start) | collective-permute-done | bytes 589856 | tf_op jit(solution)/shard_map/ppermute | solution.py:616
  39.2 3.1 %bc.1 = (bf16[64,2048]{1,0:T(8,128)(2,1)S(1)}, bf16[64,2048]{1,0:T(8,128)(2,1)S(1)}, s32[16,512]{1,0:T(8,128)S(1)}) custom-call(s32[4]{0:T(128)S(1)} %pad_add_fusion.at_ref, s32[512]{0:T(512)S(1)} %reshape.16.ab_ref, bf16[8,144,256]{2,1,0:T(8,128)(2,1)S(1)} %all-to-all-done.own_ref, bf16[8,144,256]{2,1,0:T(8,128)(2,1)S(1)} %collective-permute-done.oth_ref, ...), custom_call_target="tpu_custom_call" | custom-call | flops 1073741824 | bytes 2097152 | tf_op jit(solution)/shard_map/bc/pallas_call | solution.py:622
  42.3 1.3 %collective-permute-start.1 = (bf16[64,2048]{1,0:T(8,128)(2,1)S(1)}, bf16[64,2048]{1,0:T(8,128)(2,1)S(1)}, u32[]{:S(2)}, u32[]{:S(2)}) collective-permute-start(bf16[64,2048]{1,0:T(8,128)(2,1)S(1)} %get-tuple-element.23.refs_0_), channel_id=1, source_target_pairs={{0,4},{4,8},{8,12},{12,0},{1,5},{5,9},{9,13},{13,1},{2,6},{6,10},{... | collective-permute-start | bytes 786440 | tf_op jit(solution)/shard_map/ppermute | solution.py:634
  43.6 1.5 %collective-permute-start.2 = (bf16[64,2048]{1,0:T(8,128)(2,1)S(1)}, bf16[64,2048]{1,0:T(8,128)(2,1)S(1)}, u32[]{:S(2)}, u32[]{:S(2)}) collective-permute-start(bf16[64,2048]{1,0:T(8,128)(2,1)S(1)} %get-tuple-element.24.refs_1_), channel_id=1, source_target_pairs={{0,12},{4,0},{8,4},{12,8},{1,13},{5,1},{9,5},{13,9},{2,14},{6,2},{... | collective-permute-start | bytes 786440 | tf_op jit(solution)/shard_map/ppermute | solution.py:634
  45.1 2.7 %collective-permute-start.6 = (bf16[64,2048]{1,0:T(8,128)(2,1)S(1)}, bf16[64,2048]{1,0:T(8,128)(2,1)}, u32[]{:S(2)}, u32[]{:S(2)}) collective-permute-start(bf16[64,2048]{1,0:T(8,128)(2,1)S(1)} %get-tuple-element.23.refs_0_), channel_id=1, source_target_pairs={{0,12},{4,0},{8,4},{12,8},{1,13},{5,1},{9,5},{13,9},{2,14},{6,2},{... | collective-permute-start | bytes 786440 | tf_op jit(solution)/shard_map/ppermute | solution.py:635
  49.8 3.5 %time.1.table_ref = f32[128,512]{1,0:T(8,128)S(1)} custom-call(s32[4]{0:T(128)S(1)} %pad_add_fusion.at_ref, s32[512]{0:T(512)S(1)} %reshape.16.ab_ref, f32[8]{0:T(128)S(1)} %copy-done.8, f32[8]{0:T(128)S(1)} %copy-done.9, f32[8]{0:T(128)S(1)} %copy-done.10, s32[16,512]{1,0:T(8,128)S(1)} %get-tuple-element.25.code_ref, ...), custom_call_target="tpu_custom_call" | custom-call | flops 2147483648 | bytes 2097152 | tf_op jit(solution)/shard_map/time/pallas_call | solution.py:472
  54.0 2.7 %collective-permute-start.5 = (bf16[64,2048]{1,0:T(8,128)(2,1)S(1)}, bf16[64,2048]{1,0:T(8,128)(2,1)S(1)}, u32[]{:S(2)}, u32[]{:S(2)}) collective-permute-start(bf16[64,2048]{1,0:T(8,128)(2,1)S(1)} %collective-permute-done.2.refs_3_.refs_7_), channel_id=1, source_target_pairs={{0,12},{4,0},{8,4},{12,8},{1,13},{5,1},{9,5},{13,9},{2,14},{6,2},{... | collective-permute-start | bytes 786440 | tf_op jit(solution)/shard_map/ppermute | solution.py:638
  56.7 8.4 %all-to-all-done.1.x_ref = bf16[16,128,256]{2,1,0:T(8,128)(2,1)S(1)} async-done(((bf16[16,128,256]{2,1,0:T(8,128)(2,1)}), bf16[16,128,256]{2,1,0:T(8,128)(2,1)S(1)}, u32[]{:S(2)}, u32[]{:S(2)}) %all-to-all-start.1) | async-done | bytes 1048608 | tf_op jit(solution)/shard_map/all_to_all | solution.py:617
  66.0 2.9 %place.2 = (bf16[64,4096]{1,0:T(8,128)(2,1)S(1)}, f32[64,128]{1,0:T(8,128)S(1)}, bf16[4,64,2048]{2,1,0:T(8,128)(2,1)S(1)}) custom-call(s32[4]{0:T(128)S(1)} %pad_add_fusion.at_ref, s32[512]{0:T(512)S(1)} %reshape.16.ab_ref, f32[128,512]{1,0:T(8,128)S(1)} %copy-done.12, bf16[16,128,256]{2,1,0:T(8,128)(2,1)S(1)} %all-to-all-done.1.x_ref, ...), custom_call_target="tpu_custom_call" | custom-call | flops 2147483648 | bytes 2097152 | tf_op jit(solution)/shard_map/place/pallas_call | solution.py:491
  70.2 2.8 %place.3.xact_b = bf16[64,4096]{1,0:T(8,128)(2,1)S(1)} custom-call(s32[4]{0:T(128)S(1)} %pad_add_fusion.at_ref, s32[512]{0:T(512)S(1)} %reshape.16.ab_ref, f32[128,512]{1,0:T(8,128)S(1)} %copy-done.13, bf16[16,128,256]{2,1,0:T(8,128)(2,1)S(1)} %all-to-all-done.1.x_ref, f32[64,128]{1,0:T(8,128)S(1)} %get-tuple-element.33.last_ref), custom_call_target="tpu_custom_call" | custom-call | flops 2147483648 | bytes 2097152 | tf_op jit(solution)/shard_map/place/pallas_call | solution.py:491
  73.3 9.5 %scan.1 = bf16[16,128,256]{2,1,0:T(8,128)(2,1)} custom-call(s32[4]{0:T(128)S(1)} %pad_add_fusion.at_ref, s32[512]{0:T(512)S(1)} %reshape.16.ab_ref, f32[128,512]{1,0:T(8,128)S(1)} %copy-done.13, bf16[64,4096]{1,0:T(8,128)(2,1)S(1)} %get-tuple-element.32.xact_a, bf16[64,4096]{1,0:T(8,128)(2,1)S(1)} %place.3.xact_b, ...), custom_call_target="tpu_custom_call" | custom-call | flops 8589934592 | bytes 8388608 | tf_op jit(solution)/shard_map/scan/pallas_call | solution.py:504
  82.8 4.5 %all-to-all-start.2 = ((bf16[16,128,256]{2,1,0:T(8,128)(2,1)}), bf16[16,128,256]{2,1,0:T(8,128)(2,1)S(1)}, u32[]{:S(2)}, u32[]{:S(2)}) async-start(bf16[16,128,256]{2,1,0:T(8,128)(2,1)} %scan.1), calls=%async_computation.2 | async-start | bytes 2097152 | tf_op jit(solution)/shard_map/all_to_all | solution.py:651
  87.3 2.2 %copy-done.1 = bf16[2048,1024]{1,0:T(8,128)(2,1)S(1)} copy-done((bf16[2048,1024]{1,0:T(8,128)(2,1)S(1)}, bf16[2048,1024]{1,0:T(8,128)(2,1)}, u32[]{:S(2)}) %copy-start.1) | copy-done | bytes 4194328
  89.5 1.6 %copy-done.3 = bf16[512,2048]{1,0:T(8,128)(2,1)S(1)} copy-done((bf16[512,2048]{1,0:T(8,128)(2,1)S(1)}, bf16[512,2048]{1,0:T(8,128)(2,1)}, u32[]{:S(2)}) %copy-start.3) | copy-done | bytes 2097176
  91.1 3.6 %gate.1.gate_hbm = bf16[512,1024]{1,0:T(8,128)(2,1)S(1)} custom-call(bf16[512,2048]{1,0:T(8,128)(2,1)S(1)} %copy-done.3, bf16[2048,1024]{1,0:T(8,128)(2,1)S(1)} %copy-done.1), custom_call_target="tpu_custom_call" | custom-call | flops 2147483648 | bytes 8388608 | tf_op jit(solution)/shard_map/gate/pallas_call | solution.py:601
  94.7 20.6 %all-to-all-done.2.y_ref = bf16[16,128,256]{2,1,0:T(8,128)(2,1)S(1)} async-done(((bf16[16,128,256]{2,1,0:T(8,128)(2,1)}), bf16[16,128,256]{2,1,0:T(8,128)(2,1)S(1)}, u32[]{:S(2)}, u32[]{:S(2)}) %all-to-all-start.2) | async-done | bytes 1048608 | tf_op jit(solution)/shard_map/all_to_all | solution.py:651
  115.3 3.2 %final.1 = bf16[512,1024]{1,0:T(8,128)(2,1)} custom-call(s32[1,512]{1,0:T(1,128)S(1)} %bitcast.10, bf16[16,128,256]{2,1,0:T(8,128)(2,1)S(1)} %all-to-all-done.2.y_ref, bf16[512,1024]{1,0:T(8,128)(2,1)S(1)} %gate.1.gate_hbm, f32[1,1024]{1,0:T(1,128)S(1)} %bitcast.7), custom_call_target="tpu_custom_call" | custom-call | flops 1073741824 | bytes 3145728 | tf_op jit(solution)/shard_map/final/pallas_call | solution.py:540
  (48 shorter events, 5.6 us)
Async XLA Ops:
  0.0 13.8 %copy-start.7 = (s32[512]{0:T(512)S(1)}, s32[512]{0:T(512)}, u32[]{:S(2)}) copy-start(s32[512]{0:T(512)} %param.15) | copy-start | bytes 6148
  4.8 28.4 %all-to-all-start = ((bf16[8,144,256]{2,1,0:T(8,128)(2,1)}), bf16[8,144,256]{2,1,0:T(8,128)(2,1)S(1)}, u32[]{:S(2)}, u32[]{:S(2)}) async-start(bf16[8,144,256]{2,1,0:T(8,128)(2,1)} %front.1), calls=%async_computation | async-start | bytes 1179648 | tf_op jit(solution)/shard_map/all_to_all | solution.py:584
  13.8 2.2 %copy-start = (bf16[2048,1024]{1,0:T(8,128)(2,1)S(1)}, bf16[2048,1024]{1,0:T(8,128)(2,1)}, u32[]{:S(2)}) copy-start(bf16[2048,1024]{1,0:T(8,128)(2,1)} %wv_ref.1) | copy-start | bytes 12582916
  16.0 1.6 %copy-start.2 = (bf16[512,2048]{1,0:T(8,128)(2,1)S(1)}, bf16[512,2048]{1,0:T(8,128)(2,1)}, u32[]{:S(2)}) copy-start(bf16[512,2048]{1,0:T(8,128)(2,1)} %lat_ref.3) | copy-start | bytes 6291460
  17.6 21.6 %copy-start.5 = (f32[4,256]{1,0:T(4,128)S(1)}, f32[4,256]{1,0:T(4,128)}, u32[]{:S(2)}) copy-start(f32[4,256]{1,0:T(4,128)} %conv_ref.2) | copy-start | bytes 12292
  24.2 23.6 %copy-start.8 = (f32[8]{0:T(128)S(1)}, f32[8]{0:T(128)}, u32[]{:S(2)}) copy-start(f32[8]{0:T(128)} %bias_ref.1) | copy-start | bytes 100
  33.2 31.9 %all-to-all-start.1 = ((bf16[16,128,256]{2,1,0:T(8,128)(2,1)}), bf16[16,128,256]{2,1,0:T(8,128)(2,1)S(1)}, u32[]{:S(2)}, u32[]{:S(2)}) async-start(bf16[16,128,256]{2,1,0:T(8,128)(2,1)} %value.1), calls=%async_computation.1 | async-start | bytes 2097152 | tf_op jit(solution)/shard_map/all_to_all | solution.py:617
  37.1 2.0 %collective-permute-start = (bf16[8,144,256]{2,1,0:T(8,128)(2,1)S(1)}, bf16[8,144,256]{2,1,0:T(8,128)(2,1)S(1)}, u32[]{:S(2)}, u32[]{:S(2)}) collective-permute-start(bf16[8,144,256]{2,1,0:T(8,128)(2,1)S(1)} %all-to-all-done.own_ref), channel_id=1, source_target_pairs={{0,16},{16,0},{32,48},{48,32},{64,80},{80,64},{96,112},{112,96},{1... | collective-permute-start | bytes 1769480 | tf_op jit(solution)/shard_map/ppermute | solution.py:616
  42.3 11.7 %collective-permute-start.1 = (bf16[64,2048]{1,0:T(8,128)(2,1)S(1)}, bf16[64,2048]{1,0:T(8,128)(2,1)S(1)}, u32[]{:S(2)}, u32[]{:S(2)}) collective-permute-start(bf16[64,2048]{1,0:T(8,128)(2,1)S(1)} %get-tuple-element.23.refs_0_), channel_id=1, source_target_pairs={{0,4},{4,8},{8,12},{12,0},{1,5},{5,9},{9,13},{13,1},{2,6},{6,10},{... | collective-permute-start | bytes 786440 | tf_op jit(solution)/shard_map/ppermute | solution.py:634
  43.6 10.4 %collective-permute-start.2 = (bf16[64,2048]{1,0:T(8,128)(2,1)S(1)}, bf16[64,2048]{1,0:T(8,128)(2,1)S(1)}, u32[]{:S(2)}, u32[]{:S(2)}) collective-permute-start(bf16[64,2048]{1,0:T(8,128)(2,1)S(1)} %get-tuple-element.24.refs_1_), channel_id=1, source_target_pairs={{0,12},{4,0},{8,4},{12,8},{1,13},{5,1},{9,5},{13,9},{2,14},{6,2},{... | collective-permute-start | bytes 786440 | tf_op jit(solution)/shard_map/ppermute | solution.py:634
  45.1 23.9 %collective-permute-start.3 = (bf16[64,2048]{1,0:T(8,128)(2,1)S(1)}, bf16[64,2048]{1,0:T(8,128)(2,1)S(1)}, u32[]{:S(2)}, u32[]{:S(2)}) collective-permute-start(bf16[64,2048]{1,0:T(8,128)(2,1)S(1)} %get-tuple-element.24.refs_1_), channel_id=1, source_target_pairs={{0,4},{4,8},{8,12},{12,0},{1,5},{5,9},{9,13},{13,1},{2,6},{6,10},{... | collective-permute-start | bytes 786440 | tf_op jit(solution)/shard_map/ppermute | solution.py:635
  45.1 23.9 %collective-permute-start.6 = (bf16[64,2048]{1,0:T(8,128)(2,1)S(1)}, bf16[64,2048]{1,0:T(8,128)(2,1)}, u32[]{:S(2)}, u32[]{:S(2)}) collective-permute-start(bf16[64,2048]{1,0:T(8,128)(2,1)S(1)} %get-tuple-element.23.refs_0_), channel_id=1, source_target_pairs={{0,12},{4,0},{8,4},{12,8},{1,13},{5,1},{9,5},{13,9},{2,14},{6,2},{... | collective-permute-start | bytes 786440 | tf_op jit(solution)/shard_map/ppermute | solution.py:635
  54.0 15.0 %collective-permute-start.4 = (bf16[64,2048]{1,0:T(8,128)(2,1)S(1)}, bf16[64,2048]{1,0:T(8,128)(2,1)S(1)}, u32[]{:S(2)}, u32[]{:S(2)}) collective-permute-start(bf16[64,2048]{1,0:T(8,128)(2,1)S(1)} %collective-permute-done.1.refs_2_), channel_id=1, source_target_pairs={{0,4},{4,8},{8,12},{12,0},{1,5},{5,9},{9,13},{13,1},{2,6},{6,10},{... | collective-permute-start | bytes 786440 | tf_op jit(solution)/shard_map/ppermute | solution.py:638
  54.0 15.0 %collective-permute-start.5 = (bf16[64,2048]{1,0:T(8,128)(2,1)S(1)}, bf16[64,2048]{1,0:T(8,128)(2,1)S(1)}, u32[]{:S(2)}, u32[]{:S(2)}) collective-permute-start(bf16[64,2048]{1,0:T(8,128)(2,1)S(1)} %collective-permute-done.2.refs_3_.refs_7_), channel_id=1, source_target_pairs={{0,12},{4,0},{8,4},{12,8},{1,13},{5,1},{9,5},{13,9},{2,14},{6,2},{... | collective-permute-start | bytes 786440 | tf_op jit(solution)/shard_map/ppermute | solution.py:638
  66.0 4.2 %copy-start.13 = (f32[128,512]{1,0:T(8,128)S(1)}, f32[128,512]{1,0:T(8,128)}, u32[]{:S(2)}) copy-start(f32[128,512]{1,0:T(8,128)} %copy-done.11) | copy-start | bytes 786436
  69.0 4.2 %collective-permute-start.7 = (bf16[4,64,2048]{2,1,0:T(8,128)(2,1)S(1)}, bf16[4,64,2048]{2,1,0:T(8,128)(2,1)S(1)}, u32[]{:S(2)}, u32[]{:S(2)}) collective-permute-start(bf16[4,64,2048]{2,1,0:T(8,128)(2,1)S(1)} %get-tuple-element.38), channel_id=1, source_target_pairs={{0,16},{16,0},{32,48},{48,32},{64,80},{80,64},{96,112},{112,96},{1... | collective-permute-start | bytes 3145736 | tf_op jit(solution)/shard_map/ppermute | solution.py:648
  69.1 3.9 %collective-permute-start.10 = (bf16[64,2048]{1,0:T(8,128)(2,1)S(1)}, bf16[64,2048]{1,0:T(8,128)(2,1)S(1)}, u32[]{:S(2)}, u32[]{:S(2)}) collective-permute-start(bf16[64,2048]{1,0:T(8,128)(2,1)S(1)} %collective-permute-done.5.refs_5_), channel_id=1, source_target_pairs={{0,16},{16,0},{32,48},{48,32},{64,80},{80,64},{96,112},{112,96},{1... | collective-permute-start | bytes 786440 | tf_op jit(solution)/shard_map/ppermute | solution.py:648
  69.6 3.4 %collective-permute-start.11 = (bf16[64,2048]{1,0:T(8,128)(2,1)}, bf16[64,2048]{1,0:T(8,128)(2,1)S(1)}, u32[]{:S(2)}, u32[]{:S(2)}) collective-permute-start(bf16[64,2048]{1,0:T(8,128)(2,1)} %collective-permute-done.6.refs_6_), channel_id=1, source_target_pairs={{0,16},{16,0},{32,48},{48,32},{64,80},{80,64},{96,112},{112,96},{1... | collective-permute-start | bytes 786440 | tf_op jit(solution)/shard_map/ppermute | solution.py:648
  69.7 3.4 %collective-permute-start.8 = (bf16[64,2048]{1,0:T(8,128)(2,1)S(1)}, bf16[64,2048]{1,0:T(8,128)(2,1)S(1)}, u32[]{:S(2)}, u32[]{:S(2)}) collective-permute-start(bf16[64,2048]{1,0:T(8,128)(2,1)S(1)} %collective-permute-done.3.refs_3_), channel_id=1, source_target_pairs={{0,16},{16,0},{32,48},{48,32},{64,80},{80,64},{96,112},{112,96},{1... | collective-permute-start | bytes 786440 | tf_op jit(solution)/shard_map/ppermute | solution.py:648
  70.1 3.1 %collective-permute-start.9 = (bf16[64,2048]{1,0:T(8,128)(2,1)S(1)}, bf16[64,2048]{1,0:T(8,128)(2,1)S(1)}, u32[]{:S(2)}, u32[]{:S(2)}) collective-permute-start(bf16[64,2048]{1,0:T(8,128)(2,1)S(1)} %collective-permute-done.4.refs_4_), channel_id=1, source_target_pairs={{0,16},{16,0},{32,48},{48,32},{64,80},{80,64},{96,112},{112,96},{1... | collective-permute-start | bytes 786440 | tf_op jit(solution)/shard_map/ppermute | solution.py:648
  82.8 32.5 %all-to-all-start.2 = ((bf16[16,128,256]{2,1,0:T(8,128)(2,1)}), bf16[16,128,256]{2,1,0:T(8,128)(2,1)S(1)}, u32[]{:S(2)}, u32[]{:S(2)}) async-start(bf16[16,128,256]{2,1,0:T(8,128)(2,1)} %scan.1), calls=%async_computation.2 | async-start | bytes 2097152 | tf_op jit(solution)/shard_map/all_to_all | solution.py:651
  87.3 2.2 %copy-start.1 = (bf16[2048,1024]{1,0:T(8,128)(2,1)S(1)}, bf16[2048,1024]{1,0:T(8,128)(2,1)}, u32[]{:S(2)}) copy-start(bf16[2048,1024]{1,0:T(8,128)(2,1)} %w_ref.1) | copy-start | bytes 12582916
  89.5 1.6 %copy-start.3 = (bf16[512,2048]{1,0:T(8,128)(2,1)S(1)}, bf16[512,2048]{1,0:T(8,128)(2,1)}, u32[]{:S(2)}) copy-start(bf16[512,2048]{1,0:T(8,128)(2,1)} %lat_ref.3) | copy-start | bytes 6291460
  91.1 24.2 %copy-start.6 = (f32[1024]{0:T(1024)S(1)}, f32[1024]{0:T(1024)}, u32[]{:S(2)}) copy-start(f32[1024]{0:T(1024)} %param.25) | copy-start | bytes 12292
  (5 other events, 3.7 us)

commit v5 on v4

--- a/solution.py
+++ b/solution.py
@@ -81,12 +81,12 @@
         pltpu.make_async_copy(ord_hbm, ord_ref, sem_ref.at[1]),
     ]
     large = []
-    for k in range(4):
-        part = pl.ds(512 * k, 512)
+    for k in range(8):
+        part = pl.ds(256 * k, 256)
         large.append(
             (
                 pltpu.make_async_copy(lat_hbm.at[:, part], lat_ref.at[:, part], sem_ref.at[2 + k]),
-                pltpu.make_async_copy(wio_hbm.at[part], wio_ref.at[part], sem_ref.at[6 + k]),
+                pltpu.make_async_copy(wio_hbm.at[part], wio_ref.at[part], sem_ref.at[10 + k]),
             )
         )
     for copy in small:
@@ -132,7 +132,7 @@
     for k, pair in enumerate(large):
         for copy in pair:
             copy.wait()
-        part = slice(512 * k, 512 * k + 512)
+        part = slice(256 * k, 256 * k + 256)
         io = io + dot(lat_ref[:, part], wio_ref[part, :])
         rest = rest + dot(lat_ref[:, part], ws[:, part], ((1,), (1,)))
     io = dot(deal, io.astype(BF))
@@ -326,7 +326,7 @@
         xact_ref[:, pl.ds(pl.multiple_of(ROWS * e, ROWS), ROWS)] = act.astype(BF)
         return cur[:, ROWS - 128 :]
 
-    return lax.fori_loop(0, SEQ // 2, gather, prev, unroll=4)
+    return lax.fori_loop(0, SEQ // 2, gather, prev, unroll=8)
 
 
 def place_first(at_ref, ab_ref, table_ref, x_ref, *refs):
@@ -527,7 +527,7 @@
             pltpu.VMEM((1, ROWS), I32),
             pltpu.VMEM(args[2].shape, BF),
             pltpu.VMEM(args[3].shape, BF),
-            pltpu.SemaphoreType.DMA((10,)),
+            pltpu.SemaphoreType.DMA((18,)),
         ],
         compiler_params=params(60),
         cost_estimate=cost(1 << 30, 4 << 20),

time: 119 us -> 119 us (level)
  transfers between devices with their start and end apart: 15 -> 15, of which waited for: 5 -> 7; matrix products, arithmetic and copies ran while one was open for 0% -> 0% of each run, Pallas kernels for 19% -> 18%
where the time goes in v5:
time: 119 us; the launch traced here: 118 us
  waiting for transfers between devices  40.3 us (34%)
  Pallas kernels  39.1 us (33%)
  starting transfers between devices  27 us (23%)
  local copies, waits for them, and re-layouts  11.3 us (9%)
    all_to_all x1, waiting for transfers between devices, body(): y_all = lax.all_to_all(y_slots, 'seq', 0, 0, tiled=True)  20.6 us
    unnamed x28, local copies, waits for them, and re-layouts  11.2 us
    pallas_call x1, Pallas kernels, run_scan(): pl.pallas_call(scan_body, out_shape=jax.ShapeDtypeStruct((SEQ, QUAD, 256)...  9.54 us
    all_to_all x1, starting transfers between devices, body(): lax.all_to_all(bc_slots, 'seq', 0, 0, axis_index_groups=lines, tiled=True)  9.03 us
    all_to_all x1, waiting for transfers between devices, body(): lax.all_to_all(bc_slots, 'seq', 0, 0, axis_index_groups=lines, tiled=True)  9 us
    all_to_all x1, waiting for transfers between devices, body(): x_all = lax.all_to_all(x_slots, 'seq', 0, 0, tiled=True)  8.42 us
    pallas_call x1, Pallas kernels, body(): pl.pallas_call(value_body, grid=(4,), out_shape=jax.ShapeDtypeStruct((SEQ...  6.57 us
    pallas_call x2, Pallas kernels, run_place(): pl.pallas_call(kernel, out_shape=outs, in_specs=[smem()] * 2 + [vmem()] *...  4.8 us
  transfers between devices with their start and end apart: 15, of which 7 were waited for; matrix products, arithmetic and copies ran while one was open for 0% of the time, Pallas kernels for 18%

profile of v5, /device:TPU:1, one launch (start us, length us, event | category | flops | bytes accessed | tf_op | source)
XLA Modules:
  0.0 118.1 jit_solution(4309825577077702279)
XLA Ops:
  0.0 4.8 %front.1 = bf16[8,144,256]{2,1,0:T(8,128)(2,1)} custom-call(s32[1,512]{1,0:T(1,128)} %bitcast.8, s32[1,512]{1,0:T(1,128)} %bitcast.12, bf16[512,2048]{1,0:T(8,128)(2,1)} %lat_ref.3, bf16[2048,256]{1,0:T(8,128)(2,1)} %wio_hbm.1, bf16[8,2048]{1,0:T(8,128)(2,1)} %bitcast.11), custom_call_target="tpu_custom_call" | custom-call | flops 1073741824 | bytes 4194304 | tf_op jit(solution)/shard_map/front/pallas_call | solution.py:520
  4.8 9.0 %all-to-all-start = ((bf16[8,144,256]{2,1,0:T(8,128)(2,1)}), bf16[8,144,256]{2,1,0:T(8,128)(2,1)S(1)}, u32[]{:S(2)}, u32[]{:S(2)}) async-start(bf16[8,144,256]{2,1,0:T(8,128)(2,1)} %front.1), calls=%async_computation | async-start | bytes 1179648 | tf_op jit(solution)/shard_map/all_to_all | solution.py:584
  13.8 2.2 %copy-done = bf16[2048,1024]{1,0:T(8,128)(2,1)S(1)} copy-done((bf16[2048,1024]{1,0:T(8,128)(2,1)S(1)}, bf16[2048,1024]{1,0:T(8,128)(2,1)}, u32[]{:S(2)}) %copy-start) | copy-done | bytes 4194328
  16.0 1.6 %copy-done.2 = bf16[512,2048]{1,0:T(8,128)(2,1)S(1)} copy-done((bf16[512,2048]{1,0:T(8,128)(2,1)S(1)}, bf16[512,2048]{1,0:T(8,128)(2,1)}, u32[]{:S(2)}) %copy-start.2) | copy-done | bytes 2097176
  17.6 6.6 %value.1 = bf16[16,128,256]{2,1,0:T(8,128)(2,1)} custom-call(s32[1,512]{1,0:T(1,128)S(1)} %bitcast.9, bf16[512,2048]{1,0:T(8,128)(2,1)S(1)} %copy-done.2, bf16[2048,1024]{1,0:T(8,128)(2,1)S(1)} %copy-done), custom_call_target="tpu_custom_call" | custom-call | flops 3221225472 | bytes 8388608 | tf_op jit(solution)/shard_map/value/pallas_call | solution.py:586
  24.2 9.0 %all-to-all-done.own_ref = bf16[8,144,256]{2,1,0:T(8,128)(2,1)S(1)} async-done(((bf16[8,144,256]{2,1,0:T(8,128)(2,1)}), bf16[8,144,256]{2,1,0:T(8,128)(2,1)S(1)}, u32[]{:S(2)}, u32[]{:S(2)}) %all-to-all-start) | async-done | bytes 589856 | tf_op jit(solution)/shard_map/all_to_all | solution.py:584
  33.2 3.9 %all-to-all-start.1 = ((bf16[16,128,256]{2,1,0:T(8,128)(2,1)}), bf16[16,128,256]{2,1,0:T(8,128)(2,1)S(1)}, u32[]{:S(2)}, u32[]{:S(2)}) async-start(bf16[16,128,256]{2,1,0:T(8,128)(2,1)} %value.1), calls=%async_computation.1 | async-start | bytes 2097152 | tf_op jit(solution)/shard_map/all_to_all | solution.py:617
  37.5 1.6 %collective-permute-done.oth_ref = bf16[8,144,256]{2,1,0:T(8,128)(2,1)S(1)} collective-permute-done((bf16[8,144,256]{2,1,0:T(8,128)(2,1)S(1)}, bf16[8,144,256]{2,1,0:T(8,128)(2,1)S(1)}, u32[]{:S(2)}, u32[]{:S(2)}) %collective-permute-start) | collective-permute-done | bytes 589856 | tf_op jit(solution)/shard_map/ppermute | solution.py:616
  39.2 3.1 %bc.1 = (bf16[64,2048]{1,0:T(8,128)(2,1)S(1)}, bf16[64,2048]{1,0:T(8,128)(2,1)S(1)}, s32[16,512]{1,0:T(8,128)S(1)}) custom-call(s32[4]{0:T(128)S(1)} %pad_add_fusion.at_ref, s32[512]{0:T(512)S(1)} %reshape.16.ab_ref, bf16[8,144,256]{2,1,0:T(8,128)(2,1)S(1)} %all-to-all-done.own_ref, bf16[8,144,256]{2,1,0:T(8,128)(2,1)S(1)} %collective-permute-done.oth_ref, ...), custom_call_target="tpu_custom_call" | custom-call | flops 1073741824 | bytes 2097152 | tf_op jit(solution)/shard_map/bc/pallas_call | solution.py:622
  42.3 1.3 %collective-permute-start.1 = (bf16[64,2048]{1,0:T(8,128)(2,1)S(1)}, bf16[64,2048]{1,0:T(8,128)(2,1)S(1)}, u32[]{:S(2)}, u32[]{:S(2)}) collective-permute-start(bf16[64,2048]{1,0:T(8,128)(2,1)S(1)} %get-tuple-element.23.refs_0_), channel_id=1, source_target_pairs={{0,4},{4,8},{8,12},{12,0},{1,5},{5,9},{9,13},{13,1},{2,6},{6,10},{... | collective-permute-start | bytes 786440 | tf_op jit(solution)/shard_map/ppermute | solution.py:634
  43.6 1.5 %collective-permute-start.2 = (bf16[64,2048]{1,0:T(8,128)(2,1)S(1)}, bf16[64,2048]{1,0:T(8,128)(2,1)S(1)}, u32[]{:S(2)}, u32[]{:S(2)}) collective-permute-start(bf16[64,2048]{1,0:T(8,128)(2,1)S(1)} %get-tuple-element.24.refs_1_), channel_id=1, source_target_pairs={{0,12},{4,0},{8,4},{12,8},{1,13},{5,1},{9,5},{13,9},{2,14},{6,2},{... | collective-permute-start | bytes 786440 | tf_op jit(solution)/shard_map/ppermute | solution.py:634
  45.1 2.7 %collective-permute-start.6 = (bf16[64,2048]{1,0:T(8,128)(2,1)S(1)}, bf16[64,2048]{1,0:T(8,128)(2,1)}, u32[]{:S(2)}, u32[]{:S(2)}) collective-permute-start(bf16[64,2048]{1,0:T(8,128)(2,1)S(1)} %get-tuple-element.23.refs_0_), channel_id=1, source_target_pairs={{0,12},{4,0},{8,4},{12,8},{1,13},{5,1},{9,5},{13,9},{2,14},{6,2},{... | collective-permute-start | bytes 786440 | tf_op jit(solution)/shard_map/ppermute | solution.py:635
  49.8 3.5 %time.1.table_ref = f32[128,512]{1,0:T(8,128)S(1)} custom-call(s32[4]{0:T(128)S(1)} %pad_add_fusion.at_ref, s32[512]{0:T(512)S(1)} %reshape.16.ab_ref, f32[8]{0:T(128)S(1)} %copy-done.8, f32[8]{0:T(128)S(1)} %copy-done.9, f32[8]{0:T(128)S(1)} %copy-done.10, s32[16,512]{1,0:T(8,128)S(1)} %get-tuple-element.25.code_ref, ...), custom_call_target="tpu_custom_call" | custom-call | flops 2147483648 | bytes 2097152 | tf_op jit(solution)/shard_map/time/pallas_call | solution.py:472
  54.0 2.7 %collective-permute-start.5 = (bf16[64,2048]{1,0:T(8,128)(2,1)S(1)}, bf16[64,2048]{1,0:T(8,128)(2,1)S(1)}, u32[]{:S(2)}, u32[]{:S(2)}) collective-permute-start(bf16[64,2048]{1,0:T(8,128)(2,1)S(1)} %collective-permute-done.2.refs_3_.refs_7_), channel_id=1, source_target_pairs={{0,12},{4,0},{8,4},{12,8},{1,13},{5,1},{9,5},{13,9},{2,14},{6,2},{... | collective-permute-start | bytes 786440 | tf_op jit(solution)/shard_map/ppermute | solution.py:638
  56.6 8.4 %all-to-all-done.1.x_ref = bf16[16,128,256]{2,1,0:T(8,128)(2,1)S(1)} async-done(((bf16[16,128,256]{2,1,0:T(8,128)(2,1)}), bf16[16,128,256]{2,1,0:T(8,128)(2,1)S(1)}, u32[]{:S(2)}, u32[]{:S(2)}) %all-to-all-start.1) | async-done | bytes 1048608 | tf_op jit(solution)/shard_map/all_to_all | solution.py:617
  66.0 2.5 %place.2 = (bf16[64,4096]{1,0:T(8,128)(2,1)S(1)}, f32[64,128]{1,0:T(8,128)S(1)}, bf16[4,64,2048]{2,1,0:T(8,128)(2,1)S(1)}) custom-call(s32[4]{0:T(128)S(1)} %pad_add_fusion.at_ref, s32[512]{0:T(512)S(1)} %reshape.16.ab_ref, f32[128,512]{1,0:T(8,128)S(1)} %copy-done.12, bf16[16,128,256]{2,1,0:T(8,128)(2,1)S(1)} %all-to-all-done.1.x_ref, ...), custom_call_target="tpu_custom_call" | custom-call | flops 2147483648 | bytes 2097152 | tf_op jit(solution)/shard_map/place/pallas_call | solution.py:491
  69.8 2.3 %place.3.xact_b = bf16[64,4096]{1,0:T(8,128)(2,1)S(1)} custom-call(s32[4]{0:T(128)S(1)} %pad_add_fusion.at_ref, s32[512]{0:T(512)S(1)} %reshape.16.ab_ref, f32[128,512]{1,0:T(8,128)S(1)} %copy-done.13, bf16[16,128,256]{2,1,0:T(8,128)(2,1)S(1)} %all-to-all-done.1.x_ref, f32[64,128]{1,0:T(8,128)S(1)} %get-tuple-element.33.last_ref), custom_call_target="tpu_custom_call" | custom-call | flops 2147483648 | bytes 2097152 | tf_op jit(solution)/shard_map/place/pallas_call | solution.py:491
  72.8 9.5 %scan.1 = bf16[16,128,256]{2,1,0:T(8,128)(2,1)} custom-call(s32[4]{0:T(128)S(1)} %pad_add_fusion.at_ref, s32[512]{0:T(512)S(1)} %reshape.16.ab_ref, f32[128,512]{1,0:T(8,128)S(1)} %copy-done.13, bf16[64,4096]{1,0:T(8,128)(2,1)S(1)} %get-tuple-element.32.xact_a, bf16[64,4096]{1,0:T(8,128)(2,1)S(1)} %place.3.xact_b, ...), custom_call_target="tpu_custom_call" | custom-call | flops 8589934592 | bytes 8388608 | tf_op jit(solution)/shard_map/scan/pallas_call | solution.py:504
  82.3 4.4 %all-to-all-start.2 = ((bf16[16,128,256]{2,1,0:T(8,128)(2,1)}), bf16[16,128,256]{2,1,0:T(8,128)(2,1)S(1)}, u32[]{:S(2)}, u32[]{:S(2)}) async-start(bf16[16,128,256]{2,1,0:T(8,128)(2,1)} %scan.1), calls=%async_computation.2 | async-start | bytes 2097152 | tf_op jit(solution)/shard_map/all_to_all | solution.py:651
  86.8 2.2 %copy-done.1 = bf16[2048,1024]{1,0:T(8,128)(2,1)S(1)} copy-done((bf16[2048,1024]{1,0:T(8,128)(2,1)S(1)}, bf16[2048,1024]{1,0:T(8,128)(2,1)}, u32[]{:S(2)}) %copy-start.1) | copy-done | bytes 4194328
  88.9 1.6 %copy-done.3 = bf16[512,2048]{1,0:T(8,128)(2,1)S(1)} copy-done((bf16[512,2048]{1,0:T(8,128)(2,1)S(1)}, bf16[512,2048]{1,0:T(8,128)(2,1)}, u32[]{:S(2)}) %copy-start.3) | copy-done | bytes 2097176
  90.5 3.6 %gate.1.gate_hbm = bf16[512,1024]{1,0:T(8,128)(2,1)S(1)} custom-call(bf16[512,2048]{1,0:T(8,128)(2,1)S(1)} %copy-done.3, bf16[2048,1024]{1,0:T(8,128)(2,1)S(1)} %copy-done.1), custom_call_target="tpu_custom_call" | custom-call | flops 2147483648 | bytes 8388608 | tf_op jit(solution)/shard_map/gate/pallas_call | solution.py:601
  94.1 20.6 %all-to-all-done.2.y_ref = bf16[16,128,256]{2,1,0:T(8,128)(2,1)S(1)} async-done(((bf16[16,128,256]{2,1,0:T(8,128)(2,1)}), bf16[16,128,256]{2,1,0:T(8,128)(2,1)S(1)}, u32[]{:S(2)}, u32[]{:S(2)}) %all-to-all-start.2) | async-done | bytes 1048608 | tf_op jit(solution)/shard_map/all_to_all | solution.py:651
  114.7 3.2 %final.1 = bf16[512,1024]{1,0:T(8,128)(2,1)} custom-call(s32[1,512]{1,0:T(1,128)S(1)} %bitcast.10, bf16[16,128,256]{2,1,0:T(8,128)(2,1)S(1)} %all-to-all-done.2.y_ref, bf16[512,1024]{1,0:T(8,128)(2,1)S(1)} %gate.1.gate_hbm, f32[1,1024]{1,0:T(1,128)S(1)} %bitcast.7), custom_call_target="tpu_custom_call" | custom-call | flops 1073741824 | bytes 3145728 | tf_op jit(solution)/shard_map/final/pallas_call | solution.py:540
  (48 shorter events, 6.1 us)
Async XLA Ops:
  0.0 13.8 %copy-start.7 = (s32[512]{0:T(512)S(1)}, s32[512]{0:T(512)}, u32[]{:S(2)}) copy-start(s32[512]{0:T(512)} %param.15) | copy-start | bytes 6148
  4.8 28.4 %all-to-all-start = ((bf16[8,144,256]{2,1,0:T(8,128)(2,1)}), bf16[8,144,256]{2,1,0:T(8,128)(2,1)S(1)}, u32[]{:S(2)}, u32[]{:S(2)}) async-start(bf16[8,144,256]{2,1,0:T(8,128)(2,1)} %front.1), calls=%async_computation | async-start | bytes 1179648 | tf_op jit(solution)/shard_map/all_to_all | solution.py:584
  13.8 2.2 %copy-start = (bf16[2048,1024]{1,0:T(8,128)(2,1)S(1)}, bf16[2048,1024]{1,0:T(8,128)(2,1)}, u32[]{:S(2)}) copy-start(bf16[2048,1024]{1,0:T(8,128)(2,1)} %wv_ref.1) | copy-start | bytes 12582916
  16.0 1.6 %copy-start.2 = (bf16[512,2048]{1,0:T(8,128)(2,1)S(1)}, bf16[512,2048]{1,0:T(8,128)(2,1)}, u32[]{:S(2)}) copy-start(bf16[512,2048]{1,0:T(8,128)(2,1)} %lat_ref.3) | copy-start | bytes 6291460
  17.6 21.6 %copy-start.5 = (f32[4,256]{1,0:T(4,128)S(1)}, f32[4,256]{1,0:T(4,128)}, u32[]{:S(2)}) copy-start(f32[4,256]{1,0:T(4,128)} %conv_ref.2) | copy-start | bytes 12292
  24.2 23.6 %copy-start.8 = (f32[8]{0:T(128)S(1)}, f32[8]{0:T(128)}, u32[]{:S(2)}) copy-start(f32[8]{0:T(128)} %bias_ref.1) | copy-start | bytes 100
  33.2 31.9 %all-to-all-start.1 = ((bf16[16,128,256]{2,1,0:T(8,128)(2,1)}), bf16[16,128,256]{2,1,0:T(8,128)(2,1)S(1)}, u32[]{:S(2)}, u32[]{:S(2)}) async-start(bf16[16,128,256]{2,1,0:T(8,128)(2,1)} %value.1), calls=%async_computation.1 | async-start | bytes 2097152 | tf_op jit(solution)/shard_map/all_to_all | solution.py:617
  37.1 2.0 %collective-permute-start = (bf16[8,144,256]{2,1,0:T(8,128)(2,1)S(1)}, bf16[8,144,256]{2,1,0:T(8,128)(2,1)S(1)}, u32[]{:S(2)}, u32[]{:S(2)}) collective-permute-start(bf16[8,144,256]{2,1,0:T(8,128)(2,1)S(1)} %all-to-all-done.own_ref), channel_id=1, source_target_pairs={{0,16},{16,0},{32,48},{48,32},{64,80},{80,64},{96,112},{112,96},{1... | collective-permute-start | bytes 1769480 | tf_op jit(solution)/shard_map/ppermute | solution.py:616
  42.3 11.7 %collective-permute-start.1 = (bf16[64,2048]{1,0:T(8,128)(2,1)S(1)}, bf16[64,2048]{1,0:T(8,128)(2,1)S(1)}, u32[]{:S(2)}, u32[]{:S(2)}) collective-permute-start(bf16[64,2048]{1,0:T(8,128)(2,1)S(1)} %get-tuple-element.23.refs_0_), channel_id=1, source_target_pairs={{0,4},{4,8},{8,12},{12,0},{1,5},{5,9},{9,13},{13,1},{2,6},{6,10},{... | collective-permute-start | bytes 786440 | tf_op jit(solution)/shard_map/ppermute | solution.py:634
  43.6 10.4 %collective-permute-start.2 = (bf16[64,2048]{1,0:T(8,128)(2,1)S(1)}, bf16[64,2048]{1,0:T(8,128)(2,1)S(1)}, u32[]{:S(2)}, u32[]{:S(2)}) collective-permute-start(bf16[64,2048]{1,0:T(8,128)(2,1)S(1)} %get-tuple-element.24.refs_1_), channel_id=1, source_target_pairs={{0,12},{4,0},{8,4},{12,8},{1,13},{5,1},{9,5},{13,9},{2,14},{6,2},{... | collective-permute-start | bytes 786440 | tf_op jit(solution)/shard_map/ppermute | solution.py:634
  45.1 23.5 %collective-permute-start.3 = (bf16[64,2048]{1,0:T(8,128)(2,1)S(1)}, bf16[64,2048]{1,0:T(8,128)(2,1)S(1)}, u32[]{:S(2)}, u32[]{:S(2)}) collective-permute-start(bf16[64,2048]{1,0:T(8,128)(2,1)S(1)} %get-tuple-element.24.refs_1_), channel_id=1, source_target_pairs={{0,4},{4,8},{8,12},{12,0},{1,5},{5,9},{9,13},{13,1},{2,6},{6,10},{... | collective-permute-start | bytes 786440 | tf_op jit(solution)/shard_map/ppermute | solution.py:635
  45.1 23.5 %collective-permute-start.6 = (bf16[64,2048]{1,0:T(8,128)(2,1)S(1)}, bf16[64,2048]{1,0:T(8,128)(2,1)}, u32[]{:S(2)}, u32[]{:S(2)}) collective-permute-start(bf16[64,2048]{1,0:T(8,128)(2,1)S(1)} %get-tuple-element.23.refs_0_), channel_id=1, source_target_pairs={{0,12},{4,0},{8,4},{12,8},{1,13},{5,1},{9,5},{13,9},{2,14},{6,2},{... | collective-permute-start | bytes 786440 | tf_op jit(solution)/shard_map/ppermute | solution.py:635
  54.0 14.6 %collective-permute-start.4 = (bf16[64,2048]{1,0:T(8,128)(2,1)S(1)}, bf16[64,2048]{1,0:T(8,128)(2,1)S(1)}, u32[]{:S(2)}, u32[]{:S(2)}) collective-permute-start(bf16[64,2048]{1,0:T(8,128)(2,1)S(1)} %collective-permute-done.1.refs_2_), channel_id=1, source_target_pairs={{0,4},{4,8},{8,12},{12,0},{1,5},{5,9},{9,13},{13,1},{2,6},{6,10},{... | collective-permute-start | bytes 786440 | tf_op jit(solution)/shard_map/ppermute | solution.py:638
  54.0 14.6 %collective-permute-start.5 = (bf16[64,2048]{1,0:T(8,128)(2,1)S(1)}, bf16[64,2048]{1,0:T(8,128)(2,1)S(1)}, u32[]{:S(2)}, u32[]{:S(2)}) collective-permute-start(bf16[64,2048]{1,0:T(8,128)(2,1)S(1)} %collective-permute-done.2.refs_3_.refs_7_), channel_id=1, source_target_pairs={{0,12},{4,0},{8,4},{12,8},{1,13},{5,1},{9,5},{13,9},{2,14},{6,2},{... | collective-permute-start | bytes 786440 | tf_op jit(solution)/shard_map/ppermute | solution.py:638
  66.0 3.7 %copy-start.13 = (f32[128,512]{1,0:T(8,128)S(1)}, f32[128,512]{1,0:T(8,128)}, u32[]{:S(2)}) copy-start(f32[128,512]{1,0:T(8,128)} %copy-done.11) | copy-start | bytes 786436
  68.6 4.2 %collective-permute-start.7 = (bf16[4,64,2048]{2,1,0:T(8,128)(2,1)S(1)}, bf16[4,64,2048]{2,1,0:T(8,128)(2,1)S(1)}, u32[]{:S(2)}, u32[]{:S(2)}) collective-permute-start(bf16[4,64,2048]{2,1,0:T(8,128)(2,1)S(1)} %get-tuple-element.38), channel_id=1, source_target_pairs={{0,16},{16,0},{32,48},{48,32},{64,80},{80,64},{96,112},{112,96},{1... | collective-permute-start | bytes 3145736 | tf_op jit(solution)/shard_map/ppermute | solution.py:648
  68.7 3.4 %collective-permute-start.10 = (bf16[64,2048]{1,0:T(8,128)(2,1)S(1)}, bf16[64,2048]{1,0:T(8,128)(2,1)S(1)}, u32[]{:S(2)}, u32[]{:S(2)}) collective-permute-start(bf16[64,2048]{1,0:T(8,128)(2,1)S(1)} %collective-permute-done.5.refs_5_), channel_id=1, source_target_pairs={{0,16},{16,0},{32,48},{48,32},{64,80},{80,64},{96,112},{112,96},{1... | collective-permute-start | bytes 786440 | tf_op jit(solution)/shard_map/ppermute | solution.py:648
  69.1 3.1 %collective-permute-start.11 = (bf16[64,2048]{1,0:T(8,128)(2,1)}, bf16[64,2048]{1,0:T(8,128)(2,1)S(1)}, u32[]{:S(2)}, u32[]{:S(2)}) collective-permute-start(bf16[64,2048]{1,0:T(8,128)(2,1)} %collective-permute-done.6.refs_6_), channel_id=1, source_target_pairs={{0,16},{16,0},{32,48},{48,32},{64,80},{80,64},{96,112},{112,96},{1... | collective-permute-start | bytes 786440 | tf_op jit(solution)/shard_map/ppermute | solution.py:648
  69.2 3.2 %collective-permute-start.8 = (bf16[64,2048]{1,0:T(8,128)(2,1)S(1)}, bf16[64,2048]{1,0:T(8,128)(2,1)S(1)}, u32[]{:S(2)}, u32[]{:S(2)}) collective-permute-start(bf16[64,2048]{1,0:T(8,128)(2,1)S(1)} %collective-permute-done.3.refs_3_), channel_id=1, source_target_pairs={{0,16},{16,0},{32,48},{48,32},{64,80},{80,64},{96,112},{112,96},{1... | collective-permute-start | bytes 786440 | tf_op jit(solution)/shard_map/ppermute | solution.py:648
  69.7 3.1 %collective-permute-start.9 = (bf16[64,2048]{1,0:T(8,128)(2,1)S(1)}, bf16[64,2048]{1,0:T(8,128)(2,1)S(1)}, u32[]{:S(2)}, u32[]{:S(2)}) collective-permute-start(bf16[64,2048]{1,0:T(8,128)(2,1)S(1)} %collective-permute-done.4.refs_4_), channel_id=1, source_target_pairs={{0,16},{16,0},{32,48},{48,32},{64,80},{80,64},{96,112},{112,96},{1... | collective-permute-start | bytes 786440 | tf_op jit(solution)/shard_map/ppermute | solution.py:648
  82.3 32.4 %all-to-all-start.2 = ((bf16[16,128,256]{2,1,0:T(8,128)(2,1)}), bf16[16,128,256]{2,1,0:T(8,128)(2,1)S(1)}, u32[]{:S(2)}, u32[]{:S(2)}) async-start(bf16[16,128,256]{2,1,0:T(8,128)(2,1)} %scan.1), calls=%async_computation.2 | async-start | bytes 2097152 | tf_op jit(solution)/shard_map/all_to_all | solution.py:651
  86.7 2.2 %copy-start.1 = (bf16[2048,1024]{1,0:T(8,128)(2,1)S(1)}, bf16[2048,1024]{1,0:T(8,128)(2,1)}, u32[]{:S(2)}) copy-start(bf16[2048,1024]{1,0:T(8,128)(2,1)} %w_ref.1) | copy-start | bytes 12582916
  88.9 1.6 %copy-start.3 = (bf16[512,2048]{1,0:T(8,128)(2,1)S(1)}, bf16[512,2048]{1,0:T(8,128)(2,1)}, u32[]{:S(2)}) copy-start(bf16[512,2048]{1,0:T(8,128)(2,1)} %lat_ref.3) | copy-start | bytes 6291460
  90.5 24.2 %copy-start.6 = (f32[1024]{0:T(1024)S(1)}, f32[1024]{0:T(1024)}, u32[]{:S(2)}) copy-start(f32[1024]{0:T(1024)} %param.25) | copy-start | bytes 12292
  (5 other events, 3.7 us)
